TPU v7x, 32 devices: a whole 2x2x4 slice. The times are simulated.
32 devices in a mesh: frame: 8 (over y, x, core), qblk: 4 (over z).
Axes of the slice: x: 2, y: 2, z: 4, core: 2. Of those that a mesh axis runs over, the one named last changes fastest.
Arguments:
- query_tokens: bfloat16 [8, 144, 768], P('frame', 'qblk'), may hold values from -12 to 12
- key_tokens: bfloat16 [8, 144, 768], P('frame', 'qblk'), may hold values from -12 to 12
- value_tokens: bfloat16 [8, 144, 768], P('frame', 'qblk'), may hold values from -4 to 4
- w_query: bfloat16 [768, 768], replicated, as said below
- w_key: bfloat16 [768, 768], replicated, as said below
- w_value: bfloat16 [768, 768], replicated, may hold values from -0.4375 to 0.4375
Outputs:
- trajectory: bfloat16 [8, 144, 768], P('frame', 'qblk')
Inputs may be any that keep to these rules, and one draw needn't show every extreme that they name: `w_query`: entries of order one over the square root of 768. `w_key`: entries of order one over the square root of 768.
All inputs are finite; a program needn't handle non-finite values.
Results may differ from a plain program's by a relative error of at most 0.0091.
Values may be sent and summed in bfloat16 or wider, within the bound.
No kernel may reach another device: no remote copies, remote signals or barrier semaphores. Data moves between devices by JAX's collectives and lax.ppermute only.
A program may use at most 64 MiB of HBM per device.

v0:
```python
import math

import jax
import jax.numpy as jnp
from jax import lax
from jax.sharding import PartitionSpec as P

HEADS = 12


def split_heads(matrix):
    return matrix.reshape(matrix.shape[0], HEADS, -1).transpose(1, 0, 2)


def attend_frame(query_rows, key_heads, value_heads):
    scale_factor = 1.0 / math.sqrt(key_heads.shape[2])

    def one_head(operands):
        query_head, key_head, value_head = operands
        scores = jnp.dot(query_head, key_head.T, preferred_element_type=jnp.float32) * scale_factor
        shifted = jnp.exp(scores - jnp.max(scores, axis=1, keepdims=True))
        weights = (shifted / jnp.sum(shifted, axis=1, keepdims=True)).astype(jnp.bfloat16)
        return jnp.dot(weights, value_head, preferred_element_type=jnp.float32).astype(jnp.bfloat16)

    pooled_heads = lax.map(one_head, (split_heads(query_rows), key_heads, value_heads))
    return pooled_heads.transpose(1, 0, 2).reshape(query_rows.shape[0], -1)


def project(rows, matrix):
    return jnp.dot(rows, matrix, preferred_element_type=jnp.float32).astype(jnp.bfloat16)


def trajectory_mix(query_proj, key_proj, value_proj):
    frame_count, row_count, feature_width = key_proj.shape
    head_width = feature_width // HEADS
    scale_factor = 1.0 / math.sqrt(head_width)
    query_split = query_proj.reshape(row_count, HEADS, head_width)
    key_split = key_proj.reshape(frame_count, row_count, HEADS, head_width)
    value_split = value_proj.reshape(frame_count, row_count, HEADS, head_width)
    scores = (
        jnp.einsum("nhd,fnhd->nhf", query_split, key_split, preferred_element_type=jnp.float32)
        * scale_factor
    )
    shifted = jnp.exp(scores - jnp.max(scores, axis=2, keepdims=True))
    weights = (shifted / jnp.sum(shifted, axis=2, keepdims=True)).astype(jnp.bfloat16)
    mixed_rows = jnp.einsum(
        "nhf,fnhd->nhd", weights, value_split, preferred_element_type=jnp.float32
    )
    return mixed_rows.reshape(row_count, feature_width).astype(jnp.bfloat16)


def per_device(query_tokens, key_tokens, value_tokens, w_query, w_key, w_value):
    frame_keys, frame_values = (
        lax.all_gather(key_tokens, "qblk", axis=1, tiled=True),
        lax.all_gather(value_tokens, "qblk", axis=1, tiled=True),
    )
    key_heads = split_heads(frame_keys[0])
    value_heads = split_heads(frame_values[0])
    pooled = attend_frame(
        lax.all_gather(query_tokens[0], "frame", axis=0, tiled=True), key_heads, value_heads
    )
    frame_total = lax.axis_size("frame")
    own_frame = lax.axis_index("frame")
    local_rows = query_tokens.shape[1]
    feature_width = query_tokens.shape[2]
    pooled_grid = pooled.reshape(frame_total, local_rows, feature_width)
    received = lax.all_to_all(pooled_grid, "frame", split_axis=0, concat_axis=0, tiled=True)
    row_total = received.shape[1]
    diagonal = lax.dynamic_index_in_dim(received, own_frame, 0, keepdims=False)
    flat_rows = received.reshape(frame_total * row_total, feature_width)
    key_proj = project(flat_rows, w_key).reshape(frame_total, row_total, feature_width)
    value_proj = project(flat_rows, w_value).reshape(frame_total, row_total, feature_width)
    mixed_rows = trajectory_mix(project(diagonal, w_query), key_proj, value_proj)
    return mixed_rows.reshape(1, local_rows, feature_width)


def solution(mesh):
    in_specs = (
        P("frame", "qblk", None),
        P("frame", "qblk", None),
        P("frame", "qblk", None),
        P(),
        P(),
        P(),
    )
    out_specs = P("frame", "qblk", None)
    return jax.shard_map(
        per_device, mesh=mesh, in_specs=in_specs, out_specs=out_specs, check_vma=False
    )
```

profile of v0, /device:TPU:0, one launch (start us, length us, event | category | flops | bytes accessed | tf_op | source)
XLA Modules:
  0.0 85.1 jit_solution(15348114285782481384)
XLA Ops:
  0.0 1.0 %copy.24 = bf16[1,36,768]{2,0,1:T(2,128)(2,1)S(1)} copy(bf16[1,36,768]{2,1,0:T(8,128)(2,1)} %param.8) | data formatting | bytes 110592 | tf_op args[0]
  1.0 12.3 %all-gather = bf16[1,288,768]{2,0,1:T(2,128)(2,1)S(1)} all-gather(bf16[1,36,768]{2,0,1:T(2,128)(2,1)S(1)} %copy.24), channel_id=2, replica_groups=mesh['frame'=8,'qblk'=4] {'frame'}, dimensions={1}, use_global_device_ids=true | all-gather | bytes 497664 | tf_op jit(solution)/shard_map/all_gather | solution.py:60
  13.3 0.9 %copy.25 = bf16[1,288,768]{1,2,0:T(8,128)(2,1)S(1)} copy(bf16[1,288,768]{2,0,1:T(2,128)(2,1)S(1)} %all-gather) | data formatting | bytes 884736 | tf_op jit(solution)/shard_map/all_gather | solution.py:60
  14.3 15.4 %all_gather.10 = bf16[1,144,768]{2,0,1:T(2,128)(2,1)S(1)} all-gather(bf16[1,36,768]{2,0,1:T(2,128)(2,1)S(1)} %copy.26), channel_id=1, replica_groups=mesh['frame'=8,'qblk'=4] {'qblk'}, dimensions={1}, use_global_device_ids=true | all-gather | bytes 276480 | tf_op jit(solution)/shard_map/all_gather | solution.py:54
  30.3 15.4 %all_gather.11 = bf16[1,144,768]{2,0,1:T(2,128)(2,1)S(1)} all-gather(bf16[1,36,768]{2,0,1:T(2,128)(2,1)S(1)} %copy.28), channel_id=1, replica_groups=mesh['frame'=8,'qblk'=4] {'qblk'}, dimensions={1}, use_global_device_ids=true | all-gather | bytes 276480 | tf_op jit(solution)/shard_map/all_gather | solution.py:55
  45.8 1.1 %copy.29 = bf16[1,144,768]{1,2,0:T(8,128)(2,1)} copy(bf16[1,144,768]{2,0,1:T(2,128)(2,1)S(1)} %all_gather.11) | data formatting | bytes 442368 | tf_op jit(solution)/shard_map/all_gather | solution.py:55
  46.9 15.3 %while.10 = (s32[]{:T(128)}, bf16[12,288,64]{1,2,0:T(8,128)(2,1)S(1)}, bf16[12,288,64]{1,2,0:T(8,128)(2,1)S(1)}, bf16[12,144,64]{1,2,0:T(8,128)(2,1)S(1)}, bf16[12,144,64]{1,2,0:T(8,128)(2,1)}, /*index=5*/s32[]{:T(128)}) while((s32[]{:T(128)}, bf16[12,288,64]{1,2,0:T(8,128)(2,1)S(1)}, bf16[12,288,64]{1,2,0:T(8,128)(2,1)S(1)}, ...), condition=%wide.region_3.4_spmd, body=%wide.region_0.3_spmd.sunk | while | flops 10924994 | bytes 726469 | solution.py:25
  47.2 0.9 %fusion.45 = bf16[12,288,64]{1,2,0:T(8,128)(2,1)S(1)} fusion(bf16[12,288,64]{1,2,0:T(8,128)(2,1)S(1)} %get-tuple-element.102, s32[]{:T(128)} %get-tuple-element.101, f32[288,144]{0,1:T(8,128)S(1)} %get-tuple-element.93, f32[288]{0:T(512)S(1)} %fusion.44, f32[288]{0:T(512)S(1)} %get-tuple-element.94, bf16[12,144,64]{1,2,0:T(8,128)(2,1)} %get-tuple-element.111), kind=kOutput, calls=%fused_computation.3.clone.1 | convolution fusion | flops 5451264 | bytes 308224 | tf_op jit(solution)/shard_map/while/body/eval_jaxpr/dot_general | solution.py:23
  48.5 0.9 %fusion.45 = bf16[12,288,64]{1,2,0:T(8,128)(2,1)S(1)} fusion(bf16[12,288,64]{1,2,0:T(8,128)(2,1)S(1)} %get-tuple-element.102, s32[]{:T(128)} %get-tuple-element.101, f32[288,144]{0,1:T(8,128)S(1)} %get-tuple-element.93, f32[288]{0:T(512)S(1)} %fusion.44, f32[288]{0:T(512)S(1)} %get-tuple-element.94, bf16[12,144,64]{1,2,0:T(8,128)(2,1)} %get-tuple-element.111), kind=kOutput, calls=%fused_computation.3.clone.1 | convolution fusion | flops 5451264 | bytes 308224 | tf_op jit(solution)/shard_map/while/body/eval_jaxpr/dot_general | solution.py:23
  49.8 0.9 %fusion.45 = bf16[12,288,64]{1,2,0:T(8,128)(2,1)S(1)} fusion(bf16[12,288,64]{1,2,0:T(8,128)(2,1)S(1)} %get-tuple-element.102, s32[]{:T(128)} %get-tuple-element.101, f32[288,144]{0,1:T(8,128)S(1)} %get-tuple-element.93, f32[288]{0:T(512)S(1)} %fusion.44, f32[288]{0:T(512)S(1)} %get-tuple-element.94, bf16[12,144,64]{1,2,0:T(8,128)(2,1)} %get-tuple-element.111), kind=kOutput, calls=%fused_computation.3.clone.1 | convolution fusion | flops 5451264 | bytes 308224 | tf_op jit(solution)/shard_map/while/body/eval_jaxpr/dot_general | solution.py:23
  51.1 0.9 %fusion.45 = bf16[12,288,64]{1,2,0:T(8,128)(2,1)S(1)} fusion(bf16[12,288,64]{1,2,0:T(8,128)(2,1)S(1)} %get-tuple-element.102, s32[]{:T(128)} %get-tuple-element.101, f32[288,144]{0,1:T(8,128)S(1)} %get-tuple-element.93, f32[288]{0:T(512)S(1)} %fusion.44, f32[288]{0:T(512)S(1)} %get-tuple-element.94, bf16[12,144,64]{1,2,0:T(8,128)(2,1)} %get-tuple-element.111), kind=kOutput, calls=%fused_computation.3.clone.1 | convolution fusion | flops 5451264 | bytes 308224 | tf_op jit(solution)/shard_map/while/body/eval_jaxpr/dot_general | solution.py:23
  52.3 0.9 %fusion.45 = bf16[12,288,64]{1,2,0:T(8,128)(2,1)S(1)} fusion(bf16[12,288,64]{1,2,0:T(8,128)(2,1)S(1)} %get-tuple-element.102, s32[]{:T(128)} %get-tuple-element.101, f32[288,144]{0,1:T(8,128)S(1)} %get-tuple-element.93, f32[288]{0:T(512)S(1)} %fusion.44, f32[288]{0:T(512)S(1)} %get-tuple-element.94, bf16[12,144,64]{1,2,0:T(8,128)(2,1)} %get-tuple-element.111), kind=kOutput, calls=%fused_computation.3.clone.1 | convolution fusion | flops 5451264 | bytes 308224 | tf_op jit(solution)/shard_map/while/body/eval_jaxpr/dot_general | solution.py:23
  53.6 0.9 %fusion.45 = bf16[12,288,64]{1,2,0:T(8,128)(2,1)S(1)} fusion(bf16[12,288,64]{1,2,0:T(8,128)(2,1)S(1)} %get-tuple-element.102, s32[]{:T(128)} %get-tuple-element.101, f32[288,144]{0,1:T(8,128)S(1)} %get-tuple-element.93, f32[288]{0:T(512)S(1)} %fusion.44, f32[288]{0:T(512)S(1)} %get-tuple-element.94, bf16[12,144,64]{1,2,0:T(8,128)(2,1)} %get-tuple-element.111), kind=kOutput, calls=%fused_computation.3.clone.1 | convolution fusion | flops 5451264 | bytes 308224 | tf_op jit(solution)/shard_map/while/body/eval_jaxpr/dot_general | solution.py:23
  54.9 0.9 %fusion.45 = bf16[12,288,64]{1,2,0:T(8,128)(2,1)S(1)} fusion(bf16[12,288,64]{1,2,0:T(8,128)(2,1)S(1)} %get-tuple-element.102, s32[]{:T(128)} %get-tuple-element.101, f32[288,144]{0,1:T(8,128)S(1)} %get-tuple-element.93, f32[288]{0:T(512)S(1)} %fusion.44, f32[288]{0:T(512)S(1)} %get-tuple-element.94, bf16[12,144,64]{1,2,0:T(8,128)(2,1)} %get-tuple-element.111), kind=kOutput, calls=%fused_computation.3.clone.1 | convolution fusion | flops 5451264 | bytes 308224 | tf_op jit(solution)/shard_map/while/body/eval_jaxpr/dot_general | solution.py:23
  56.2 0.9 %fusion.45 = bf16[12,288,64]{1,2,0:T(8,128)(2,1)S(1)} fusion(bf16[12,288,64]{1,2,0:T(8,128)(2,1)S(1)} %get-tuple-element.102, s32[]{:T(128)} %get-tuple-element.101, f32[288,144]{0,1:T(8,128)S(1)} %get-tuple-element.93, f32[288]{0:T(512)S(1)} %fusion.44, f32[288]{0:T(512)S(1)} %get-tuple-element.94, bf16[12,144,64]{1,2,0:T(8,128)(2,1)} %get-tuple-element.111), kind=kOutput, calls=%fused_computation.3.clone.1 | convolution fusion | flops 5451264 | bytes 308224 | tf_op jit(solution)/shard_map/while/body/eval_jaxpr/dot_general | solution.py:23
  57.5 0.9 %fusion.45 = bf16[12,288,64]{1,2,0:T(8,128)(2,1)S(1)} fusion(bf16[12,288,64]{1,2,0:T(8,128)(2,1)S(1)} %get-tuple-element.102, s32[]{:T(128)} %get-tuple-element.101, f32[288,144]{0,1:T(8,128)S(1)} %get-tuple-element.93, f32[288]{0:T(512)S(1)} %fusion.44, f32[288]{0:T(512)S(1)} %get-tuple-element.94, bf16[12,144,64]{1,2,0:T(8,128)(2,1)} %get-tuple-element.111), kind=kOutput, calls=%fused_computation.3.clone.1 | convolution fusion | flops 5451264 | bytes 308224 | tf_op jit(solution)/shard_map/while/body/eval_jaxpr/dot_general | solution.py:23
  58.7 0.9 %fusion.45 = bf16[12,288,64]{1,2,0:T(8,128)(2,1)S(1)} fusion(bf16[12,288,64]{1,2,0:T(8,128)(2,1)S(1)} %get-tuple-element.102, s32[]{:T(128)} %get-tuple-element.101, f32[288,144]{0,1:T(8,128)S(1)} %get-tuple-element.93, f32[288]{0:T(512)S(1)} %fusion.44, f32[288]{0:T(512)S(1)} %get-tuple-element.94, bf16[12,144,64]{1,2,0:T(8,128)(2,1)} %get-tuple-element.111), kind=kOutput, calls=%fused_computation.3.clone.1 | convolution fusion | flops 5451264 | bytes 308224 | tf_op jit(solution)/shard_map/while/body/eval_jaxpr/dot_general | solution.py:23
  60.0 0.9 %fusion.45 = bf16[12,288,64]{1,2,0:T(8,128)(2,1)S(1)} fusion(bf16[12,288,64]{1,2,0:T(8,128)(2,1)S(1)} %get-tuple-element.102, s32[]{:T(128)} %get-tuple-element.101, f32[288,144]{0,1:T(8,128)S(1)} %get-tuple-element.93, f32[288]{0:T(512)S(1)} %fusion.44, f32[288]{0:T(512)S(1)} %get-tuple-element.94, bf16[12,144,64]{1,2,0:T(8,128)(2,1)} %get-tuple-element.111), kind=kOutput, calls=%fused_computation.3.clone.1 | convolution fusion | flops 5451264 | bytes 308224 | tf_op jit(solution)/shard_map/while/body/eval_jaxpr/dot_general | solution.py:23
  61.3 0.9 %fusion.45 = bf16[12,288,64]{1,2,0:T(8,128)(2,1)S(1)} fusion(bf16[12,288,64]{1,2,0:T(8,128)(2,1)S(1)} %get-tuple-element.102, s32[]{:T(128)} %get-tuple-element.101, f32[288,144]{0,1:T(8,128)S(1)} %get-tuple-element.93, f32[288]{0:T(512)S(1)} %fusion.44, f32[288]{0:T(512)S(1)} %get-tuple-element.94, bf16[12,144,64]{1,2,0:T(8,128)(2,1)} %get-tuple-element.111), kind=kOutput, calls=%fused_computation.3.clone.1 | convolution fusion | flops 5451264 | bytes 308224 | tf_op jit(solution)/shard_map/while/body/eval_jaxpr/dot_general | solution.py:23
  62.2 1.4 %copy.33 = bf16[288,12,64]{2,1,0:T(8,128)(2,1)S(1)} copy(bf16[288,12,64]{0,2,1:T(8,128)(2,1)S(1)} %bitcast.62) | data formatting | bytes 884736 | tf_op jit(solution)/shard_map/transpose | solution.py:26
  63.6 1.5 %reshape_reshape.9 = bf16[8,36,768]{2,1,0:T(8,128)(2,1)} reshape(bf16[288,12,64]{2,1,0:T(8,128)(2,1)S(1)} %copy.33) | data formatting | bytes 884736 | tf_op jit(solution)/shard_map/reshape;reshape | solution.py:66
  65.1 3.5 %all-to-all-start = ((bf16[8,36,768]{2,1,0:T(8,128)(2,1)}), bf16[8,36,768]{2,1,0:T(8,128)(2,1)S(1)}, u32[]{:S(2)}, u32[]{:S(2)}) async-start(bf16[8,36,768]{2,1,0:T(8,128)(2,1)} %reshape_reshape.9), calls=%async_computation | async-start | bytes 983040 | tf_op jit(solution)/shard_map/all_to_all | solution.py:67
  68.6 9.3 %all-to-all-done = bf16[8,36,768]{2,1,0:T(8,128)(2,1)S(1)} async-done(((bf16[8,36,768]{2,1,0:T(8,128)(2,1)}), bf16[8,36,768]{2,1,0:T(8,128)(2,1)S(1)}, u32[]{:S(2)}, u32[]{:S(2)}) %all-to-all-start) | async-done | bytes 442400 | tf_op jit(solution)/shard_map/all_to_all | solution.py:67
  81.0 1.8 %convolution_convert_fusion.1 = bf16[288,768]{1,0:T(8,128)(2,1)S(1)} fusion(bf16[288,768]{1,0:T(8,128)(2,1)S(1)} %reshape.28, bf16[768,768]{1,0:T(8,128)(2,1)} %param.13), kind=kOutput, calls=%fused_computation.19 | convolution fusion | flops 339959808 | bytes 2064384 | tf_op jit(solution)/shard_map/dot_general | solution.py:30
  (49 shorter events, 9.7 us)
Async XLA Ops:
  0.0 78.5 %copy-start = (bf16[768,768]{1,0:T(8,128)(2,1)S(1)}, bf16[768,768]{1,0:T(8,128)(2,1)}, u32[]{:S(2)}) copy-start(bf16[768,768]{1,0:T(8,128)(2,1)} %param.12) | copy-start | bytes 3538948
  1.0 13.2 %copy-start.2 = (bf16[1,36,768]{2,1,0:T(8,128)(2,1)S(1)}, bf16[1,36,768]{2,1,0:T(8,128)(2,1)}, u32[]{:S(2)}) copy-start(bf16[1,36,768]{2,1,0:T(8,128)(2,1)} %param.9) | copy-start | bytes 165892
  13.3 16.9 %copy-start.3 = (bf16[1,36,768]{2,1,0:T(8,128)(2,1)S(1)}, bf16[1,36,768]{2,1,0:T(8,128)(2,1)}, u32[]{:S(2)}) copy-start(bf16[1,36,768]{2,1,0:T(8,128)(2,1)} %param.10) | copy-start | bytes 165892
  63.6 14.3 %copy-start.1 = (bf16[768,768]{1,0:T(8,128)(2,1)S(1)}, bf16[768,768]{1,0:T(8,128)(2,1)}, u32[]{:S(2)}) copy-start(bf16[768,768]{1,0:T(8,128)(2,1)} %param.11) | copy-start | bytes 3538948
  65.1 12.8 %all-to-all-start = ((bf16[8,36,768]{2,1,0:T(8,128)(2,1)}), bf16[8,36,768]{2,1,0:T(8,128)(2,1)S(1)}, u32[]{:S(2)}, u32[]{:S(2)}) async-start(bf16[8,36,768]{2,1,0:T(8,128)(2,1)} %reshape_reshape.9), calls=%async_computation | async-start | bytes 983040 | tf_op jit(solution)/shard_map/all_to_all | solution.py:67
where the time goes:
time: 86.2 us; the launch traced here: 85.1 us
  blocking collectives  43.1 us (50%)
  matrix products  18.5 us (21%)
  local copies, waits for them, and re-layouts  9.37 us (11%)
  waiting for transfers between devices  9.32 us (11%)
  starting transfers between devices  3.48 us (4%)
    all_gather x1, blocking collectives, per_device(): lax.all_gather(value_tokens, 'qblk', axis=1, tiled=True)  15.4 us
    all_gather x1, blocking collectives, per_device(): lax.all_gather(key_tokens, 'qblk', axis=1, tiled=True)  15.4 us
    all_gather x1, blocking collectives, per_device(): lax.all_gather(query_tokens[0], 'frame', axis=0, tiled=True)  12.3 us
    dot_general x12, matrix products, one_head(): jnp.dot(weights, value_head, preferred_element_type=jnp.float32)  11.2 us
    all_to_all x1, waiting for transfers between devices, per_device(): lax.all_to_all(pooled_grid, 'frame', split_axis=0, concat_axis=0, tiled=T...  9.32 us
    all_to_all x1, starting transfers between devices, per_device(): lax.all_to_all(pooled_grid, 'frame', split_axis=0, concat_axis=0, tiled=T...  3.48 us
    dot_general x12, matrix products, one_head(): jnp.dot(query_head, key_head.T, preferred_element_type=jnp.float32)  3.09 us
    dot_general x3, matrix products, project(): jnp.dot(rows, matrix, preferred_element_type=jnp.float32)  2.63 us
  transfers between devices with their start and end apart: 1, of which 1 were waited for; matrix products, arithmetic and copies ran while one was open for 0% of the time, Pallas kernels for 0%

commit v1 on v0

v1 whole, which is shorter than its diff:
```python
import functools
import math

import jax
import jax.numpy as jnp
from jax import lax
from jax.experimental import pallas as pl
from jax.experimental.pallas import tpu as pltpu
from jax.sharding import PartitionSpec as P

HEADS = 12
LANES = 128
VMEM = pl.BlockSpec(memory_space=pltpu.VMEM)
NT = (((1,), (1,)), ((), ()))


def ceil_to(value, unit):
    return -(-value // unit) * unit


def stack_rows(blocks, stage):
    rows = blocks[0].shape[0]
    pitch = ceil_to(rows, 8)
    for index, block in enumerate(blocks):
        stage[pl.ds(index * pitch, rows), :] = block.astype(jnp.float32)
        if pitch > rows:
            stage[pl.ds(index * pitch + rows, pitch - rows), :] = jnp.zeros(
                (pitch - rows, stage.shape[1]), jnp.float32
            )
    return stage[...].astype(jnp.bfloat16)


def attend(query, key, value, valid, head_width, put):
    per_slab = LANES // head_width
    factor = math.log2(math.e) / math.sqrt(head_width)
    key_total = key.shape[0]
    lane = lax.broadcasted_iota(jnp.int32, (key_total, LANES), 1) // head_width
    bias = jnp.where(valid, 0.0, -1e30)
    for slab in range(query.shape[1] // LANES):
        cut = slice(slab * LANES, (slab + 1) * LANES)
        query_slab, key_slab, value_slab = query[:, cut], key[:, cut], value[:, cut]
        total = None
        for head in range(per_slab):
            own = lane == head
            masked_key = jnp.where(own, key_slab, 0)
            scores = lax.dot_general(query_slab, masked_key, NT, preferred_element_type=jnp.float32)
            scores = scores + bias
            top = jnp.max(scores, axis=1, keepdims=True)
            weights = jnp.exp2((scores - top) * factor)
            weights = weights * (1.0 / jnp.sum(weights, axis=1, keepdims=True))
            part = jnp.dot(
                weights.astype(jnp.bfloat16),
                jnp.where(own, value_slab, 0),
                preferred_element_type=jnp.float32,
            )
            total = part if total is None else total + part
        put(slab, total)


def attention_kernel(head_width, query_count, block_count, has_earlier, *refs):
    queries = refs[:query_count]
    keys = refs[query_count : query_count + block_count]
    values = refs[query_count + block_count : query_count + 2 * block_count]
    refs = refs[query_count + 2 * block_count :]
    earlier = refs[:query_count] if has_earlier else ()
    refs = refs[len(earlier) :]
    outs, (query_stage, key_stage, value_stage) = refs[:query_count], refs[query_count:]
    rows = queries[0].shape[-2]
    pitch = ceil_to(rows, 8)
    query = stack_rows([ref[0] for ref in queries], query_stage)
    key = stack_rows([ref[0] for ref in keys], key_stage)
    value = stack_rows([ref[0] for ref in values], value_stage)
    place = lax.broadcasted_iota(jnp.int32, (1, key.shape[0]), 1)
    valid = lax.rem(place, pitch) < rows

    def put(slab, pooled):
        for index in range(query_count):
            outs[index][outs[index].shape[0] - 1, :, pl.ds(slab * LANES, LANES)] = pooled[
                index * pitch : index * pitch + rows
            ].astype(jnp.bfloat16)

    attend(query, key, value, valid, head_width, put)
    for index, ref in enumerate(earlier):
        outs[index][0] = ref[0]


def attention(queries, keys, values, earlier=()):
    _, rows, width = queries[0].shape
    pitch = ceil_to(rows, 8)
    count = len(queries)
    kernel = functools.partial(attention_kernel, width // HEADS, count, len(keys), bool(earlier))
    flops = 4 * count * rows * len(keys) * rows * width
    shape = jax.ShapeDtypeStruct((2 if earlier else 1, rows, width), jnp.bfloat16)
    return pl.pallas_call(
        kernel,
        out_shape=[shape] * count,
        in_specs=[VMEM] * (count + 2 * len(keys) + len(earlier)),
        out_specs=[VMEM] * count,
        scratch_shapes=[
            pltpu.VMEM((count * pitch, width), jnp.float32),
            pltpu.VMEM((len(keys) * pitch, width), jnp.float32),
            pltpu.VMEM((len(keys) * pitch, width), jnp.float32),
        ],
        compiler_params=pltpu.CompilerParams(vmem_limit_bytes=48 << 20),
        cost_estimate=pl.CostEstimate(flops=flops, bytes_accessed=1 << 20, transcendentals=0),
        name="attention",
    )(*queries, *keys, *values, *earlier)


def mix_kernel(head_width, pieces, *refs):
    arrived = refs[:pieces]
    w_query, w_key, w_value, out, stage, key_stage, value_stage = refs[pieces:]
    blocks = [ref[index] for ref in arrived for index in range(ref.shape[0])]
    rows, width = blocks[0].shape
    pitch = ceil_to(rows, 8)
    count = len(blocks)
    scale = 1.0 / math.sqrt(head_width)
    pooled = stack_rows(blocks, stage)
    own = pooled[:ceil_to(rows, 16)]
    query = jnp.dot(own, w_query[...], preferred_element_type=jnp.float32)[:pitch]
    query = query.astype(jnp.bfloat16).astype(jnp.float32)
    key_stage[...] = (
        jnp.dot(pooled, w_key[...], preferred_element_type=jnp.float32)
        .astype(jnp.bfloat16)
        .astype(jnp.float32)
    )
    value_stage[...] = (
        jnp.dot(pooled, w_value[...], preferred_element_type=jnp.float32)
        .astype(jnp.bfloat16)
        .astype(jnp.float32)
    )
    member = (
        lax.broadcasted_iota(jnp.int32, (width, LANES), 0) // head_width
        == lax.broadcasted_iota(jnp.int32, (width, LANES), 1)
    ).astype(jnp.bfloat16)
    spread = (
        lax.broadcasted_iota(jnp.int32, (LANES, width), 1) // head_width
        == lax.broadcasted_iota(jnp.int32, (LANES, width), 0)
    ).astype(jnp.bfloat16)
    product = jnp.concatenate(
        [key_stage[pl.ds(index * pitch, pitch), :] * query for index in range(count)], axis=0
    )
    high = product.astype(jnp.bfloat16)
    low = (product - high.astype(jnp.float32)).astype(jnp.bfloat16)
    scores = jnp.dot(high, member, preferred_element_type=jnp.float32) + jnp.dot(
        low, member, preferred_element_type=jnp.float32
    )
    scores = scores * scale
    parts = [scores[index * pitch : (index + 1) * pitch] for index in range(count)]
    top = functools.reduce(jnp.maximum, parts)
    parts = [jnp.exp(part - top) for part in parts]
    total = functools.reduce(jnp.add, parts)
    weights = jnp.concatenate([part / total for part in parts], axis=0).astype(jnp.bfloat16)
    weights = jnp.dot(weights, spread, preferred_element_type=jnp.float32)
    mixed = functools.reduce(
        jnp.add,
        [
            weights[index * pitch : (index + 1) * pitch]
            * value_stage[pl.ds(index * pitch, pitch), :]
            for index in range(count)
        ],
    )
    out[0] = mixed[:rows].astype(jnp.bfloat16)


def mix(arrived, w_query, w_key, w_value):
    _, rows, width = arrived[0].shape
    pitch = ceil_to(rows, 8)
    count = sum(array.shape[0] for array in arrived)
    total = ceil_to(count * pitch, 16)
    return pl.pallas_call(
        functools.partial(mix_kernel, width // HEADS, len(arrived)),
        out_shape=jax.ShapeDtypeStruct((1, rows, width), jnp.bfloat16),
        in_specs=[VMEM] * (len(arrived) + 3),
        out_specs=VMEM,
        scratch_shapes=[pltpu.VMEM((total, width), jnp.float32)] * 3,
        compiler_params=pltpu.CompilerParams(vmem_limit_bytes=48 << 20),
        cost_estimate=pl.CostEstimate(
            flops=4 * count * rows * width * width, bytes_accessed=4 << 20, transcendentals=0
        ),
        name="mix",
    )(*arrived, w_query, w_key, w_value)


def rounds(total):
    for step in range(1, total):
        if total & (total - 1) == 0:
            there = [(index, index ^ step) for index in range(total)]
        else:
            there = [(index, (index + step) % total) for index in range(total)]
        yield there, [(target, source) for source, target in there]


def chip_rounds(total):
    for there, back in rounds(total // 2):
        yield tuple(
            [(2 * source + core, 2 * target + core) for source, target in pairs for core in range(2)]
            for pairs in (there, back)
        )


def per_device(query_tokens, key_tokens, value_tokens, w_query, w_key, w_value):
    frame_total = lax.axis_size("frame")
    block_total = lax.axis_size("qblk")
    swap = [(index, index ^ 1) for index in range(frame_total)]
    keys, values = [key_tokens], [value_tokens]
    for there, _ in rounds(block_total):
        keys.append(lax.ppermute(key_tokens, "qblk", there))
        values.append(lax.ppermute(value_tokens, "qblk", there))
    paths = list(chip_rounds(frame_total))
    queries = [query_tokens] + [lax.ppermute(query_tokens, "frame", there) for there, _ in paths]
    other_keys = [lax.ppermute(block, "frame", swap) for block in keys]
    other_values = [lax.ppermute(block, "frame", swap) for block in values]
    own = attention(queries, keys, values)
    pooled = attention(queries, other_keys, other_values, own)
    arrived = [pooled[0]] + [
        lax.ppermute(block, "frame", back) for block, (_, back) in zip(pooled[1:], paths)
    ]
    return mix(arrived, w_query, w_key, w_value)


def solution(mesh):
    in_specs = (
        P("frame", "qblk", None),
        P("frame", "qblk", None),
        P("frame", "qblk", None),
        P(),
        P(),
        P(),
    )
    out_specs = P("frame", "qblk", None)
    return jax.shard_map(
        per_device, mesh=mesh, in_specs=in_specs, out_specs=out_specs, check_vma=False
    )
```

time: 86.2 us -> 40.6 us (0.47)
  blocking collectives: 43.1 us -> 0 us
  matrix products: 18.5 us -> 0 us
  starting transfers between devices: 3.48 us -> 21.2 us
  Pallas kernels: 0 us -> 5.4 us
  local copies, waits for them, and re-layouts: 9.37 us -> 5.03 us
    all_gather x3 -> x0, blocking collectives: 43.1 us -> none  [the longest x1 15.4 us: per_device(): lax.all_gather(value_tokens, 'qblk', axis=1, tiled=True)]
    ppermute x0 -> x20, starting transfers between devices: none -> 21.2 us  [the longest x3 7.39 us: per_device(): keys.append(lax.ppermute(key_tokens, 'qblk', there))]
    dot_general x29 -> x0, matrix products: 18.5 us -> none  [the longest x12 11.2 us: one_head(): jnp.dot(weights, value_head, preferred_element_type=jnp.float32)]
    all_to_all x1 -> x0, waiting for transfers between devices: 9.32 us -> none  [per_device(): lax.all_to_all(pooled_grid, 'frame', split_axis=0, concat_axis=0, tiled=T...]
    ppermute x0 -> x20, waiting for transfers between devices: none -> 8.59 us  [the longest x3 5.59 us: per_device(): lax.ppermute(block, 'frame', back)]
    pallas_call x0 -> x3, Pallas kernels: none -> 5.4 us  [the longest x2 2.87 us: attention(): pl.pallas_call(kernel, out_shape=[shape] * count, in_specs=[VMEM] * (coun...]
    unnamed x11 -> x12, local copies, waits for them, and re-layouts: 1.2 us -> 5.03 us
    all_to_all x1 -> x0, starting transfers between devices: 3.48 us -> none  [per_device(): lax.all_to_all(pooled_grid, 'frame', split_axis=0, concat_axis=0, tiled=T...]
  transfers between devices with their start and end apart: 1 -> 20, of which waited for: 1 -> 4; matrix products, arithmetic and copies ran while one was open for 0% -> 0% of each run, Pallas kernels for 0% -> 4%
where the time goes in v1:
time: 40.6 us; the launch traced here: 40.3 us
  starting transfers between devices  21.2 us (52%)
  waiting for transfers between devices  8.59 us (21%)
  Pallas kernels  5.4 us (13%)
  local copies, waits for them, and re-layouts  5.03 us (12%)
    ppermute x3, starting transfers between devices, per_device(): keys.append(lax.ppermute(key_tokens, 'qblk', there))  7.39 us
    ppermute x3, waiting for transfers between devices, per_device(): lax.ppermute(block, 'frame', back)  5.59 us
    unnamed x12, local copies, waits for them, and re-layouts  5.03 us
    ppermute x3, starting transfers between devices, per_device(): lax.ppermute(query_tokens, 'frame', there)  4.52 us
    ppermute x3, starting transfers between devices, per_device(): values.append(lax.ppermute(value_tokens, 'qblk', there))  4.45 us
    ppermute x3, starting transfers between devices, per_device(): lax.ppermute(block, 'frame', back)  3.55 us
    ppermute x3, waiting for transfers between devices, per_device(): values.append(lax.ppermute(value_tokens, 'qblk', there))  2.97 us
    pallas_call x2, Pallas kernels, attention(): pl.pallas_call(kernel, out_shape=[shape] * count, in_specs=[VMEM] * (coun...  2.87 us
  transfers between devices with their start and end apart: 20, of which 4 were waited for; matrix products, arithmetic and copies ran while one was open for 0% of the time, Pallas kernels for 4%

profile of v1, /device:TPU:0, one launch (start us, length us, event | category | flops | bytes accessed | tf_op | source)
XLA Modules:
  0.0 40.3 jit_solution(14404038754472026408)
XLA Ops:
  0.0 3.9 %collective-permute-start.2 = (bf16[1,36,768]{2,1,0:T(8,128)(2,1)}, bf16[1,36,768]{2,1,0:T(8,128)(2,1)S(1)}, u32[]{:S(2)}, u32[]{:S(2)}) collective-permute-start(bf16[1,36,768]{2,1,0:T(8,128)(2,1)} %refs_0_.3), channel_id=1, source_target_pairs={{0,24},{4,28},{8,16},{12,20},{16,8},{20,12},{24,0},{28,4},{1,25},{... | collective-permute-start | bytes 165896 | tf_op jit(solution)/shard_map/ppermute | solution.py:211
  3.9 0.5 %collective-permute-start.1 = (bf16[1,36,768]{2,1,0:T(8,128)(2,1)}, bf16[1,36,768]{2,1,0:T(8,128)(2,1)S(1)}, u32[]{:S(2)}, u32[]{:S(2)}) collective-permute-start(bf16[1,36,768]{2,1,0:T(8,128)(2,1)} %refs_0_.3), channel_id=1, source_target_pairs={{0,16},{4,20},{8,24},{12,28},{16,0},{20,4},{24,8},{28,12},{1,17},{... | collective-permute-start | bytes 165896 | tf_op jit(solution)/shard_map/ppermute | solution.py:211
  4.5 3.0 %collective-permute-start.6 = (bf16[1,36,768]{2,1,0:T(8,128)(2,1)}, bf16[1,36,768]{2,1,0:T(8,128)(2,1)S(1)}, u32[]{:S(2)}, u32[]{:S(2)}) collective-permute-start(bf16[1,36,768]{2,1,0:T(8,128)(2,1)} %refs_4_.2), channel_id=1, source_target_pairs={{0,2},{1,3},{2,0},{3,1},{4,6},{5,7},{6,4},{7,5},{8,10},{9,11},{10,... | collective-permute-start | bytes 165896 | tf_op jit(solution)/shard_map/ppermute | solution.py:208
  7.5 1.6 %collective-permute-start.4 = (bf16[1,36,768]{2,1,0:T(8,128)(2,1)}, bf16[1,36,768]{2,1,0:T(8,128)(2,1)S(1)}, u32[]{:S(2)}, u32[]{:S(2)}) collective-permute-start(bf16[1,36,768]{2,1,0:T(8,128)(2,1)} %refs_4_.2), channel_id=1, source_target_pairs={{0,1},{1,0},{2,3},{3,2},{4,5},{5,4},{6,7},{7,6},{8,9},{9,8},{10,11... | collective-permute-start | bytes 165896 | tf_op jit(solution)/shard_map/ppermute | solution.py:208
  9.1 2.8 %collective-permute-start.8 = (bf16[1,36,768]{2,1,0:T(8,128)(2,1)}, bf16[1,36,768]{2,1,0:T(8,128)(2,1)S(1)}, u32[]{:S(2)}, u32[]{:S(2)}) collective-permute-start(bf16[1,36,768]{2,1,0:T(8,128)(2,1)} %refs_4_.2), channel_id=1, source_target_pairs={{0,3},{1,2},{2,1},{3,0},{4,7},{5,6},{6,5},{7,4},{8,11},{9,10},{10,... | collective-permute-start | bytes 165896 | tf_op jit(solution)/shard_map/ppermute | solution.py:208
  11.9 1.6 %collective-permute-start.11 = (bf16[1,36,768]{2,1,0:T(8,128)(2,1)}, bf16[1,36,768]{2,1,0:T(8,128)(2,1)S(1)}, u32[]{:S(2)}, u32[]{:S(2)}) collective-permute-start(bf16[1,36,768]{2,1,0:T(8,128)(2,1)} %refs_8_.1), channel_id=1, source_target_pairs={{0,1},{1,0},{2,3},{3,2},{4,5},{5,4},{6,7},{7,6},{8,9},{9,8},{10,11... | collective-permute-start | bytes 165896 | tf_op jit(solution)/shard_map/ppermute | solution.py:209
  13.6 2.8 %collective-permute-start.15 = (bf16[1,36,768]{2,1,0:T(8,128)(2,1)}, bf16[1,36,768]{2,1,0:T(8,128)(2,1)S(1)}, u32[]{:S(2)}, u32[]{:S(2)}) collective-permute-start(bf16[1,36,768]{2,1,0:T(8,128)(2,1)} %refs_8_.1), channel_id=1, source_target_pairs={{0,3},{1,2},{2,1},{3,0},{4,7},{5,6},{6,5},{7,4},{8,11},{9,10},{10,... | collective-permute-start | bytes 165896 | tf_op jit(solution)/shard_map/ppermute | solution.py:209
  16.6 1.7 %collective-permute-done.13.refs_10_ = bf16[1,36,768]{2,1,0:T(8,128)(2,1)S(1)} collective-permute-done((bf16[1,36,768]{2,1,0:T(8,128)(2,1)}, bf16[1,36,768]{2,1,0:T(8,128)(2,1)S(1)}, u32[]{:S(2)}, u32[]{:S(2)}) %collective-permute-start.13) | collective-permute-done | bytes 55328 | tf_op jit(solution)/shard_map/ppermute | solution.py:209
  18.3 0.5 %collective-permute-start.9 = (bf16[1,36,768]{2,1,0:T(8,128)(2,1)S(1)}, bf16[1,36,768]{2,1,0:T(8,128)(2,1)S(1)}, u32[]{:S(2)}, u32[]{:S(2)}) collective-permute-start(bf16[1,36,768]{2,1,0:T(8,128)(2,1)S(1)} %collective-permute-done.8.refs_7_), channel_id=1, source_target_pairs={{0,4},{4,0},{8,12},{12,8},{16,20},{20,16},{24,28},{28,24},{1,5},{5... | collective-permute-start | bytes 165896 | tf_op jit(solution)/shard_map/ppermute | solution.py:212
  18.9 1.2 %collective-permute-done.15.refs_11_ = bf16[1,36,768]{2,1,0:T(8,128)(2,1)S(1)} collective-permute-done((bf16[1,36,768]{2,1,0:T(8,128)(2,1)}, bf16[1,36,768]{2,1,0:T(8,128)(2,1)S(1)}, u32[]{:S(2)}, u32[]{:S(2)}) %collective-permute-start.15) | collective-permute-done | bytes 55328 | tf_op jit(solution)/shard_map/ppermute | solution.py:209
  20.1 0.5 %collective-permute-start.16 = (bf16[1,36,768]{2,1,0:T(8,128)(2,1)S(1)}, bf16[1,36,768]{2,1,0:T(8,128)(2,1)S(1)}, u32[]{:S(2)}, u32[]{:S(2)}) collective-permute-start(bf16[1,36,768]{2,1,0:T(8,128)(2,1)S(1)} %collective-permute-done.15.refs_11_), channel_id=1, source_target_pairs={{0,4},{4,0},{8,12},{12,8},{16,20},{20,16},{24,28},{28,24},{1,5},{5... | collective-permute-start | bytes 165896 | tf_op jit(solution)/shard_map/ppermute | solution.py:213
  20.6 0.8 %copy-done.3 = bf16[1,36,768]{2,1,0:T(8,128)(2,1)S(1)} copy-done((bf16[1,36,768]{2,1,0:T(8,128)(2,1)S(1)}, bf16[1,36,768]{2,1,0:T(8,128)(2,1)}, u32[]{:S(2)}) %copy-start.3) | copy-done | bytes 55320
  21.5 0.8 %copy-done.4 = bf16[1,36,768]{2,1,0:T(8,128)(2,1)S(1)} copy-done((bf16[1,36,768]{2,1,0:T(8,128)(2,1)S(1)}, bf16[1,36,768]{2,1,0:T(8,128)(2,1)}, u32[]{:S(2)}) %copy-start.4) | copy-done | bytes 55320
  22.3 0.8 %copy-done.5 = bf16[1,36,768]{2,1,0:T(8,128)(2,1)S(1)} copy-done((bf16[1,36,768]{2,1,0:T(8,128)(2,1)S(1)}, bf16[1,36,768]{2,1,0:T(8,128)(2,1)}, u32[]{:S(2)}) %copy-start.5) | copy-done | bytes 55320
  23.1 1.4 %attention.2 = (bf16[1,36,768]{2,1,0:T(8,128)(2,1)S(1)}, bf16[1,36,768]{2,1,0:T(8,128)(2,1)S(1)}, bf16[1,36,768]{2,1,0:T(8,128)(2,1)S(1)}, bf16[1,36,768]{2,1,0:T(8,128)(2,1)S(1)}) custom-call(bf16[1,36,768]{2,1,0:T(8,128)(2,1)S(1)} %copy-done.3, bf16[1,36,768]{2,1,0:T(8,128)(2,1)S(1)} %collective-permute-done.refs_1_, ...), custom_call_target="tpu_custom_call" | custom-call | flops 63700992 | bytes 1048576 | tf_op jit(solution)/shard_map/attention/pallas_call | solution.py:94
  24.6 1.4 %attention.3 = (bf16[2,36,768]{2,1,0:T(8,128)(2,1)S(1)}, bf16[2,36,768]{2,1,0:T(8,128)(2,1)S(1)}, bf16[2,36,768]{2,1,0:T(8,128)(2,1)S(1)}, bf16[2,36,768]{2,1,0:T(8,128)(2,1)S(1)}) custom-call(bf16[1,36,768]{2,1,0:T(8,128)(2,1)S(1)} %copy-done.3, bf16[1,36,768]{2,1,0:T(8,128)(2,1)S(1)} %collective-permute-done.refs_1_, ...), custom_call_target="tpu_custom_call" | custom-call | flops 63700992 | bytes 1048576 | tf_op jit(solution)/shard_map/attention/pallas_call | solution.py:94
  26.1 1.6 %collective-permute-start.17 = (bf16[2,36,768]{2,1,0:T(8,128)(2,1)S(1)}, bf16[2,36,768]{2,1,0:T(8,128)(2,1)S(1)}, u32[]{:S(2)}, u32[]{:S(2)}) collective-permute-start(bf16[2,36,768]{2,1,0:T(8,128)(2,1)S(1)} %get-tuple-element.18), channel_id=1, source_target_pairs={{8,0},{12,4},{0,8},{4,12},{24,16},{28,20},{16,24},{20,28},{9,1},{1... | collective-permute-start | bytes 331784 | tf_op jit(solution)/shard_map/ppermute | solution.py:217
  27.6 1.5 %collective-permute-start.18 = (bf16[2,36,768]{2,1,0:T(8,128)(2,1)S(1)}, bf16[2,36,768]{2,1,0:T(8,128)(2,1)S(1)}, u32[]{:S(2)}, u32[]{:S(2)}) collective-permute-start(bf16[2,36,768]{2,1,0:T(8,128)(2,1)S(1)} %get-tuple-element.19), channel_id=1, source_target_pairs={{16,0},{20,4},{24,8},{28,12},{0,16},{4,20},{8,24},{12,28},{17,1},{... | collective-permute-start | bytes 331784 | tf_op jit(solution)/shard_map/ppermute | solution.py:217
  29.1 0.5 %collective-permute-start.19 = (bf16[2,36,768]{2,1,0:T(8,128)(2,1)S(1)}, bf16[2,36,768]{2,1,0:T(8,128)(2,1)S(1)}, u32[]{:S(2)}, u32[]{:S(2)}) collective-permute-start(bf16[2,36,768]{2,1,0:T(8,128)(2,1)S(1)} %get-tuple-element.20), channel_id=1, source_target_pairs={{24,0},{28,4},{16,8},{20,12},{8,16},{12,20},{0,24},{4,28},{25,1},{... | collective-permute-start | bytes 331784 | tf_op jit(solution)/shard_map/ppermute | solution.py:217
  29.6 1.9 %collective-permute-done.17.refs_1_ = bf16[2,36,768]{2,1,0:T(8,128)(2,1)S(1)} collective-permute-done((bf16[2,36,768]{2,1,0:T(8,128)(2,1)S(1)}, bf16[2,36,768]{2,1,0:T(8,128)(2,1)S(1)}, u32[]{:S(2)}, u32[]{:S(2)}) %collective-permute-start.17) | collective-permute-done | bytes 110624 | tf_op jit(solution)/shard_map/ppermute | solution.py:217
  31.5 3.7 %collective-permute-done.18.refs_2_ = bf16[2,36,768]{2,1,0:T(8,128)(2,1)S(1)} collective-permute-done((bf16[2,36,768]{2,1,0:T(8,128)(2,1)S(1)}, bf16[2,36,768]{2,1,0:T(8,128)(2,1)S(1)}, u32[]{:S(2)}, u32[]{:S(2)}) %collective-permute-start.18) | collective-permute-done | bytes 110624 | tf_op jit(solution)/shard_map/ppermute | solution.py:217
  35.2 1.3 %copy-done.1 = bf16[768,768]{1,0:T(8,128)(2,1)S(1)} copy-done((bf16[768,768]{1,0:T(8,128)(2,1)S(1)}, bf16[768,768]{1,0:T(8,128)(2,1)}, u32[]{:S(2)}) %copy-start.1) | copy-done | bytes 1179672
  36.5 1.3 %copy-done.2 = bf16[768,768]{1,0:T(8,128)(2,1)S(1)} copy-done((bf16[768,768]{1,0:T(8,128)(2,1)S(1)}, bf16[768,768]{1,0:T(8,128)(2,1)}, u32[]{:S(2)}) %copy-start.2) | copy-done | bytes 1179672
  37.8 2.5 %mix.1 = bf16[1,36,768]{2,1,0:T(8,128)(2,1)} custom-call(bf16[2,36,768]{2,1,0:T(8,128)(2,1)S(1)} %get-tuple-element.17.refs_0_, bf16[2,36,768]{2,1,0:T(8,128)(2,1)S(1)} %collective-permute-done.17.refs_1_, bf16[2,36,768]{2,1,0:T(8,128)(2,1)S(1)} %collective-permute-done.18.refs_2_, bf16[2,36,768]{2,1,0:T(8,128)(2,1)S(1)} %collective-permute-done.19.refs_3_, ...), custom_call_target="tpu_custom_call" | custom-call | flops 679477248 | bytes 4194304 | tf_op jit(solution)/shard_map/mix/pallas_call | solution.py:171
  (31 shorter events, 0.4 us)
Async XLA Ops:
  0.0 35.2 %copy-start = (bf16[768,768]{1,0:T(8,128)(2,1)S(1)}, bf16[768,768]{1,0:T(8,128)(2,1)}, u32[]{:S(2)}) copy-start(bf16[768,768]{1,0:T(8,128)(2,1)} %refs_4_.3) | copy-start | bytes 3538948
  0.0 9.1 %collective-permute-start.2 = (bf16[1,36,768]{2,1,0:T(8,128)(2,1)}, bf16[1,36,768]{2,1,0:T(8,128)(2,1)S(1)}, u32[]{:S(2)}, u32[]{:S(2)}) collective-permute-start(bf16[1,36,768]{2,1,0:T(8,128)(2,1)} %refs_0_.3), channel_id=1, source_target_pairs={{0,24},{4,28},{8,16},{12,20},{16,8},{20,12},{24,0},{28,4},{1,25},{... | collective-permute-start | bytes 165896 | tf_op jit(solution)/shard_map/ppermute | solution.py:211
  3.9 5.2 %collective-permute-start.1 = (bf16[1,36,768]{2,1,0:T(8,128)(2,1)}, bf16[1,36,768]{2,1,0:T(8,128)(2,1)S(1)}, u32[]{:S(2)}, u32[]{:S(2)}) collective-permute-start(bf16[1,36,768]{2,1,0:T(8,128)(2,1)} %refs_0_.3), channel_id=1, source_target_pairs={{0,16},{4,20},{8,24},{12,28},{16,0},{20,4},{24,8},{28,12},{1,17},{... | collective-permute-start | bytes 165896 | tf_op jit(solution)/shard_map/ppermute | solution.py:211
  4.4 7.5 %collective-permute-start = (bf16[1,36,768]{2,1,0:T(8,128)(2,1)}, bf16[1,36,768]{2,1,0:T(8,128)(2,1)S(1)}, u32[]{:S(2)}, u32[]{:S(2)}) collective-permute-start(bf16[1,36,768]{2,1,0:T(8,128)(2,1)} %refs_0_.3), channel_id=1, source_target_pairs={{0,8},{4,12},{8,0},{12,4},{16,24},{20,28},{24,16},{28,20},{1,9},{5... | collective-permute-start | bytes 165896 | tf_op jit(solution)/shard_map/ppermute | solution.py:211
  4.5 7.4 %collective-permute-start.6 = (bf16[1,36,768]{2,1,0:T(8,128)(2,1)}, bf16[1,36,768]{2,1,0:T(8,128)(2,1)S(1)}, u32[]{:S(2)}, u32[]{:S(2)}) collective-permute-start(bf16[1,36,768]{2,1,0:T(8,128)(2,1)} %refs_4_.2), channel_id=1, source_target_pairs={{0,2},{1,3},{2,0},{3,1},{4,6},{5,7},{6,4},{7,5},{8,10},{9,11},{10,... | collective-permute-start | bytes 165896 | tf_op jit(solution)/shard_map/ppermute | solution.py:208
  7.5 6.1 %collective-permute-start.4 = (bf16[1,36,768]{2,1,0:T(8,128)(2,1)}, bf16[1,36,768]{2,1,0:T(8,128)(2,1)S(1)}, u32[]{:S(2)}, u32[]{:S(2)}) collective-permute-start(bf16[1,36,768]{2,1,0:T(8,128)(2,1)} %refs_4_.2), channel_id=1, source_target_pairs={{0,1},{1,0},{2,3},{3,2},{4,5},{5,4},{6,7},{7,6},{8,9},{9,8},{10,11... | collective-permute-start | bytes 165896 | tf_op jit(solution)/shard_map/ppermute | solution.py:208
  9.1 4.5 %collective-permute-start.3 = (bf16[1,36,768]{2,1,0:T(8,128)(2,1)}, bf16[1,36,768]{2,1,0:T(8,128)(2,1)S(1)}, u32[]{:S(2)}, u32[]{:S(2)}) collective-permute-start(bf16[1,36,768]{2,1,0:T(8,128)(2,1)} %refs_4_.2), channel_id=1, source_target_pairs={{0,4},{4,0},{8,12},{12,8},{16,20},{20,16},{24,28},{28,24},{1,5},{5... | collective-permute-start | bytes 165896 | tf_op jit(solution)/shard_map/ppermute | solution.py:212
  9.1 7.3 %collective-permute-start.8 = (bf16[1,36,768]{2,1,0:T(8,128)(2,1)}, bf16[1,36,768]{2,1,0:T(8,128)(2,1)S(1)}, u32[]{:S(2)}, u32[]{:S(2)}) collective-permute-start(bf16[1,36,768]{2,1,0:T(8,128)(2,1)} %refs_4_.2), channel_id=1, source_target_pairs={{0,3},{1,2},{2,1},{3,0},{4,7},{5,6},{6,5},{7,4},{8,11},{9,10},{10,... | collective-permute-start | bytes 165896 | tf_op jit(solution)/shard_map/ppermute | solution.py:208
  11.9 6.4 %collective-permute-start.13 = (bf16[1,36,768]{2,1,0:T(8,128)(2,1)}, bf16[1,36,768]{2,1,0:T(8,128)(2,1)S(1)}, u32[]{:S(2)}, u32[]{:S(2)}) collective-permute-start(bf16[1,36,768]{2,1,0:T(8,128)(2,1)} %refs_8_.1), channel_id=1, source_target_pairs={{0,2},{1,3},{2,0},{3,1},{4,6},{5,7},{6,4},{7,5},{8,10},{9,11},{10,... | collective-permute-start | bytes 165896 | tf_op jit(solution)/shard_map/ppermute | solution.py:209
  11.9 6.4 %collective-permute-start.11 = (bf16[1,36,768]{2,1,0:T(8,128)(2,1)}, bf16[1,36,768]{2,1,0:T(8,128)(2,1)S(1)}, u32[]{:S(2)}, u32[]{:S(2)}) collective-permute-start(bf16[1,36,768]{2,1,0:T(8,128)(2,1)} %refs_8_.1), channel_id=1, source_target_pairs={{0,1},{1,0},{2,3},{3,2},{4,5},{5,4},{6,7},{7,6},{8,9},{9,8},{10,11... | collective-permute-start | bytes 165896 | tf_op jit(solution)/shard_map/ppermute | solution.py:209
  13.6 5.2 %collective-permute-start.10 = (bf16[1,36,768]{2,1,0:T(8,128)(2,1)}, bf16[1,36,768]{2,1,0:T(8,128)(2,1)S(1)}, u32[]{:S(2)}, u32[]{:S(2)}) collective-permute-start(bf16[1,36,768]{2,1,0:T(8,128)(2,1)} %refs_8_.1), channel_id=1, source_target_pairs={{0,4},{4,0},{8,12},{12,8},{16,20},{20,16},{24,28},{28,24},{1,5},{5... | collective-permute-start | bytes 165896 | tf_op jit(solution)/shard_map/ppermute | solution.py:213
  13.6 6.5 %collective-permute-start.15 = (bf16[1,36,768]{2,1,0:T(8,128)(2,1)}, bf16[1,36,768]{2,1,0:T(8,128)(2,1)S(1)}, u32[]{:S(2)}, u32[]{:S(2)}) collective-permute-start(bf16[1,36,768]{2,1,0:T(8,128)(2,1)} %refs_8_.1), channel_id=1, source_target_pairs={{0,3},{1,2},{2,1},{3,0},{4,7},{5,6},{6,5},{7,4},{8,11},{9,10},{10,... | collective-permute-start | bytes 165896 | tf_op jit(solution)/shard_map/ppermute | solution.py:209
  16.4 3.7 %collective-permute-start.7 = (bf16[1,36,768]{2,1,0:T(8,128)(2,1)S(1)}, bf16[1,36,768]{2,1,0:T(8,128)(2,1)S(1)}, u32[]{:S(2)}, u32[]{:S(2)}) collective-permute-start(bf16[1,36,768]{2,1,0:T(8,128)(2,1)S(1)} %collective-permute-done.6.refs_6_), channel_id=1, source_target_pairs={{0,4},{4,0},{8,12},{12,8},{16,20},{20,16},{24,28},{28,24},{1,5},{5... | collective-permute-start | bytes 165896 | tf_op jit(solution)/shard_map/ppermute | solution.py:212
  18.3 6.3 %collective-permute-start.5 = (bf16[1,36,768]{2,1,0:T(8,128)(2,1)S(1)}, bf16[1,36,768]{2,1,0:T(8,128)(2,1)S(1)}, u32[]{:S(2)}, u32[]{:S(2)}) collective-permute-start(bf16[1,36,768]{2,1,0:T(8,128)(2,1)S(1)} %collective-permute-done.4.refs_5_), channel_id=1, source_target_pairs={{0,4},{4,0},{8,12},{12,8},{16,20},{20,16},{24,28},{28,24},{1,5},{5... | collective-permute-start | bytes 165896 | tf_op jit(solution)/shard_map/ppermute | solution.py:212
  18.3 6.3 %collective-permute-start.9 = (bf16[1,36,768]{2,1,0:T(8,128)(2,1)S(1)}, bf16[1,36,768]{2,1,0:T(8,128)(2,1)S(1)}, u32[]{:S(2)}, u32[]{:S(2)}) collective-permute-start(bf16[1,36,768]{2,1,0:T(8,128)(2,1)S(1)} %collective-permute-done.8.refs_7_), channel_id=1, source_target_pairs={{0,4},{4,0},{8,12},{12,8},{16,20},{20,16},{24,28},{28,24},{1,5},{5... | collective-permute-start | bytes 165896 | tf_op jit(solution)/shard_map/ppermute | solution.py:212
  18.8 5.8 %collective-permute-start.14 = (bf16[1,36,768]{2,1,0:T(8,128)(2,1)S(1)}, bf16[1,36,768]{2,1,0:T(8,128)(2,1)S(1)}, u32[]{:S(2)}, u32[]{:S(2)}) collective-permute-start(bf16[1,36,768]{2,1,0:T(8,128)(2,1)S(1)} %collective-permute-done.13.refs_10_), channel_id=1, source_target_pairs={{0,4},{4,0},{8,12},{12,8},{16,20},{20,16},{24,28},{28,24},{1,5},{5... | collective-permute-start | bytes 165896 | tf_op jit(solution)/shard_map/ppermute | solution.py:213
  20.1 4.5 %collective-permute-start.12 = (bf16[1,36,768]{2,1,0:T(8,128)(2,1)S(1)}, bf16[1,36,768]{2,1,0:T(8,128)(2,1)S(1)}, u32[]{:S(2)}, u32[]{:S(2)}) collective-permute-start(bf16[1,36,768]{2,1,0:T(8,128)(2,1)S(1)} %collective-permute-done.11.refs_9_), channel_id=1, source_target_pairs={{0,4},{4,0},{8,12},{12,8},{16,20},{20,16},{24,28},{28,24},{1,5},{5... | collective-permute-start | bytes 165896 | tf_op jit(solution)/shard_map/ppermute | solution.py:213
  20.1 4.5 %collective-permute-start.16 = (bf16[1,36,768]{2,1,0:T(8,128)(2,1)S(1)}, bf16[1,36,768]{2,1,0:T(8,128)(2,1)S(1)}, u32[]{:S(2)}, u32[]{:S(2)}) collective-permute-start(bf16[1,36,768]{2,1,0:T(8,128)(2,1)S(1)} %collective-permute-done.15.refs_11_), channel_id=1, source_target_pairs={{0,4},{4,0},{8,12},{12,8},{16,20},{20,16},{24,28},{28,24},{1,5},{5... | collective-permute-start | bytes 165896 | tf_op jit(solution)/shard_map/ppermute | solution.py:213
  20.6 0.8 %copy-start.3 = (bf16[1,36,768]{2,1,0:T(8,128)(2,1)S(1)}, bf16[1,36,768]{2,1,0:T(8,128)(2,1)}, u32[]{:S(2)}) copy-start(bf16[1,36,768]{2,1,0:T(8,128)(2,1)} %refs_0_.3) | copy-start | bytes 165892
  26.1 5.5 %collective-permute-start.17 = (bf16[2,36,768]{2,1,0:T(8,128)(2,1)S(1)}, bf16[2,36,768]{2,1,0:T(8,128)(2,1)S(1)}, u32[]{:S(2)}, u32[]{:S(2)}) collective-permute-start(bf16[2,36,768]{2,1,0:T(8,128)(2,1)S(1)} %get-tuple-element.18), channel_id=1, source_target_pairs={{8,0},{12,4},{0,8},{4,12},{24,16},{28,20},{16,24},{20,28},{9,1},{1... | collective-permute-start | bytes 331784 | tf_op jit(solution)/shard_map/ppermute | solution.py:217
  27.6 7.6 %collective-permute-start.18 = (bf16[2,36,768]{2,1,0:T(8,128)(2,1)S(1)}, bf16[2,36,768]{2,1,0:T(8,128)(2,1)S(1)}, u32[]{:S(2)}, u32[]{:S(2)}) collective-permute-start(bf16[2,36,768]{2,1,0:T(8,128)(2,1)S(1)} %get-tuple-element.19), channel_id=1, source_target_pairs={{16,0},{20,4},{24,8},{28,12},{0,16},{4,20},{8,24},{12,28},{17,1},{... | collective-permute-start | bytes 331784 | tf_op jit(solution)/shard_map/ppermute | solution.py:217
  29.1 6.1 %collective-permute-start.19 = (bf16[2,36,768]{2,1,0:T(8,128)(2,1)S(1)}, bf16[2,36,768]{2,1,0:T(8,128)(2,1)S(1)}, u32[]{:S(2)}, u32[]{:S(2)}) collective-permute-start(bf16[2,36,768]{2,1,0:T(8,128)(2,1)S(1)} %get-tuple-element.20), channel_id=1, source_target_pairs={{24,0},{28,4},{16,8},{20,12},{8,16},{12,20},{0,24},{4,28},{25,1},{... | collective-permute-start | bytes 331784 | tf_op jit(solution)/shard_map/ppermute | solution.py:217
  35.2 1.3 %copy-start.1 = (bf16[768,768]{1,0:T(8,128)(2,1)S(1)}, bf16[768,768]{1,0:T(8,128)(2,1)}, u32[]{:S(2)}) copy-start(bf16[768,768]{1,0:T(8,128)(2,1)} %refs_5_.1) | copy-start | bytes 3538948
  36.5 1.3 %copy-start.2 = (bf16[768,768]{1,0:T(8,128)(2,1)S(1)}, bf16[768,768]{1,0:T(8,128)(2,1)}, u32[]{:S(2)}) copy-start(bf16[768,768]{1,0:T(8,128)(2,1)} %refs_6_.1) | copy-start | bytes 3538948
  (2 other events, 1.7 us)

commit v2 on v1

--- a/solution.py
+++ b/solution.py
@@ -11,7 +11,12 @@
 HEADS = 12
 LANES = 128
 VMEM = pl.BlockSpec(memory_space=pltpu.VMEM)
+FAR = pl.BlockSpec(memory_space=pltpu.HBM)
 NT = (((1,), (1,)), ((), ()))
+
+
+def far(array):
+    return pltpu.with_memory_space_constraint(array, pltpu.HBM)
 
 
 def ceil_to(value, unit):
@@ -57,54 +62,105 @@
         put(slab, total)
 
 
+def pair_kernel(key, value, out, sems):
+    copies = [
+        pltpu.make_async_copy(ref.at[0], out.at[index], sems.at[index])
+        for index, ref in enumerate((key, value))
+    ]
+    for copy in copies:
+        copy.start()
+    for copy in copies:
+        copy.wait()
+
+
+def pair(key, value):
+    return pl.pallas_call(
+        pair_kernel,
+        out_shape=pltpu.VMEM((2,) + key.shape[1:], key.dtype),
+        in_specs=[FAR] * 2,
+        out_specs=VMEM,
+        scratch_shapes=[pltpu.SemaphoreType.DMA((2,))],
+        name="pair",
+    )(far(key), far(value))
+
+
+def stage_kernel(arrived, *refs):
+    queries, own, weights = refs[:arrived], refs[arrived], refs[arrived + 1 : arrived + 4]
+    stacked, *held = refs[arrived + 4 : arrived + 8]
+    stage, own_block, sems = refs[arrived + 8 :]
+    copies = [
+        pltpu.make_async_copy(source, target, sems.at[index])
+        for index, (source, target) in enumerate(zip((own, *weights), (own_block, *held)))
+    ]
+    for copy in copies:
+        copy.start()
+    copies[0].wait()
+    stacked[...] = stack_rows([own_block[0]] + [ref[0] for ref in queries], stage)
+    for copy in copies[1:]:
+        copy.wait()
+
+
+def stage_operands(arrived, own, weights):
+    _, rows, width = own.shape
+    total = (len(arrived) + 1) * ceil_to(rows, 8)
+    return pl.pallas_call(
+        functools.partial(stage_kernel, len(arrived)),
+        out_shape=[pltpu.VMEM((total, width), own.dtype)]
+        + [pltpu.VMEM(matrix.shape, matrix.dtype) for matrix in weights],
+        in_specs=[VMEM] * len(arrived) + [FAR] * 4,
+        out_specs=[VMEM] * 4,
+        scratch_shapes=[
+            pltpu.VMEM((total, width), jnp.float32),
+            pltpu.VMEM(own.shape, own.dtype),
+            pltpu.SemaphoreType.DMA((4,)),
+        ],
+        compiler_params=pltpu.CompilerParams(vmem_limit_bytes=32 << 20),
+        cost_estimate=pl.CostEstimate(flops=0, bytes_accessed=8 << 20, transcendentals=0),
+        name="stage",
+    )(*arrived, far(own), *map(far, weights))
+
+
 def attention_kernel(head_width, query_count, block_count, has_earlier, *refs):
-    queries = refs[:query_count]
-    keys = refs[query_count : query_count + block_count]
-    values = refs[query_count + block_count : query_count + 2 * block_count]
-    refs = refs[query_count + 2 * block_count :]
+    query, blocks = refs[0], refs[1 : 1 + block_count]
+    refs = refs[1 + block_count :]
     earlier = refs[:query_count] if has_earlier else ()
     refs = refs[len(earlier) :]
-    outs, (query_stage, key_stage, value_stage) = refs[:query_count], refs[query_count:]
-    rows = queries[0].shape[-2]
-    pitch = ceil_to(rows, 8)
-    query = stack_rows([ref[0] for ref in queries], query_stage)
-    key = stack_rows([ref[0] for ref in keys], key_stage)
-    value = stack_rows([ref[0] for ref in values], value_stage)
+    outs, (key_stage, value_stage) = refs[:query_count], refs[query_count:]
+    rows = blocks[0].shape[-2]
+    pitch = ceil_to(rows, 8)
+    key = stack_rows([ref[0] for ref in blocks], key_stage)
+    value = stack_rows([ref[1] for ref in blocks], value_stage)
     place = lax.broadcasted_iota(jnp.int32, (1, key.shape[0]), 1)
     valid = lax.rem(place, pitch) < rows
 
     def put(slab, pooled):
-        for index in range(query_count):
-            outs[index][outs[index].shape[0] - 1, :, pl.ds(slab * LANES, LANES)] = pooled[
+        for index, out in enumerate(outs):
+            out[out.shape[0] - 1, :, pl.ds(slab * LANES, LANES)] = pooled[
                 index * pitch : index * pitch + rows
             ].astype(jnp.bfloat16)
 
-    attend(query, key, value, valid, head_width, put)
+    attend(query[...], key, value, valid, head_width, put)
     for index, ref in enumerate(earlier):
         outs[index][0] = ref[0]
 
 
-def attention(queries, keys, values, earlier=()):
-    _, rows, width = queries[0].shape
-    pitch = ceil_to(rows, 8)
-    count = len(queries)
-    kernel = functools.partial(attention_kernel, width // HEADS, count, len(keys), bool(earlier))
-    flops = 4 * count * rows * len(keys) * rows * width
+def attention(query, blocks, earlier=()):
+    _, rows, width = blocks[0].shape
+    pitch = ceil_to(rows, 8)
+    count = query.shape[0] // pitch
+    kernel = functools.partial(attention_kernel, width // HEADS, count, len(blocks), bool(earlier))
+    flops = 4 * count * rows * len(blocks) * rows * width
     shape = jax.ShapeDtypeStruct((2 if earlier else 1, rows, width), jnp.bfloat16)
     return pl.pallas_call(
         kernel,
         out_shape=[shape] * count,
-        in_specs=[VMEM] * (count + 2 * len(keys) + len(earlier)),
+        in_specs=[VMEM] * (1 + len(blocks) + len(earlier)),
         out_specs=[VMEM] * count,
-        scratch_shapes=[
-            pltpu.VMEM((count * pitch, width), jnp.float32),
-            pltpu.VMEM((len(keys) * pitch, width), jnp.float32),
-            pltpu.VMEM((len(keys) * pitch, width), jnp.float32),
-        ],
-        compiler_params=pltpu.CompilerParams(vmem_limit_bytes=48 << 20),
+        scratch_shapes=[pltpu.VMEM((len(blocks) * pitch, width), jnp.float32)] * 2,
+        compiler_params=pltpu.CompilerParams(vmem_limit_bytes=32 << 20),
         cost_estimate=pl.CostEstimate(flops=flops, bytes_accessed=1 << 20, transcendentals=0),
         name="attention",
-    )(*queries, *keys, *values, *earlier)
+    )(query, *blocks, *earlier)
 
 
 def mix_kernel(head_width, pieces, *refs):
@@ -174,7 +230,7 @@
         in_specs=[VMEM] * (len(arrived) + 3),
         out_specs=VMEM,
         scratch_shapes=[pltpu.VMEM((total, width), jnp.float32)] * 3,
-        compiler_params=pltpu.CompilerParams(vmem_limit_bytes=48 << 20),
+        compiler_params=pltpu.CompilerParams(vmem_limit_bytes=32 << 20),
         cost_estimate=pl.CostEstimate(
             flops=4 * count * rows * width * width, bytes_accessed=4 << 20, transcendentals=0
         ),
@@ -203,20 +259,20 @@
     frame_total = lax.axis_size("frame")
     block_total = lax.axis_size("qblk")
     swap = [(index, index ^ 1) for index in range(frame_total)]
-    keys, values = [key_tokens], [value_tokens]
-    for there, _ in rounds(block_total):
-        keys.append(lax.ppermute(key_tokens, "qblk", there))
-        values.append(lax.ppermute(value_tokens, "qblk", there))
+    own_block = pair(key_tokens, value_tokens)
+    blocks = [own_block] + [lax.ppermute(own_block, "qblk", there) for there, _ in rounds(block_total)]
     paths = list(chip_rounds(frame_total))
-    queries = [query_tokens] + [lax.ppermute(query_tokens, "frame", there) for there, _ in paths]
-    other_keys = [lax.ppermute(block, "frame", swap) for block in keys]
-    other_values = [lax.ppermute(block, "frame", swap) for block in values]
-    own = attention(queries, keys, values)
-    pooled = attention(queries, other_keys, other_values, own)
+    queries = [lax.ppermute(query_tokens, "frame", there) for there, _ in paths]
+    query, *weights = stage_operands(queries, query_tokens, (w_query, w_key, w_value))
+    held = lax.optimization_barrier((query, *blocks))
+    query, blocks = held[0], held[1:]
+    other_blocks = [lax.ppermute(block, "frame", swap) for block in blocks]
+    own = attention(query, blocks)
+    pooled = attention(query, other_blocks, own)
     arrived = [pooled[0]] + [
         lax.ppermute(block, "frame", back) for block, (_, back) in zip(pooled[1:], paths)
     ]
-    return mix(arrived, w_query, w_key, w_value)
+    return mix(arrived, *weights)
 
 
 def solution(mesh):

time: 40.6 us -> 33.4 us (0.82)
  starting transfers between devices: 21.2 us -> 13.8 us
  local copies, waits for them, and re-layouts: 5.03 us -> 0 us
  Pallas kernels: 5.4 us -> 8.3 us
  waiting for transfers between devices: 8.59 us -> 11 us
    ppermute x17 -> x10, starting transfers between devices: 17.6 us -> 10.3 us  [the longest x3 4.79 us: per_device(): queries = [lax.ppermute(query_tokens, 'frame', there) for there, _ in paths]]
    unnamed x12 -> x0, local copies, waits for them, and re-layouts: 5.03 us -> none
    pallas_call x2 -> x4, Pallas kernels: 2.87 us -> 5.76 us  [the longest x2 2.83 us: attention(): pl.pallas_call(kernel, out_shape=[shape] * count, in_specs=[VMEM] * (1 +...]
    ppermute x17 -> x10, waiting for transfers between devices: 3 us -> 5.42 us  [the longest x3 5 us: per_device(): queries = [lax.ppermute(query_tokens, 'frame', there) for there, _ in paths]]
  transfers between devices with their start and end apart: 20 -> 13, of which waited for: 4 -> 5; matrix products, arithmetic and copies ran while one was open for 0% -> 0% of each run, Pallas kernels for 4% -> 13%
where the time goes in v2:
time: 33.4 us; the launch traced here: 33.2 us
  starting transfers between devices  13.8 us (41%)
  waiting for transfers between devices  11 us (33%)
  Pallas kernels  8.3 us (25%)
    ppermute x3, waiting for transfers between devices, per_device(): lax.ppermute(block, 'frame', back)  5.59 us
    ppermute x3, waiting for transfers between devices, per_device(): queries = [lax.ppermute(query_tokens, 'frame', there) for there, _ in paths]  5 us
    ppermute x3, starting transfers between devices, per_device(): queries = [lax.ppermute(query_tokens, 'frame', there) for there, _ in paths]  4.79 us
    ppermute x3, starting transfers between devices, per_device(): lax.ppermute(own_block, 'qblk', there)  4.45 us
    ppermute x3, starting transfers between devices, per_device(): lax.ppermute(block, 'frame', back)  3.55 us
    pallas_call x2, Pallas kernels, attention(): pl.pallas_call(kernel, out_shape=[shape] * count, in_specs=[VMEM] * (1 +...  2.83 us
    pallas_call x1, Pallas kernels, mix(): pl.pallas_call(functools.partial(mix_kernel, width // HEADS, len(arrived)...  2.54 us
    pallas_call x1, Pallas kernels, stage_operands(): pl.pallas_call(functools.partial(stage_kernel, len(arrived)), out_shape=[...  2.05 us
  transfers between devices with their start and end apart: 13, of which 5 were waited for; matrix products, arithmetic and copies ran while one was open for 0% of the time, Pallas kernels for 13%

profile of v2, /device:TPU:0, one launch (start us, length us, event | category | flops | bytes accessed | tf_op | source)
XLA Modules:
  0.0 33.2 jit_solution(9308444571383850655)
XLA Ops:
  0.0 3.0 %collective-permute-start.1 = (bf16[1,36,768]{2,1,0:T(8,128)(2,1)}, bf16[1,36,768]{2,1,0:T(8,128)(2,1)S(1)}, u32[]{:S(2)}, u32[]{:S(2)}) collective-permute-start(bf16[1,36,768]{2,1,0:T(8,128)(2,1)} %refs_3_.1), channel_id=1, source_target_pairs={{0,16},{4,20},{8,24},{12,28},{16,0},{20,4},{24,8},{28,12},{1,17},{... | collective-permute-start | bytes 165896 | tf_op jit(solution)/shard_map/ppermute | solution.py:265
  3.0 0.9 %pair.1.refs_1_ = bf16[2,36,768]{2,1,0:T(8,128)(2,1)S(1)} custom-call(bf16[1,36,768]{2,1,0:T(8,128)(2,1)} %key.1, bf16[1,36,768]{2,1,0:T(8,128)(2,1)} %value.1), custom_call_target="tpu_custom_call" | custom-call | tf_op jit(solution)/shard_map/pair/pallas_call | solution.py:77
  3.9 3.7 %collective-permute-start.5 = (bf16[2,36,768]{2,1,0:T(8,128)(2,1)S(1)}, bf16[2,36,768]{2,1,0:T(8,128)(2,1)S(1)}, u32[]{:S(2)}, u32[]{:S(2)}) collective-permute-start(bf16[2,36,768]{2,1,0:T(8,128)(2,1)S(1)} %pair.1.refs_1_), channel_id=1, source_target_pairs={{0,3},{1,2},{2,1},{3,0},{4,7},{5,6},{6,5},{7,4},{8,11},{9,10},{10,... | collective-permute-start | bytes 331784 | tf_op jit(solution)/shard_map/ppermute | solution.py:263
  7.5 0.0 collective-permute-start.4
  7.5 0.8 %collective-permute-start.3 = (bf16[2,36,768]{2,1,0:T(8,128)(2,1)S(1)}, bf16[2,36,768]{2,1,0:T(8,128)(2,1)S(1)}, u32[]{:S(2)}, u32[]{:S(2)}) collective-permute-start(bf16[2,36,768]{2,1,0:T(8,128)(2,1)S(1)} %pair.1.refs_1_), channel_id=1, source_target_pairs={{0,1},{1,0},{2,3},{3,2},{4,5},{5,4},{6,7},{7,6},{8,9},{9,8},{10,11... | collective-permute-start | bytes 331784 | tf_op jit(solution)/shard_map/ppermute | solution.py:263
  8.3 1.5 %collective-permute-start = (bf16[1,36,768]{2,1,0:T(8,128)(2,1)}, bf16[1,36,768]{2,1,0:T(8,128)(2,1)S(1)}, u32[]{:S(2)}, u32[]{:S(2)}) collective-permute-start(bf16[1,36,768]{2,1,0:T(8,128)(2,1)} %refs_3_.1), channel_id=1, source_target_pairs={{0,8},{4,12},{8,0},{12,4},{16,24},{20,28},{24,16},{28,20},{1,9},{5... | collective-permute-start | bytes 165896 | tf_op jit(solution)/shard_map/ppermute | solution.py:265
  9.8 0.0 collective-permute-done.1.refs_1_
  9.8 0.3 %collective-permute-start.2 = (bf16[1,36,768]{2,1,0:T(8,128)(2,1)}, bf16[1,36,768]{2,1,0:T(8,128)(2,1)S(1)}, u32[]{:S(2)}, u32[]{:S(2)}) collective-permute-start(bf16[1,36,768]{2,1,0:T(8,128)(2,1)} %refs_3_.1), channel_id=1, source_target_pairs={{0,24},{4,28},{8,16},{12,20},{16,8},{20,12},{24,0},{28,4},{1,25},{... | collective-permute-start | bytes 165896 | tf_op jit(solution)/shard_map/ppermute | solution.py:265
  10.1 2.6 %collective-permute-done.refs_0_ = bf16[1,36,768]{2,1,0:T(8,128)(2,1)S(1)} collective-permute-done((bf16[1,36,768]{2,1,0:T(8,128)(2,1)}, bf16[1,36,768]{2,1,0:T(8,128)(2,1)S(1)}, u32[]{:S(2)}, u32[]{:S(2)}) %collective-permute-start) | collective-permute-done | bytes 55328 | tf_op jit(solution)/shard_map/ppermute | solution.py:265
  12.7 2.4 %collective-permute-done.2.refs_2_ = bf16[1,36,768]{2,1,0:T(8,128)(2,1)S(1)} collective-permute-done((bf16[1,36,768]{2,1,0:T(8,128)(2,1)}, bf16[1,36,768]{2,1,0:T(8,128)(2,1)S(1)}, u32[]{:S(2)}, u32[]{:S(2)}) %collective-permute-start.2) | collective-permute-done | bytes 55328 | tf_op jit(solution)/shard_map/ppermute | solution.py:265
  15.1 2.1 %stage.1 = (bf16[160,768]{1,0:T(8,128)(2,1)S(1)}, bf16[768,768]{1,0:T(8,128)(2,1)S(1)}, bf16[768,768]{1,0:T(8,128)(2,1)S(1)}, bf16[768,768]{1,0:T(8,128)(2,1)S(1)}) custom-call(bf16[1,36,768]{2,1,0:T(8,128)(2,1)S(1)} %collective-permute-done.refs_0_, bf16[1,36,768]{2,1,0:T(8,128)(2,1)S(1)} %collective-permute-done.1.refs_1_, ...), custom_call_target="tpu_custom_call" | custom-call | bytes 8388608 | tf_op jit(solution)/shard_map/stage/pallas_call | solution.py:106
  17.2 0.0 collective-permute-done.5.refs_4_
  17.2 0.4 %collective-permute-done.4.refs_3_ = bf16[2,36,768]{2,1,0:T(8,128)(2,1)S(1)} collective-permute-done((bf16[2,36,768]{2,1,0:T(8,128)(2,1)S(1)}, bf16[2,36,768]{2,1,0:T(8,128)(2,1)S(1)}, u32[]{:S(2)}, u32[]{:S(2)}) %collective-permute-start.4) | collective-permute-done | bytes 110624 | tf_op jit(solution)/shard_map/ppermute | solution.py:263
  17.6 0.5 %collective-permute-start.7 = (bf16[2,36,768]{2,1,0:T(8,128)(2,1)S(1)}, bf16[2,36,768]{2,1,0:T(8,128)(2,1)S(1)}, u32[]{:S(2)}, u32[]{:S(2)}) collective-permute-start(bf16[2,36,768]{2,1,0:T(8,128)(2,1)S(1)} %collective-permute-done.3.refs_2_), channel_id=1, source_target_pairs={{0,4},{4,0},{8,12},{12,8},{16,20},{20,16},{24,28},{28,24},{1,5},{5... | collective-permute-start | bytes 331784 | tf_op jit(solution)/shard_map/ppermute | solution.py:269
  18.1 0.0 collective-permute-start.8
  18.1 0.5 %collective-permute-start.9 = (bf16[2,36,768]{2,1,0:T(8,128)(2,1)S(1)}, bf16[2,36,768]{2,1,0:T(8,128)(2,1)S(1)}, u32[]{:S(2)}, u32[]{:S(2)}) collective-permute-start(bf16[2,36,768]{2,1,0:T(8,128)(2,1)S(1)} %collective-permute-done.5.refs_4_), channel_id=1, source_target_pairs={{0,4},{4,0},{8,12},{12,8},{16,20},{20,16},{24,28},{28,24},{1,5},{5... | collective-permute-start | bytes 331784 | tf_op jit(solution)/shard_map/ppermute | solution.py:269
  18.6 1.4 %attention.2 = (bf16[1,36,768]{2,1,0:T(8,128)(2,1)S(1)}, bf16[1,36,768]{2,1,0:T(8,128)(2,1)S(1)}, bf16[1,36,768]{2,1,0:T(8,128)(2,1)S(1)}, bf16[1,36,768]{2,1,0:T(8,128)(2,1)S(1)}) custom-call(bf16[160,768]{1,0:T(8,128)(2,1)S(1)} %get-tuple-element.23.refs_0_, bf16[2,36,768]{2,1,0:T(8,128)(2,1)S(1)} %pair.1.refs_1_, ...), custom_call_target="tpu_custom_call" | custom-call | flops 63700992 | bytes 1048576 | tf_op jit(solution)/shard_map/attention/pallas_call | solution.py:154
  20.1 1.4 %attention.3 = (bf16[2,36,768]{2,1,0:T(8,128)(2,1)S(1)}, bf16[2,36,768]{2,1,0:T(8,128)(2,1)S(1)}, bf16[2,36,768]{2,1,0:T(8,128)(2,1)S(1)}, bf16[2,36,768]{2,1,0:T(8,128)(2,1)S(1)}) custom-call(bf16[160,768]{1,0:T(8,128)(2,1)S(1)} %get-tuple-element.23.refs_0_, bf16[2,36,768]{2,1,0:T(8,128)(2,1)S(1)} %collective-permute-done.6.refs_1_, ...), custom_call_target="tpu_custom_call" | custom-call | flops 63700992 | bytes 1048576 | tf_op jit(solution)/shard_map/attention/pallas_call | solution.py:154
  21.5 1.6 %collective-permute-start.10 = (bf16[2,36,768]{2,1,0:T(8,128)(2,1)S(1)}, bf16[2,36,768]{2,1,0:T(8,128)(2,1)S(1)}, u32[]{:S(2)}, u32[]{:S(2)}) collective-permute-start(bf16[2,36,768]{2,1,0:T(8,128)(2,1)S(1)} %get-tuple-element.33), channel_id=1, source_target_pairs={{8,0},{12,4},{0,8},{4,12},{24,16},{28,20},{16,24},{20,28},{9,1},{1... | collective-permute-start | bytes 331784 | tf_op jit(solution)/shard_map/ppermute | solution.py:273
  23.1 0.5 %collective-permute-start.11 = (bf16[2,36,768]{2,1,0:T(8,128)(2,1)S(1)}, bf16[2,36,768]{2,1,0:T(8,128)(2,1)S(1)}, u32[]{:S(2)}, u32[]{:S(2)}) collective-permute-start(bf16[2,36,768]{2,1,0:T(8,128)(2,1)S(1)} %get-tuple-element.34), channel_id=1, source_target_pairs={{16,0},{20,4},{24,8},{28,12},{0,16},{4,20},{8,24},{12,28},{17,1},{... | collective-permute-start | bytes 331784 | tf_op jit(solution)/shard_map/ppermute | solution.py:273
  23.6 1.5 %collective-permute-start.12 = (bf16[2,36,768]{2,1,0:T(8,128)(2,1)S(1)}, bf16[2,36,768]{2,1,0:T(8,128)(2,1)S(1)}, u32[]{:S(2)}, u32[]{:S(2)}) collective-permute-start(bf16[2,36,768]{2,1,0:T(8,128)(2,1)S(1)} %get-tuple-element.35), channel_id=1, source_target_pairs={{24,0},{28,4},{16,8},{20,12},{8,16},{12,20},{0,24},{4,28},{25,1},{... | collective-permute-start | bytes 331784 | tf_op jit(solution)/shard_map/ppermute | solution.py:273
  25.1 1.9 %collective-permute-done.10.refs_1_ = bf16[2,36,768]{2,1,0:T(8,128)(2,1)S(1)} collective-permute-done((bf16[2,36,768]{2,1,0:T(8,128)(2,1)S(1)}, bf16[2,36,768]{2,1,0:T(8,128)(2,1)S(1)}, u32[]{:S(2)}, u32[]{:S(2)}) %collective-permute-start.10) | collective-permute-done | bytes 110624 | tf_op jit(solution)/shard_map/ppermute | solution.py:273
  27.0 3.7 %collective-permute-done.11.refs_2_ = bf16[2,36,768]{2,1,0:T(8,128)(2,1)S(1)} collective-permute-done((bf16[2,36,768]{2,1,0:T(8,128)(2,1)S(1)}, bf16[2,36,768]{2,1,0:T(8,128)(2,1)S(1)}, u32[]{:S(2)}, u32[]{:S(2)}) %collective-permute-start.11) | collective-permute-done | bytes 110624 | tf_op jit(solution)/shard_map/ppermute | solution.py:273
  30.7 2.5 %mix.1 = bf16[1,36,768]{2,1,0:T(8,128)(2,1)} custom-call(bf16[2,36,768]{2,1,0:T(8,128)(2,1)S(1)} %get-tuple-element.32.refs_0_, bf16[2,36,768]{2,1,0:T(8,128)(2,1)S(1)} %collective-permute-done.10.refs_1_, bf16[2,36,768]{2,1,0:T(8,128)(2,1)S(1)} %collective-permute-done.11.refs_2_, bf16[2,36,768]{2,1,0:T(8,128)(2,1)S(1)} %collective-permute-done.12.refs_3_, ...), custom_call_target="tpu_custom_call" | custom-call | flops 679477248 | bytes 4194304 | tf_op jit(solution)/shard_map/mix/pallas_call | solution.py:227
  (7 shorter events, 0.0 us)
Async XLA Ops:
  0.0 9.8 %collective-permute-start.1 = (bf16[1,36,768]{2,1,0:T(8,128)(2,1)}, bf16[1,36,768]{2,1,0:T(8,128)(2,1)S(1)}, u32[]{:S(2)}, u32[]{:S(2)}) collective-permute-start(bf16[1,36,768]{2,1,0:T(8,128)(2,1)} %refs_3_.1), channel_id=1, source_target_pairs={{0,16},{4,20},{8,24},{12,28},{16,0},{20,4},{24,8},{28,12},{1,17},{... | collective-permute-start | bytes 165896 | tf_op jit(solution)/shard_map/ppermute | solution.py:265
  3.9 13.3 %collective-permute-start.5 = (bf16[2,36,768]{2,1,0:T(8,128)(2,1)S(1)}, bf16[2,36,768]{2,1,0:T(8,128)(2,1)S(1)}, u32[]{:S(2)}, u32[]{:S(2)}) collective-permute-start(bf16[2,36,768]{2,1,0:T(8,128)(2,1)S(1)} %pair.1.refs_1_), channel_id=1, source_target_pairs={{0,3},{1,2},{2,1},{3,0},{4,7},{5,6},{6,5},{7,4},{8,11},{9,10},{10,... | collective-permute-start | bytes 331784 | tf_op jit(solution)/shard_map/ppermute | solution.py:263
  7.5 10.1 %collective-permute-start.4 = (bf16[2,36,768]{2,1,0:T(8,128)(2,1)S(1)}, bf16[2,36,768]{2,1,0:T(8,128)(2,1)S(1)}, u32[]{:S(2)}, u32[]{:S(2)}) collective-permute-start(bf16[2,36,768]{2,1,0:T(8,128)(2,1)S(1)} %pair.1.refs_1_), channel_id=1, source_target_pairs={{0,2},{1,3},{2,0},{3,1},{4,6},{5,7},{6,4},{7,5},{8,10},{9,11},{10,... | collective-permute-start | bytes 331784 | tf_op jit(solution)/shard_map/ppermute | solution.py:263
  7.5 10.1 %collective-permute-start.3 = (bf16[2,36,768]{2,1,0:T(8,128)(2,1)S(1)}, bf16[2,36,768]{2,1,0:T(8,128)(2,1)S(1)}, u32[]{:S(2)}, u32[]{:S(2)}) collective-permute-start(bf16[2,36,768]{2,1,0:T(8,128)(2,1)S(1)} %pair.1.refs_1_), channel_id=1, source_target_pairs={{0,1},{1,0},{2,3},{3,2},{4,5},{5,4},{6,7},{7,6},{8,9},{9,8},{10,11... | collective-permute-start | bytes 331784 | tf_op jit(solution)/shard_map/ppermute | solution.py:263
  8.3 4.4 %collective-permute-start = (bf16[1,36,768]{2,1,0:T(8,128)(2,1)}, bf16[1,36,768]{2,1,0:T(8,128)(2,1)S(1)}, u32[]{:S(2)}, u32[]{:S(2)}) collective-permute-start(bf16[1,36,768]{2,1,0:T(8,128)(2,1)} %refs_3_.1), channel_id=1, source_target_pairs={{0,8},{4,12},{8,0},{12,4},{16,24},{20,28},{24,16},{28,20},{1,9},{5... | collective-permute-start | bytes 165896 | tf_op jit(solution)/shard_map/ppermute | solution.py:265
  9.8 5.3 %collective-permute-start.2 = (bf16[1,36,768]{2,1,0:T(8,128)(2,1)}, bf16[1,36,768]{2,1,0:T(8,128)(2,1)S(1)}, u32[]{:S(2)}, u32[]{:S(2)}) collective-permute-start(bf16[1,36,768]{2,1,0:T(8,128)(2,1)} %refs_3_.1), channel_id=1, source_target_pairs={{0,24},{4,28},{8,16},{12,20},{16,8},{20,12},{24,0},{28,4},{1,25},{... | collective-permute-start | bytes 165896 | tf_op jit(solution)/shard_map/ppermute | solution.py:265
  17.6 2.5 %collective-permute-start.6 = (bf16[2,36,768]{2,1,0:T(8,128)(2,1)S(1)}, bf16[2,36,768]{2,1,0:T(8,128)(2,1)S(1)}, u32[]{:S(2)}, u32[]{:S(2)}) collective-permute-start(bf16[2,36,768]{2,1,0:T(8,128)(2,1)S(1)} %pair.1.refs_1_), channel_id=1, source_target_pairs={{0,4},{4,0},{8,12},{12,8},{16,20},{20,16},{24,28},{28,24},{1,5},{5... | collective-permute-start | bytes 331784 | tf_op jit(solution)/shard_map/ppermute | solution.py:269
  17.6 2.5 %collective-permute-start.7 = (bf16[2,36,768]{2,1,0:T(8,128)(2,1)S(1)}, bf16[2,36,768]{2,1,0:T(8,128)(2,1)S(1)}, u32[]{:S(2)}, u32[]{:S(2)}) collective-permute-start(bf16[2,36,768]{2,1,0:T(8,128)(2,1)S(1)} %collective-permute-done.3.refs_2_), channel_id=1, source_target_pairs={{0,4},{4,0},{8,12},{12,8},{16,20},{20,16},{24,28},{28,24},{1,5},{5... | collective-permute-start | bytes 331784 | tf_op jit(solution)/shard_map/ppermute | solution.py:269
  18.1 2.0 %collective-permute-start.8 = (bf16[2,36,768]{2,1,0:T(8,128)(2,1)S(1)}, bf16[2,36,768]{2,1,0:T(8,128)(2,1)S(1)}, u32[]{:S(2)}, u32[]{:S(2)}) collective-permute-start(bf16[2,36,768]{2,1,0:T(8,128)(2,1)S(1)} %collective-permute-done.4.refs_3_), channel_id=1, source_target_pairs={{0,4},{4,0},{8,12},{12,8},{16,20},{20,16},{24,28},{28,24},{1,5},{5... | collective-permute-start | bytes 331784 | tf_op jit(solution)/shard_map/ppermute | solution.py:269
  18.1 2.0 %collective-permute-start.9 = (bf16[2,36,768]{2,1,0:T(8,128)(2,1)S(1)}, bf16[2,36,768]{2,1,0:T(8,128)(2,1)S(1)}, u32[]{:S(2)}, u32[]{:S(2)}) collective-permute-start(bf16[2,36,768]{2,1,0:T(8,128)(2,1)S(1)} %collective-permute-done.5.refs_4_), channel_id=1, source_target_pairs={{0,4},{4,0},{8,12},{12,8},{16,20},{20,16},{24,28},{28,24},{1,5},{5... | collective-permute-start | bytes 331784 | tf_op jit(solution)/shard_map/ppermute | solution.py:269
  21.5 5.5 %collective-permute-start.10 = (bf16[2,36,768]{2,1,0:T(8,128)(2,1)S(1)}, bf16[2,36,768]{2,1,0:T(8,128)(2,1)S(1)}, u32[]{:S(2)}, u32[]{:S(2)}) collective-permute-start(bf16[2,36,768]{2,1,0:T(8,128)(2,1)S(1)} %get-tuple-element.33), channel_id=1, source_target_pairs={{8,0},{12,4},{0,8},{4,12},{24,16},{28,20},{16,24},{20,28},{9,1},{1... | collective-permute-start | bytes 331784 | tf_op jit(solution)/shard_map/ppermute | solution.py:273
  23.1 7.6 %collective-permute-start.11 = (bf16[2,36,768]{2,1,0:T(8,128)(2,1)S(1)}, bf16[2,36,768]{2,1,0:T(8,128)(2,1)S(1)}, u32[]{:S(2)}, u32[]{:S(2)}) collective-permute-start(bf16[2,36,768]{2,1,0:T(8,128)(2,1)S(1)} %get-tuple-element.34), channel_id=1, source_target_pairs={{16,0},{20,4},{24,8},{28,12},{0,16},{4,20},{8,24},{12,28},{17,1},{... | collective-permute-start | bytes 331784 | tf_op jit(solution)/shard_map/ppermute | solution.py:273
  23.6 7.1 %collective-permute-start.12 = (bf16[2,36,768]{2,1,0:T(8,128)(2,1)S(1)}, bf16[2,36,768]{2,1,0:T(8,128)(2,1)S(1)}, u32[]{:S(2)}, u32[]{:S(2)}) collective-permute-start(bf16[2,36,768]{2,1,0:T(8,128)(2,1)S(1)} %get-tuple-element.35), channel_id=1, source_target_pairs={{24,0},{28,4},{16,8},{20,12},{8,16},{12,20},{0,24},{4,28},{25,1},{... | collective-permute-start | bytes 331784 | tf_op jit(solution)/shard_map/ppermute | solution.py:273

commit v3 on v1

v3 whole, which is shorter than its diff:
```python
import functools
import math

import jax
import jax.numpy as jnp
from jax import lax
from jax.experimental import pallas as pl
from jax.experimental.pallas import tpu as pltpu
from jax.sharding import PartitionSpec as P

HEADS = 12
LANES = 128
VMEM = pl.BlockSpec(memory_space=pltpu.VMEM)
FAR = pl.BlockSpec(memory_space=pltpu.HBM)
NT = (((1,), (1,)), ((), ()))


def far(array):
    return pltpu.with_memory_space_constraint(array, pltpu.HBM)


def ceil_to(value, unit):
    return -(-value // unit) * unit


def stack_rows(blocks, stage):
    rows = blocks[0].shape[0]
    pitch = ceil_to(rows, 8)
    for index, block in enumerate(blocks):
        stage[pl.ds(index * pitch, rows), :] = block.astype(jnp.float32)
        if pitch > rows:
            stage[pl.ds(index * pitch + rows, pitch - rows), :] = jnp.zeros(
                (pitch - rows, stage.shape[1]), jnp.float32
            )
    return stage[...].astype(jnp.bfloat16)


def attend(query, key, value, valid, head_width, put):
    per_slab = LANES // head_width
    factor = math.log2(math.e) / math.sqrt(head_width)
    key_total = key.shape[0]
    lane = lax.broadcasted_iota(jnp.int32, (key_total, LANES), 1) // head_width
    bias = jnp.where(valid, 0.0, -1e30)
    for slab in range(query.shape[1] // LANES):
        cut = slice(slab * LANES, (slab + 1) * LANES)
        query_slab, key_slab, value_slab = query[:, cut], key[:, cut], value[:, cut]
        total = None
        for head in range(per_slab):
            own = lane == head
            masked_key = jnp.where(own, key_slab, 0)
            scores = lax.dot_general(query_slab, masked_key, NT, preferred_element_type=jnp.float32)
            scores = scores + bias
            top = jnp.max(scores, axis=1, keepdims=True)
            weights = jnp.exp2((scores - top) * factor)
            weights = weights * (1.0 / jnp.sum(weights, axis=1, keepdims=True))
            part = jnp.dot(
                weights.astype(jnp.bfloat16),
                jnp.where(own, value_slab, 0),
                preferred_element_type=jnp.float32,
            )
            total = part if total is None else total + part
        put(slab, total)


def load_kernel(key, value, query, pair, near_query, sems):
    targets = (pair.at[0], pair.at[1], near_query.at[0])
    copies = [
        pltpu.make_async_copy(source.at[0], target, sems.at[index])
        for index, (source, target) in enumerate(zip((key, value, query), targets))
    ]
    for copy in copies:
        copy.start()
    for copy in copies:
        copy.wait()


def load(key, value, query):
    return pl.pallas_call(
        load_kernel,
        out_shape=[
            pltpu.VMEM((2,) + key.shape[1:], key.dtype),
            pltpu.VMEM(query.shape, query.dtype),
        ],
        in_specs=[FAR] * 3,
        out_specs=[VMEM] * 2,
        scratch_shapes=[pltpu.SemaphoreType.DMA((3,))],
        name="load",
    )(far(key), far(value), far(query))


def fetch_kernel(*refs):
    count = len(refs) // 2
    far_refs, held, sems = refs[:count], refs[count : 2 * count], refs[-1]
    copies = [
        pltpu.make_async_copy(source, target, sems.at[index])
        for index, (source, target) in enumerate(zip(far_refs, held))
    ]
    for copy in copies:
        copy.start()
    for copy in copies:
        copy.wait()


def fetch(weights):
    return pl.pallas_call(
        fetch_kernel,
        out_shape=[pltpu.VMEM(matrix.shape, matrix.dtype) for matrix in weights],
        in_specs=[FAR] * len(weights),
        out_specs=[VMEM] * len(weights),
        scratch_shapes=[pltpu.SemaphoreType.DMA((len(weights),))],
        compiler_params=pltpu.CompilerParams(vmem_limit_bytes=32 << 20),
        cost_estimate=pl.CostEstimate(flops=0, bytes_accessed=len(weights) << 21, transcendentals=0),
        name="fetch",
    )(*map(far, weights))


def attention_kernel(head_width, query_count, forms, *refs):
    first = query_count > 1
    queries, refs = refs[:query_count], refs[query_count:]
    keys, values = [], []
    for form in forms:
        keys.append(refs[0].at[0])
        values.append(refs[form - 1].at[2 - form])
        refs = refs[form:]
    if first:
        *outs, stacked, key_stage, value_stage, query_stage = refs
        query = stack_rows([ref[0] for ref in queries], query_stage)
        stacked[...] = query
        earlier = ()
    else:
        *refs, key_stage, value_stage = refs
        earlier, outs = refs[: len(refs) // 2], refs[len(refs) // 2 :]
        query = queries[0][...]
    rows = keys[0].shape[-2]
    pitch = ceil_to(rows, 8)
    key = stack_rows([ref[...] for ref in keys], key_stage)
    value = stack_rows([ref[...] for ref in values], value_stage)
    place = lax.broadcasted_iota(jnp.int32, (1, key.shape[0]), 1)
    valid = lax.rem(place, pitch) < rows

    def put(slab, pooled):
        for index, out in enumerate(outs):
            out[out.shape[0] - 1, :, pl.ds(slab * LANES, LANES)] = pooled[
                index * pitch : index * pitch + rows
            ].astype(jnp.bfloat16)

    attend(query, key, value, valid, head_width, put)
    for out, ref in zip(outs, earlier):
        out[0] = ref[0]


def attention(queries, blocks, earlier=()):
    _, rows, width = blocks[0][0].shape
    pitch = ceil_to(rows, 8)
    count = len(earlier) or len(queries)
    total = count * pitch
    flops = 4 * count * rows * len(blocks) * rows * width
    shape = jax.ShapeDtypeStruct((2 if earlier else 1, rows, width), jnp.bfloat16)
    first = not earlier
    out = pl.pallas_call(
        functools.partial(attention_kernel, width // HEADS, len(queries), [len(block) for block in blocks]),
        out_shape=[shape] * count + [near((total, width), jnp.bfloat16)] * first,
        in_specs=[VMEM] * (len(queries) + sum(map(len, blocks)) + len(earlier)),
        out_specs=[VMEM] * (count + first),
        scratch_shapes=[near((len(blocks) * pitch, width))] * 2 + [near((total, width))] * first,
        compiler_params=pltpu.CompilerParams(vmem_limit_bytes=32 << 20),
        cost_estimate=pl.CostEstimate(flops=flops, bytes_accessed=1 << 20, transcendentals=0),
        name="attention",
    )(*queries, *(array for block in blocks for array in block), *earlier)
    return out


def head_members(width, head_width):
    channel = lax.broadcasted_iota(jnp.int32, (width, LANES), 0) // head_width
    return (channel == lax.broadcasted_iota(jnp.int32, (width, LANES), 1)).astype(jnp.bfloat16)


def head_spread(width, head_width):
    channel = lax.broadcasted_iota(jnp.int32, (LANES, width), 1) // head_width
    return (channel == lax.broadcasted_iota(jnp.int32, (LANES, width), 0)).astype(jnp.bfloat16)


def project(rows, matrix):
    wide = jnp.dot(rows, matrix[...], preferred_element_type=jnp.float32)
    return wide.astype(jnp.bfloat16).astype(jnp.float32)


def score(query, pooled, w_key, head_width):
    path_key = project(pooled, w_key)
    pitch, width = query.shape
    product = jnp.concatenate(
        [path_key[at : at + pitch] * query for at in range(0, path_key.shape[0], pitch)], axis=0
    )
    member = head_members(width, head_width)
    high = product.astype(jnp.bfloat16)
    low = (product - high.astype(jnp.float32)).astype(jnp.bfloat16)
    scores = jnp.dot(high, member, preferred_element_type=jnp.float32) + jnp.dot(
        low, member, preferred_element_type=jnp.float32
    )
    return scores * (1.0 / math.sqrt(head_width))


def stack_pooled(ref, stage):
    return stack_rows([ref[index] for index in range(ref.shape[0])], stage)


def own_kernel(head_width, block, w_query, w_key, w_value, query, scores, values, stage):
    pooled = stack_pooled(block, stage)
    rows, pitch = block.shape[1], query.shape[0]
    query[...] = project(pooled[: ceil_to(rows, 16)], w_query)[:pitch]
    scores[...] = score(query[...], pooled, w_key, head_width)
    values[...] = project(pooled, w_value)


def part_kernel(head_width, block, query, w_key, w_value, scores, values, stage):
    pooled = stack_pooled(block, stage)
    scores[...] = score(query[...], pooled, w_key, head_width)
    values[...] = project(pooled, w_value)


def last_kernel(head_width, earlier, count, *refs):
    blocks, (query, w_key, w_value), refs = refs[:count], refs[count : count + 3], refs[count + 3 :]
    score_refs, value_refs, (out, stage) = refs[:earlier], refs[earlier : 2 * earlier], refs[-2:]
    pooled = stack_rows([ref[index] for ref in blocks for index in range(ref.shape[0])], stage)
    pitch, width = query.shape
    score_parts = [ref[...] for ref in score_refs] + [score(query[...], pooled, w_key, head_width)]
    value_parts = [ref[...] for ref in value_refs] + [project(pooled, w_value)]
    places = [
        (part, at) for part in range(earlier + 1) for at in range(0, score_parts[part].shape[0], pitch)
    ]
    scores = [score_parts[part][at : at + pitch] for part, at in places]
    top = functools.reduce(jnp.maximum, scores)
    scores = [jnp.exp(part - top) for part in scores]
    share = 1.0 / functools.reduce(jnp.add, scores)
    weights = jnp.concatenate([part * share for part in scores], axis=0).astype(jnp.bfloat16)
    weights = jnp.dot(weights, head_spread(width, head_width), preferred_element_type=jnp.float32)
    mixed = functools.reduce(
        jnp.add,
        [
            weights[index * pitch : (index + 1) * pitch] * value_parts[part][at : at + pitch]
            for index, (part, at) in enumerate(places)
        ],
    )
    out[0] = mixed[: blocks[0].shape[1]].astype(jnp.bfloat16)


def near(shape, dtype=jnp.float32):
    return pltpu.VMEM(shape, dtype)


def mix_call(kernel, blocks, out_shape, operands, name):
    _, rows, width = blocks[0].shape
    count = sum(block.shape[0] for block in blocks)
    return pl.pallas_call(
        functools.partial(kernel, width // HEADS),
        out_shape=out_shape,
        in_specs=[VMEM] * (len(blocks) + len(operands)),
        out_specs=jax.tree.map(lambda _: VMEM, out_shape),
        scratch_shapes=[near((count * ceil_to(rows, 8), width))],
        compiler_params=pltpu.CompilerParams(vmem_limit_bytes=32 << 20),
        cost_estimate=pl.CostEstimate(
            flops=4 * count * rows * width * width, bytes_accessed=4 << 20, transcendentals=0
        ),
        name=name,
    )(*blocks, *operands)


def part_shapes(block):
    count, rows, width = block.shape
    total = count * ceil_to(rows, 8)
    return [near((total, LANES)), near((total, width))]


def mix_own(block, weights):
    _, rows, width = block.shape
    shapes = [near((ceil_to(rows, 8), width)), *part_shapes(block)]
    query, *part = mix_call(own_kernel, [block], shapes, weights, "mix_own")
    return query, tuple(part)


def mix_part(block, query, w_key, w_value):
    return mix_call(part_kernel, [block], part_shapes(block), (query, w_key, w_value), "mix_part")


def mix_last(blocks, query, w_key, w_value, parts):
    scores, values = zip(*parts)
    return mix_call(
        lambda head_width, *refs: last_kernel(head_width, len(parts), len(blocks), *refs),
        blocks,
        jax.ShapeDtypeStruct((1,) + blocks[0].shape[1:], blocks[0].dtype),
        (query, w_key, w_value, *scores, *values),
        "mix_last",
    )


def rounds(total):
    for step in range(1, total):
        if total & (total - 1) == 0:
            there = [(index, index ^ step) for index in range(total)]
        else:
            there = [(index, (index + step) % total) for index in range(total)]
        yield there, [(target, source) for source, target in there]


def chip_rounds(total):
    for there, back in rounds(total // 2):
        yield tuple(
            [(2 * source + core, 2 * target + core) for source, target in pairs for core in range(2)]
            for pairs in (there, back)
        )


def per_device(query_tokens, key_tokens, value_tokens, w_query, w_key, w_value):
    frame_total = lax.axis_size("frame")
    block_total = lax.axis_size("qblk")
    swap = [(index, index ^ 1) for index in range(frame_total)]
    own_block, near_query = load(key_tokens, value_tokens, query_tokens)
    blocks = [(own_block,)] + [(lax.ppermute(own_block, "qblk", there),) for there, _ in rounds(block_total)]
    paths = list(chip_rounds(frame_total))
    ready_query = lax.optimization_barrier((near_query, blocks[1 % len(blocks)][0]))[0]
    queries = [near_query] + [lax.ppermute(ready_query, "frame", there) for there, _ in paths]
    w_query, w_key, w_value = fetch((w_query, w_key, w_value))
    *queries, w_query, w_key, w_value = lax.optimization_barrier((*queries, w_query, w_key, w_value))
    turned = [lax.optimization_barrier((blocks[0], blocks[1 % len(blocks)]))[0], *blocks[1:2]]
    turned += [lax.optimization_barrier((block, *queries))[0] for block in blocks[2:]]
    other_blocks = [
        tuple(lax.ppermute(array, "frame", swap) for array in block) for block in turned
    ]
    *own, query = attention(queries, blocks)
    pooled = attention([query], other_blocks, own)
    own_query, part = mix_own(pooled[0], (w_query, w_key, w_value))
    if not paths:
        return mix_last([pooled[0]], own_query, w_key, w_value, [])
    *nearer, own_query = lax.optimization_barrier((*pooled[1:-1], own_query))
    arrived = [
        lax.ppermute(block, "frame", back)
        for block, (_, back) in zip([*nearer, pooled[-1]], paths)
    ]
    parts = [part]
    for block in arrived[:1:-1]:
        parts.append(mix_part(block, own_query, w_key, w_value))
    return mix_last(arrived[:2], own_query, w_key, w_value, parts)


def solution(mesh):
    in_specs = (
        P("frame", "qblk", None),
        P("frame", "qblk", None),
        P("frame", "qblk", None),
        P(),
        P(),
        P(),
    )
    out_specs = P("frame", "qblk", None)
    return jax.shard_map(
        per_device, mesh=mesh, in_specs=in_specs, out_specs=out_specs, check_vma=False
    )
```

time: 40.6 us -> 31.7 us (0.78)
  starting transfers between devices: 21.2 us -> 12.9 us
  local copies, waits for them, and re-layouts: 5.03 us -> 0 us
  Pallas kernels: 5.4 us -> 9.13 us
  waiting for transfers between devices: 8.59 us -> 9.43 us
    ppermute x17 -> x10, starting transfers between devices: 17.6 us -> 9.25 us  [the longest x3 5.68 us: per_device(): lax.ppermute(own_block, 'qblk', there)]
    unnamed x12 -> x0, local copies, waits for them, and re-layouts: 5.03 us -> none
    pallas_call x3 -> x7, Pallas kernels: 5.4 us -> 9.13 us  [the longest x3 3.36 us: mix_call(): pl.pallas_call(functools.partial(kernel, width // HEADS), out_shape=out_s...]
    ppermute x17 -> x10, waiting for transfers between devices: 3 us -> 5.35 us  [the longest x3 2.7 us: per_device(): lax.ppermute(ready_query, 'frame', there)]
    ppermute x3, waiting for transfers between devices: 5.59 us -> 4.09 us  [per_device(): lax.ppermute(block, 'frame', back)]
  transfers between devices with their start and end apart: 20 -> 13, of which waited for: 4 -> 7; matrix products, arithmetic and copies ran while one was open for 0% -> 0% of each run, Pallas kernels for 4% -> 16%
where the time goes in v3:
time: 31.7 us; the launch traced here: 31.5 us
  starting transfers between devices  12.9 us (41%)
  waiting for transfers between devices  9.43 us (30%)
  Pallas kernels  9.13 us (29%)
    ppermute x3, starting transfers between devices, per_device(): lax.ppermute(own_block, 'qblk', there)  5.68 us
    ppermute x3, waiting for transfers between devices, per_device(): lax.ppermute(block, 'frame', back)  4.09 us
    ppermute x3, starting transfers between devices, per_device(): lax.ppermute(block, 'frame', back)  3.62 us
    ppermute x3, starting transfers between devices, per_device(): lax.ppermute(ready_query, 'frame', there)  3.49 us
    pallas_call x3, Pallas kernels, mix_call(): pl.pallas_call(functools.partial(kernel, width // HEADS), out_shape=out_s...  3.36 us
    pallas_call x2, Pallas kernels, attention(): pl.pallas_call(functools.partial(attention_kernel, width // HEADS, len(qu...  2.85 us
    ppermute x3, waiting for transfers between devices, per_device(): lax.ppermute(ready_query, 'frame', there)  2.7 us
    ppermute x3, waiting for transfers between devices, per_device(): lax.ppermute(own_block, 'qblk', there)  2.63 us
  transfers between devices with their start and end apart: 13, of which 7 were waited for; matrix products, arithmetic and copies ran while one was open for 0% of the time, Pallas kernels for 16%

profile of v3, /device:TPU:0, one launch (start us, length us, event | category | flops | bytes accessed | tf_op | source)
XLA Modules:
  0.0 31.5 jit_solution(13561397289358757367)
XLA Ops:
  0.0 0.9 %load.1 = (bf16[2,36,768]{2,1,0:T(8,128)(2,1)S(1)}, bf16[1,36,768]{2,1,0:T(8,128)(2,1)S(1)}) custom-call(bf16[1,36,768]{2,1,0:T(8,128)(2,1)} %key.1, bf16[1,36,768]{2,1,0:T(8,128)(2,1)} %value.1, bf16[1,36,768]{2,1,0:T(8,128)(2,1)} %query.1), custom_call_target="tpu_custom_call" | custom-call | tf_op jit(solution)/shard_map/load/pallas_call | solution.py:78
  0.9 3.1 %collective-permute-start = (bf16[2,36,768]{2,1,0:T(8,128)(2,1)S(1)}, bf16[2,36,768]{2,1,0:T(8,128)(2,1)S(1)}, u32[]{:S(2)}, u32[]{:S(2)}) collective-permute-start(bf16[2,36,768]{2,1,0:T(8,128)(2,1)S(1)} %get-tuple-element.49.refs_4_), channel_id=1, source_target_pairs={{0,1},{1,0},{2,3},{3,2},{4,5},{5,4},{6,7},{7,6},{8,9},{9,8},{10,11... | collective-permute-start | bytes 331784 | tf_op jit(solution)/shard_map/ppermute | solution.py:318
  4.0 2.5 %collective-permute-start.5 = (bf16[2,36,768]{2,1,0:T(8,128)(2,1)S(1)}, bf16[2,36,768]{2,1,0:T(8,128)(2,1)S(1)}, u32[]{:S(2)}, u32[]{:S(2)}) collective-permute-start(bf16[2,36,768]{2,1,0:T(8,128)(2,1)S(1)} %get-tuple-element.49.refs_4_), channel_id=1, source_target_pairs={{0,3},{1,2},{2,1},{3,0},{4,7},{5,6},{6,5},{7,4},{8,11},{9,10},{10,... | collective-permute-start | bytes 331784 | tf_op jit(solution)/shard_map/ppermute | solution.py:318
  6.5 0.1 collective-permute-start.4
  6.6 0.7 %collective-permute-done.refs_5_ = bf16[2,36,768]{2,1,0:T(8,128)(2,1)S(1)} collective-permute-done((bf16[2,36,768]{2,1,0:T(8,128)(2,1)S(1)}, bf16[2,36,768]{2,1,0:T(8,128)(2,1)S(1)}, u32[]{:S(2)}, u32[]{:S(2)}) %collective-permute-start) | collective-permute-done | bytes 110624 | tf_op jit(solution)/shard_map/ppermute | solution.py:318
  7.3 1.7 %collective-permute-start.1 = (bf16[1,36,768]{2,1,0:T(8,128)(2,1)S(1)}, bf16[1,36,768]{2,1,0:T(8,128)(2,1)S(1)}, u32[]{:S(2)}, u32[]{:S(2)}) collective-permute-start(bf16[1,36,768]{2,1,0:T(8,128)(2,1)S(1)} %get-tuple-element.44.refs_0_), channel_id=1, source_target_pairs={{0,8},{4,12},{8,0},{12,4},{16,24},{20,28},{24,16},{28,20},{1,9},{5... | collective-permute-start | bytes 165896 | tf_op jit(solution)/shard_map/ppermute | solution.py:321
  9.0 1.5 %collective-permute-start.2 = (bf16[1,36,768]{2,1,0:T(8,128)(2,1)S(1)}, bf16[1,36,768]{2,1,0:T(8,128)(2,1)S(1)}, u32[]{:S(2)}, u32[]{:S(2)}) collective-permute-start(bf16[1,36,768]{2,1,0:T(8,128)(2,1)S(1)} %get-tuple-element.44.refs_0_), channel_id=1, source_target_pairs={{0,16},{4,20},{8,24},{12,28},{16,0},{20,4},{24,8},{28,12},{1,17},{... | collective-permute-start | bytes 165896 | tf_op jit(solution)/shard_map/ppermute | solution.py:321
  10.5 0.3 collective-permute-start.3
  10.8 2.0 %fetch.1 = (bf16[768,768]{1,0:T(8,128)(2,1)S(1)}, bf16[768,768]{1,0:T(8,128)(2,1)S(1)}, bf16[768,768]{1,0:T(8,128)(2,1)S(1)}) custom-call(bf16[768,768]{1,0:T(8,128)(2,1)} %refs_0_.1, bf16[768,768]{1,0:T(8,128)(2,1)} %refs_1_.1, bf16[768,768]{1,0:T(8,128)(2,1)} %refs_2_.1), custom_call_target="tpu_custom_call" | custom-call | bytes 6291456 | tf_op jit(solution)/shard_map/fetch/pallas_call | solution.py:105
  12.8 0.1 collective-permute-start.6
  12.9 0.8 %collective-permute-done.2.refs_2_ = bf16[1,36,768]{2,1,0:T(8,128)(2,1)S(1)} collective-permute-done((bf16[1,36,768]{2,1,0:T(8,128)(2,1)S(1)}, bf16[1,36,768]{2,1,0:T(8,128)(2,1)S(1)}, u32[]{:S(2)}, u32[]{:S(2)}) %collective-permute-start.2) | collective-permute-done | bytes 55328 | tf_op jit(solution)/shard_map/ppermute | solution.py:321
  13.8 1.9 %collective-permute-done.3.refs_3_ = bf16[1,36,768]{2,1,0:T(8,128)(2,1)S(1)} collective-permute-done((bf16[1,36,768]{2,1,0:T(8,128)(2,1)S(1)}, bf16[1,36,768]{2,1,0:T(8,128)(2,1)S(1)}, u32[]{:S(2)}, u32[]{:S(2)}) %collective-permute-start.3) | collective-permute-done | bytes 55328 | tf_op jit(solution)/shard_map/ppermute | solution.py:321
  15.6 1.9 %collective-permute-done.4.refs_6_ = bf16[2,36,768]{2,1,0:T(8,128)(2,1)S(1)} collective-permute-done((bf16[2,36,768]{2,1,0:T(8,128)(2,1)S(1)}, bf16[2,36,768]{2,1,0:T(8,128)(2,1)S(1)}, u32[]{:S(2)}, u32[]{:S(2)}) %collective-permute-start.4) | collective-permute-done | bytes 110624 | tf_op jit(solution)/shard_map/ppermute | solution.py:318
  17.5 1.4 %attention.2 = (bf16[1,36,768]{2,1,0:T(8,128)(2,1)S(1)}, bf16[1,36,768]{2,1,0:T(8,128)(2,1)S(1)}, bf16[1,36,768]{2,1,0:T(8,128)(2,1)S(1)}, bf16[1,36,768]{2,1,0:T(8,128)(2,1)S(1)}, bf16[160,768]{1,0:T(8,128)(2,1)S(1)}) custom-call(bf16[1,36,768]{2,1,0:T(8,128)(2,1)S(1)} %get-tuple-element.44.refs_0_, bf16[1,36,768]{2,1,0:T(8,128)(2,1)S(1)} %collective-permute-done.1.refs_1_, ...), custom_call_target="tpu_custom_call" | custom-call | flops 63700992 | bytes 1048576 | tf_op jit(solution)/shard_map/attention/pallas_call | solution.py:160
  19.0 1.4 %attention.3 = (bf16[2,36,768]{2,1,0:T(8,128)(2,1)S(1)}, bf16[2,36,768]{2,1,0:T(8,128)(2,1)S(1)}, bf16[2,36,768]{2,1,0:T(8,128)(2,1)S(1)}, bf16[2,36,768]{2,1,0:T(8,128)(2,1)S(1)}) custom-call(bf16[160,768]{1,0:T(8,128)(2,1)S(1)} %get-tuple-element.48.refs_0_, bf16[2,36,768]{2,1,0:T(8,128)(2,1)S(1)} %collective-permute-done.6.refs_1_, ...), custom_call_target="tpu_custom_call" | custom-call | flops 63700992 | bytes 1048576 | tf_op jit(solution)/shard_map/attention/pallas_call | solution.py:160
  20.4 2.5 %collective-permute-start.12 = (bf16[2,36,768]{2,1,0:T(8,128)(2,1)S(1)}, bf16[2,36,768]{2,1,0:T(8,128)(2,1)S(1)}, u32[]{:S(2)}, u32[]{:S(2)}) collective-permute-start(bf16[2,36,768]{2,1,0:T(8,128)(2,1)S(1)} %get-tuple-element.67), channel_id=1, source_target_pairs={{24,0},{28,4},{16,8},{20,12},{8,16},{12,20},{0,24},{4,28},{25,1},{... | collective-permute-start | bytes 331784 | tf_op jit(solution)/shard_map/ppermute | solution.py:336
  23.0 0.9 %mix_own.1 = (f32[40,768]{1,0:T(8,128)S(1)}, f32[80,128]{1,0:T(8,128)S(1)}, f32[80,768]{1,0:T(8,128)S(1)}) custom-call(bf16[2,36,768]{2,1,0:T(8,128)(2,1)S(1)} %get-tuple-element.58.block, bf16[768,768]{1,0:T(8,128)(2,1)S(1)} %get-tuple-element.59.w_query, bf16[768,768]{1,0:T(8,128)(2,1)S(1)} %get-tuple-element.60.w_key.refs_3_, ...), custom_call_target="tpu_custom_call" | custom-call | flops 169869312 | bytes 4194304 | tf_op jit(solution)/shard_map/mix_own/pallas_call | solution.py:254
  23.9 0.6 %collective-permute-start.10 = (bf16[2,36,768]{2,1,0:T(8,128)(2,1)S(1)}, bf16[2,36,768]{2,1,0:T(8,128)(2,1)S(1)}, u32[]{:S(2)}, u32[]{:S(2)}) collective-permute-start(bf16[2,36,768]{2,1,0:T(8,128)(2,1)S(1)} %get-tuple-element.63), channel_id=1, source_target_pairs={{8,0},{12,4},{0,8},{4,12},{24,16},{28,20},{16,24},{20,28},{9,1},{1... | collective-permute-start | bytes 331784 | tf_op jit(solution)/shard_map/ppermute | solution.py:336
  24.5 0.5 %collective-permute-start.11 = (bf16[2,36,768]{2,1,0:T(8,128)(2,1)S(1)}, bf16[2,36,768]{2,1,0:T(8,128)(2,1)S(1)}, u32[]{:S(2)}, u32[]{:S(2)}) collective-permute-start(bf16[2,36,768]{2,1,0:T(8,128)(2,1)S(1)} %get-tuple-element.64), channel_id=1, source_target_pairs={{16,0},{20,4},{24,8},{28,12},{0,16},{4,20},{8,24},{12,28},{17,1},{... | collective-permute-start | bytes 331784 | tf_op jit(solution)/shard_map/ppermute | solution.py:336
  25.0 2.5 %collective-permute-done.12.block = bf16[2,36,768]{2,1,0:T(8,128)(2,1)S(1)} collective-permute-done((bf16[2,36,768]{2,1,0:T(8,128)(2,1)S(1)}, bf16[2,36,768]{2,1,0:T(8,128)(2,1)S(1)}, u32[]{:S(2)}, u32[]{:S(2)}) %collective-permute-start.12) | collective-permute-done | bytes 110624 | tf_op jit(solution)/shard_map/ppermute | solution.py:336
  27.5 0.8 %mix_part.1 = (f32[80,128]{1,0:T(8,128)S(1)}, f32[80,768]{1,0:T(8,128)S(1)}) custom-call(bf16[2,36,768]{2,1,0:T(8,128)(2,1)S(1)} %collective-permute-done.12.block, f32[40,768]{1,0:T(8,128)S(1)} %get-tuple-element.65.query.refs_2_, bf16[768,768]{1,0:T(8,128)(2,1)S(1)} %get-tuple-element.60.w_key.refs_3_, bf16[768,768]{1,0:T(8,128)(2,1)S(1)} %get-tuple-element.61.w_value.refs_4_), custom_call_target="tpu_custom_call" | custom-call | flops 169869312 | bytes 4194304 | tf_op jit(solution)/shard_map/mix_part/pallas_call | solution.py:254
  28.3 1.5 %collective-permute-done.10.refs_0_ = bf16[2,36,768]{2,1,0:T(8,128)(2,1)S(1)} collective-permute-done((bf16[2,36,768]{2,1,0:T(8,128)(2,1)S(1)}, bf16[2,36,768]{2,1,0:T(8,128)(2,1)S(1)}, u32[]{:S(2)}, u32[]{:S(2)}) %collective-permute-start.10) | collective-permute-done | bytes 110624 | tf_op jit(solution)/shard_map/ppermute | solution.py:336
  29.8 0.1 collective-permute-done.11.refs_1_
  29.9 1.6 %mix_last.1 = bf16[1,36,768]{2,1,0:T(8,128)(2,1)} custom-call(bf16[2,36,768]{2,1,0:T(8,128)(2,1)S(1)} %collective-permute-done.10.refs_0_, bf16[2,36,768]{2,1,0:T(8,128)(2,1)S(1)} %collective-permute-done.11.refs_1_, f32[40,768]{1,0:T(8,128)S(1)} %get-tuple-element.65.query.refs_2_, bf16[768,768]{1,0:T(8,128)(2,1)S(1)} %get-tuple-element.60.w_key.refs_3_, ...), custom_call_target="tpu_custom_call" | custom-call | flops 339738624 | bytes 4194304 | tf_op jit(solution)/shard_map/mix_last/pallas_call | solution.py:254
  (9 shorter events, 0.0 us)
Async XLA Ops:
  0.9 6.4 %collective-permute-start = (bf16[2,36,768]{2,1,0:T(8,128)(2,1)S(1)}, bf16[2,36,768]{2,1,0:T(8,128)(2,1)S(1)}, u32[]{:S(2)}, u32[]{:S(2)}) collective-permute-start(bf16[2,36,768]{2,1,0:T(8,128)(2,1)S(1)} %get-tuple-element.49.refs_4_), channel_id=1, source_target_pairs={{0,1},{1,0},{2,3},{3,2},{4,5},{5,4},{6,7},{7,6},{8,9},{9,8},{10,11... | collective-permute-start | bytes 331784 | tf_op jit(solution)/shard_map/ppermute | solution.py:318
  4.0 11.6 %collective-permute-start.5 = (bf16[2,36,768]{2,1,0:T(8,128)(2,1)S(1)}, bf16[2,36,768]{2,1,0:T(8,128)(2,1)S(1)}, u32[]{:S(2)}, u32[]{:S(2)}) collective-permute-start(bf16[2,36,768]{2,1,0:T(8,128)(2,1)S(1)} %get-tuple-element.49.refs_4_), channel_id=1, source_target_pairs={{0,3},{1,2},{2,1},{3,0},{4,7},{5,6},{6,5},{7,4},{8,11},{9,10},{10,... | collective-permute-start | bytes 331784 | tf_op jit(solution)/shard_map/ppermute | solution.py:318
  6.5 11.1 %collective-permute-start.4 = (bf16[2,36,768]{2,1,0:T(8,128)(2,1)S(1)}, bf16[2,36,768]{2,1,0:T(8,128)(2,1)S(1)}, u32[]{:S(2)}, u32[]{:S(2)}) collective-permute-start(bf16[2,36,768]{2,1,0:T(8,128)(2,1)S(1)} %get-tuple-element.49.refs_4_), channel_id=1, source_target_pairs={{0,2},{1,3},{2,0},{3,1},{4,6},{5,7},{6,4},{7,5},{8,10},{9,11},{10,... | collective-permute-start | bytes 331784 | tf_op jit(solution)/shard_map/ppermute | solution.py:318
  7.3 5.5 %collective-permute-start.1 = (bf16[1,36,768]{2,1,0:T(8,128)(2,1)S(1)}, bf16[1,36,768]{2,1,0:T(8,128)(2,1)S(1)}, u32[]{:S(2)}, u32[]{:S(2)}) collective-permute-start(bf16[1,36,768]{2,1,0:T(8,128)(2,1)S(1)} %get-tuple-element.44.refs_0_), channel_id=1, source_target_pairs={{0,8},{4,12},{8,0},{12,4},{16,24},{20,28},{24,16},{28,20},{1,9},{5... | collective-permute-start | bytes 165896 | tf_op jit(solution)/shard_map/ppermute | solution.py:321
  9.0 4.8 %collective-permute-start.2 = (bf16[1,36,768]{2,1,0:T(8,128)(2,1)S(1)}, bf16[1,36,768]{2,1,0:T(8,128)(2,1)S(1)}, u32[]{:S(2)}, u32[]{:S(2)}) collective-permute-start(bf16[1,36,768]{2,1,0:T(8,128)(2,1)S(1)} %get-tuple-element.44.refs_0_), channel_id=1, source_target_pairs={{0,16},{4,20},{8,24},{12,28},{16,0},{20,4},{24,8},{28,12},{1,17},{... | collective-permute-start | bytes 165896 | tf_op jit(solution)/shard_map/ppermute | solution.py:321
  10.5 5.1 %collective-permute-start.3 = (bf16[1,36,768]{2,1,0:T(8,128)(2,1)S(1)}, bf16[1,36,768]{2,1,0:T(8,128)(2,1)S(1)}, u32[]{:S(2)}, u32[]{:S(2)}) collective-permute-start(bf16[1,36,768]{2,1,0:T(8,128)(2,1)S(1)} %get-tuple-element.44.refs_0_), channel_id=1, source_target_pairs={{0,24},{4,28},{8,16},{12,20},{16,8},{20,12},{24,0},{28,4},{1,25},{... | collective-permute-start | bytes 165896 | tf_op jit(solution)/shard_map/ppermute | solution.py:321
  12.8 6.1 %collective-permute-start.6 = (bf16[2,36,768]{2,1,0:T(8,128)(2,1)S(1)}, bf16[2,36,768]{2,1,0:T(8,128)(2,1)S(1)}, u32[]{:S(2)}, u32[]{:S(2)}) collective-permute-start(bf16[2,36,768]{2,1,0:T(8,128)(2,1)S(1)} %get-tuple-element.49.refs_4_), channel_id=1, source_target_pairs={{0,4},{4,0},{8,12},{12,8},{16,20},{20,16},{24,28},{28,24},{1,5},{5... | collective-permute-start | bytes 331784 | tf_op jit(solution)/shard_map/ppermute | solution.py:327
  13.7 5.2 %collective-permute-start.7 = (bf16[2,36,768]{2,1,0:T(8,128)(2,1)S(1)}, bf16[2,36,768]{2,1,0:T(8,128)(2,1)S(1)}, u32[]{:S(2)}, u32[]{:S(2)}) collective-permute-start(bf16[2,36,768]{2,1,0:T(8,128)(2,1)S(1)} %collective-permute-done.refs_5_), channel_id=1, source_target_pairs={{0,4},{4,0},{8,12},{12,8},{16,20},{20,16},{24,28},{28,24},{1,5},{5... | collective-permute-start | bytes 331784 | tf_op jit(solution)/shard_map/ppermute | solution.py:327
  15.6 3.4 %collective-permute-start.9 = (bf16[2,36,768]{2,1,0:T(8,128)(2,1)S(1)}, bf16[2,36,768]{2,1,0:T(8,128)(2,1)S(1)}, u32[]{:S(2)}, u32[]{:S(2)}) collective-permute-start(bf16[2,36,768]{2,1,0:T(8,128)(2,1)S(1)} %collective-permute-done.5.refs_7_), channel_id=1, source_target_pairs={{0,4},{4,0},{8,12},{12,8},{16,20},{20,16},{24,28},{28,24},{1,5},{5... | collective-permute-start | bytes 331784 | tf_op jit(solution)/shard_map/ppermute | solution.py:327
  17.5 1.5 %collective-permute-start.8 = (bf16[2,36,768]{2,1,0:T(8,128)(2,1)S(1)}, bf16[2,36,768]{2,1,0:T(8,128)(2,1)S(1)}, u32[]{:S(2)}, u32[]{:S(2)}) collective-permute-start(bf16[2,36,768]{2,1,0:T(8,128)(2,1)S(1)} %collective-permute-done.4.refs_6_), channel_id=1, source_target_pairs={{0,4},{4,0},{8,12},{12,8},{16,20},{20,16},{24,28},{28,24},{1,5},{5... | collective-permute-start | bytes 331784 | tf_op jit(solution)/shard_map/ppermute | solution.py:327
  20.4 7.1 %collective-permute-start.12 = (bf16[2,36,768]{2,1,0:T(8,128)(2,1)S(1)}, bf16[2,36,768]{2,1,0:T(8,128)(2,1)S(1)}, u32[]{:S(2)}, u32[]{:S(2)}) collective-permute-start(bf16[2,36,768]{2,1,0:T(8,128)(2,1)S(1)} %get-tuple-element.67), channel_id=1, source_target_pairs={{24,0},{28,4},{16,8},{20,12},{8,16},{12,20},{0,24},{4,28},{25,1},{... | collective-permute-start | bytes 331784 | tf_op jit(solution)/shard_map/ppermute | solution.py:336
  23.9 5.9 %collective-permute-start.10 = (bf16[2,36,768]{2,1,0:T(8,128)(2,1)S(1)}, bf16[2,36,768]{2,1,0:T(8,128)(2,1)S(1)}, u32[]{:S(2)}, u32[]{:S(2)}) collective-permute-start(bf16[2,36,768]{2,1,0:T(8,128)(2,1)S(1)} %get-tuple-element.63), channel_id=1, source_target_pairs={{8,0},{12,4},{0,8},{4,12},{24,16},{28,20},{16,24},{20,28},{9,1},{1... | collective-permute-start | bytes 331784 | tf_op jit(solution)/shard_map/ppermute | solution.py:336
  24.5 5.4 %collective-permute-start.11 = (bf16[2,36,768]{2,1,0:T(8,128)(2,1)S(1)}, bf16[2,36,768]{2,1,0:T(8,128)(2,1)S(1)}, u32[]{:S(2)}, u32[]{:S(2)}) collective-permute-start(bf16[2,36,768]{2,1,0:T(8,128)(2,1)S(1)} %get-tuple-element.64), channel_id=1, source_target_pairs={{16,0},{20,4},{24,8},{28,12},{0,16},{4,20},{8,24},{12,28},{17,1},{... | collective-permute-start | bytes 331784 | tf_op jit(solution)/shard_map/ppermute | solution.py:336

commit v4 on v3

--- a/solution.py
+++ b/solution.py
@@ -318,11 +318,13 @@
     blocks = [(own_block,)] + [(lax.ppermute(own_block, "qblk", there),) for there, _ in rounds(block_total)]
     paths = list(chip_rounds(frame_total))
     ready_query = lax.optimization_barrier((near_query, blocks[1 % len(blocks)][0]))[0]
-    queries = [near_query] + [lax.ppermute(ready_query, "frame", there) for there, _ in paths]
+    queries = [near_query] + [
+        lax.ppermute(ready_query if step == 0 else near_query, "frame", there)
+        for step, (there, _) in enumerate(paths)
+    ]
     w_query, w_key, w_value = fetch((w_query, w_key, w_value))
     *queries, w_query, w_key, w_value = lax.optimization_barrier((*queries, w_query, w_key, w_value))
-    turned = [lax.optimization_barrier((blocks[0], blocks[1 % len(blocks)]))[0], *blocks[1:2]]
-    turned += [lax.optimization_barrier((block, *queries))[0] for block in blocks[2:]]
+    turned = [lax.optimization_barrier((block, *queries))[0] for block in blocks]
     other_blocks = [
         tuple(lax.ppermute(array, "frame", swap) for array in block) for block in turned
     ]
@@ -331,10 +333,9 @@
     own_query, part = mix_own(pooled[0], (w_query, w_key, w_value))
     if not paths:
         return mix_last([pooled[0]], own_query, w_key, w_value, [])
-    *nearer, own_query = lax.optimization_barrier((*pooled[1:-1], own_query))
     arrived = [
         lax.ppermute(block, "frame", back)
-        for block, (_, back) in zip([*nearer, pooled[-1]], paths)
+        for block, (_, back) in zip(pooled[1:], paths)
     ]
     parts = [part]
     for block in arrived[:1:-1]:

time: 31.7 us -> 30.4 us (0.959)
  waiting for transfers between devices: 9.43 us -> 6.99 us
  starting transfers between devices: 12.9 us -> 14 us
    ppermute x3, waiting for transfers between devices: 2.7 us -> 1.6 us  [per_device(): lax.ppermute(ready_query if step == 0 else near_query, 'frame', there)]
    ppermute x4, starting transfers between devices: 0.08 us -> 1.02 us  [per_device(): lax.ppermute(array, 'frame', swap)]
    ppermute x3, waiting for transfers between devices: 2.63 us -> 1.81 us  [per_device(): lax.ppermute(own_block, 'qblk', there)]
    ppermute x3, waiting for transfers between devices: 4.09 us -> 3.57 us  [per_device(): lax.ppermute(block, 'frame', back)]
  transfers between devices with their start and end apart: 13 -> 13, of which waited for: 7 -> 5; matrix products, arithmetic and copies ran while one was open for 0% -> 0% of each run, Pallas kernels for 16% -> 17%
where the time goes in v4:
time: 30.4 us; the launch traced here: 30.2 us
  starting transfers between devices  14 us (46%)
  Pallas kernels  9.13 us (30%)
  waiting for transfers between devices  6.99 us (23%)
    ppermute x3, starting transfers between devices, per_device(): lax.ppermute(own_block, 'qblk', there)  5.68 us
    ppermute x3, starting transfers between devices, per_device(): lax.ppermute(ready_query if step == 0 else near_query, 'frame', there)  3.77 us
    ppermute x3, waiting for transfers between devices, per_device(): lax.ppermute(block, 'frame', back)  3.57 us
    ppermute x3, starting transfers between devices, per_device(): lax.ppermute(block, 'frame', back)  3.55 us
    pallas_call x3, Pallas kernels, mix_call(): pl.pallas_call(functools.partial(kernel, width // HEADS), out_shape=out_s...  3.36 us
    pallas_call x2, Pallas kernels, attention(): pl.pallas_call(functools.partial(attention_kernel, width // HEADS, len(qu...  2.85 us
    pallas_call x1, Pallas kernels, fetch(): pl.pallas_call(fetch_kernel, out_shape=[pltpu.VMEM(matrix.shape, matrix.d...  2.01 us
    ppermute x3, waiting for transfers between devices, per_device(): lax.ppermute(own_block, 'qblk', there)  1.81 us
  transfers between devices with their start and end apart: 13, of which 5 were waited for; matrix products, arithmetic and copies ran while one was open for 0% of the time, Pallas kernels for 17%

profile of v4, /device:TPU:0, one launch (start us, length us, event | category | flops | bytes accessed | tf_op | source)
XLA Modules:
  0.0 30.2 jit_solution(17159683620334428614)
XLA Ops:
  0.0 0.9 %load.1 = (bf16[2,36,768]{2,1,0:T(8,128)(2,1)S(1)}, bf16[1,36,768]{2,1,0:T(8,128)(2,1)S(1)}) custom-call(bf16[1,36,768]{2,1,0:T(8,128)(2,1)} %key.1, bf16[1,36,768]{2,1,0:T(8,128)(2,1)} %value.1, bf16[1,36,768]{2,1,0:T(8,128)(2,1)} %query.1), custom_call_target="tpu_custom_call" | custom-call | tf_op jit(solution)/shard_map/load/pallas_call | solution.py:78
  0.9 3.1 %collective-permute-start = (bf16[2,36,768]{2,1,0:T(8,128)(2,1)S(1)}, bf16[2,36,768]{2,1,0:T(8,128)(2,1)S(1)}, u32[]{:S(2)}, u32[]{:S(2)}) collective-permute-start(bf16[2,36,768]{2,1,0:T(8,128)(2,1)S(1)} %get-tuple-element.47.refs_4_), channel_id=1, source_target_pairs={{0,1},{1,0},{2,3},{3,2},{4,5},{5,4},{6,7},{7,6},{8,9},{9,8},{10,11... | collective-permute-start | bytes 331784 | tf_op jit(solution)/shard_map/ppermute | solution.py:318
  4.0 2.6 %collective-permute-start.4 = (bf16[2,36,768]{2,1,0:T(8,128)(2,1)S(1)}, bf16[2,36,768]{2,1,0:T(8,128)(2,1)S(1)}, u32[]{:S(2)}, u32[]{:S(2)}) collective-permute-start(bf16[2,36,768]{2,1,0:T(8,128)(2,1)S(1)} %get-tuple-element.47.refs_4_), channel_id=1, source_target_pairs={{0,2},{1,3},{2,0},{3,1},{4,6},{5,7},{6,4},{7,5},{8,10},{9,11},{10,... | collective-permute-start | bytes 331784 | tf_op jit(solution)/shard_map/ppermute | solution.py:318
  6.6 0.0 collective-permute-start.5
  6.6 1.7 %collective-permute-start.2 = (bf16[1,36,768]{2,1,0:T(8,128)(2,1)S(1)}, bf16[1,36,768]{2,1,0:T(8,128)(2,1)S(1)}, u32[]{:S(2)}, u32[]{:S(2)}) collective-permute-start(bf16[1,36,768]{2,1,0:T(8,128)(2,1)S(1)} %get-tuple-element.42.refs_0_), channel_id=1, source_target_pairs={{0,16},{4,20},{8,24},{12,28},{16,0},{20,4},{24,8},{28,12},{1,17},{... | collective-permute-start | bytes 165896 | tf_op jit(solution)/shard_map/ppermute | solution.py:322
  8.3 1.4 %collective-permute-start.3 = (bf16[1,36,768]{2,1,0:T(8,128)(2,1)S(1)}, bf16[1,36,768]{2,1,0:T(8,128)(2,1)S(1)}, u32[]{:S(2)}, u32[]{:S(2)}) collective-permute-start(bf16[1,36,768]{2,1,0:T(8,128)(2,1)S(1)} %get-tuple-element.42.refs_0_), channel_id=1, source_target_pairs={{0,24},{4,28},{8,16},{12,20},{16,8},{20,12},{24,0},{28,4},{1,25},{... | collective-permute-start | bytes 165896 | tf_op jit(solution)/shard_map/ppermute | solution.py:322
  9.8 0.0 collective-permute-done.refs_5_
  9.8 0.6 %collective-permute-start.1 = (bf16[1,36,768]{2,1,0:T(8,128)(2,1)S(1)}, bf16[1,36,768]{2,1,0:T(8,128)(2,1)S(1)}, u32[]{:S(2)}, u32[]{:S(2)}) collective-permute-start(bf16[1,36,768]{2,1,0:T(8,128)(2,1)S(1)} %get-tuple-element.42.refs_0_), channel_id=1, source_target_pairs={{0,8},{4,12},{8,0},{12,4},{16,24},{20,28},{24,16},{28,20},{1,9},{5... | collective-permute-start | bytes 165896 | tf_op jit(solution)/shard_map/ppermute | solution.py:322
  10.4 2.0 %fetch.1 = (bf16[768,768]{1,0:T(8,128)(2,1)S(1)}, bf16[768,768]{1,0:T(8,128)(2,1)S(1)}, bf16[768,768]{1,0:T(8,128)(2,1)S(1)}) custom-call(bf16[768,768]{1,0:T(8,128)(2,1)} %refs_0_.1, bf16[768,768]{1,0:T(8,128)(2,1)} %refs_1_.1, bf16[768,768]{1,0:T(8,128)(2,1)} %refs_2_.1), custom_call_target="tpu_custom_call" | custom-call | bytes 6291456 | tf_op jit(solution)/shard_map/fetch/pallas_call | solution.py:105
  12.4 1.1 %collective-permute-done.3.refs_3_ = bf16[1,36,768]{2,1,0:T(8,128)(2,1)S(1)} collective-permute-done((bf16[1,36,768]{2,1,0:T(8,128)(2,1)S(1)}, bf16[1,36,768]{2,1,0:T(8,128)(2,1)S(1)}, u32[]{:S(2)}, u32[]{:S(2)}) %collective-permute-start.3) | collective-permute-done | bytes 55328 | tf_op jit(solution)/shard_map/ppermute | solution.py:322
  13.5 0.5 %collective-permute-done.1.refs_1_ = bf16[1,36,768]{2,1,0:T(8,128)(2,1)S(1)} collective-permute-done((bf16[1,36,768]{2,1,0:T(8,128)(2,1)S(1)}, bf16[1,36,768]{2,1,0:T(8,128)(2,1)S(1)}, u32[]{:S(2)}, u32[]{:S(2)}) %collective-permute-start.1) | collective-permute-done | bytes 55328 | tf_op jit(solution)/shard_map/ppermute | solution.py:322
  14.0 0.5 %collective-permute-start.7 = (bf16[2,36,768]{2,1,0:T(8,128)(2,1)S(1)}, bf16[2,36,768]{2,1,0:T(8,128)(2,1)S(1)}, u32[]{:S(2)}, u32[]{:S(2)}) collective-permute-start(bf16[2,36,768]{2,1,0:T(8,128)(2,1)S(1)} %collective-permute-done.refs_5_), channel_id=1, source_target_pairs={{0,4},{4,0},{8,12},{12,8},{16,20},{20,16},{24,28},{28,24},{1,5},{5... | collective-permute-start | bytes 331784 | tf_op jit(solution)/shard_map/ppermute | solution.py:329
  14.5 1.8 %collective-permute-done.4.refs_6_ = bf16[2,36,768]{2,1,0:T(8,128)(2,1)S(1)} collective-permute-done((bf16[2,36,768]{2,1,0:T(8,128)(2,1)S(1)}, bf16[2,36,768]{2,1,0:T(8,128)(2,1)S(1)}, u32[]{:S(2)}, u32[]{:S(2)}) %collective-permute-start.4) | collective-permute-done | bytes 110624 | tf_op jit(solution)/shard_map/ppermute | solution.py:318
  16.3 0.5 %collective-permute-start.9 = (bf16[2,36,768]{2,1,0:T(8,128)(2,1)S(1)}, bf16[2,36,768]{2,1,0:T(8,128)(2,1)S(1)}, u32[]{:S(2)}, u32[]{:S(2)}) collective-permute-start(bf16[2,36,768]{2,1,0:T(8,128)(2,1)S(1)} %collective-permute-done.5.refs_7_), channel_id=1, source_target_pairs={{0,4},{4,0},{8,12},{12,8},{16,20},{20,16},{24,28},{28,24},{1,5},{5... | collective-permute-start | bytes 331784 | tf_op jit(solution)/shard_map/ppermute | solution.py:329
  16.8 1.4 %attention.2 = (bf16[1,36,768]{2,1,0:T(8,128)(2,1)S(1)}, bf16[1,36,768]{2,1,0:T(8,128)(2,1)S(1)}, bf16[1,36,768]{2,1,0:T(8,128)(2,1)S(1)}, bf16[1,36,768]{2,1,0:T(8,128)(2,1)S(1)}, bf16[160,768]{1,0:T(8,128)(2,1)S(1)}) custom-call(bf16[1,36,768]{2,1,0:T(8,128)(2,1)S(1)} %get-tuple-element.42.refs_0_, bf16[1,36,768]{2,1,0:T(8,128)(2,1)S(1)} %collective-permute-done.1.refs_1_, ...), custom_call_target="tpu_custom_call" | custom-call | flops 63700992 | bytes 1048576 | tf_op jit(solution)/shard_map/attention/pallas_call | solution.py:160
  18.3 1.4 %attention.3 = (bf16[2,36,768]{2,1,0:T(8,128)(2,1)S(1)}, bf16[2,36,768]{2,1,0:T(8,128)(2,1)S(1)}, bf16[2,36,768]{2,1,0:T(8,128)(2,1)S(1)}, bf16[2,36,768]{2,1,0:T(8,128)(2,1)S(1)}) custom-call(bf16[160,768]{1,0:T(8,128)(2,1)S(1)} %get-tuple-element.46.refs_0_, bf16[2,36,768]{2,1,0:T(8,128)(2,1)S(1)} %collective-permute-done.6.refs_1_, ...), custom_call_target="tpu_custom_call" | custom-call | flops 63700992 | bytes 1048576 | tf_op jit(solution)/shard_map/attention/pallas_call | solution.py:160
  19.7 2.5 %collective-permute-start.12 = (bf16[2,36,768]{2,1,0:T(8,128)(2,1)S(1)}, bf16[2,36,768]{2,1,0:T(8,128)(2,1)S(1)}, u32[]{:S(2)}, u32[]{:S(2)}) collective-permute-start(bf16[2,36,768]{2,1,0:T(8,128)(2,1)S(1)} %get-tuple-element.63), channel_id=1, source_target_pairs={{24,0},{28,4},{16,8},{20,12},{8,16},{12,20},{0,24},{4,28},{25,1},{... | collective-permute-start | bytes 331784 | tf_op jit(solution)/shard_map/ppermute | solution.py:337
  22.2 0.5 %collective-permute-start.10 = (bf16[2,36,768]{2,1,0:T(8,128)(2,1)S(1)}, bf16[2,36,768]{2,1,0:T(8,128)(2,1)S(1)}, u32[]{:S(2)}, u32[]{:S(2)}) collective-permute-start(bf16[2,36,768]{2,1,0:T(8,128)(2,1)S(1)} %get-tuple-element.55), channel_id=1, source_target_pairs={{8,0},{12,4},{0,8},{4,12},{24,16},{28,20},{16,24},{20,28},{9,1},{1... | collective-permute-start | bytes 331784 | tf_op jit(solution)/shard_map/ppermute | solution.py:337
  22.8 0.5 %collective-permute-start.11 = (bf16[2,36,768]{2,1,0:T(8,128)(2,1)S(1)}, bf16[2,36,768]{2,1,0:T(8,128)(2,1)S(1)}, u32[]{:S(2)}, u32[]{:S(2)}) collective-permute-start(bf16[2,36,768]{2,1,0:T(8,128)(2,1)S(1)} %get-tuple-element.56), channel_id=1, source_target_pairs={{16,0},{20,4},{24,8},{28,12},{0,16},{4,20},{8,24},{12,28},{17,1},{... | collective-permute-start | bytes 331784 | tf_op jit(solution)/shard_map/ppermute | solution.py:337
  23.3 0.9 %mix_own.1 = (f32[40,768]{1,0:T(8,128)S(1)}, f32[80,128]{1,0:T(8,128)S(1)}, f32[80,768]{1,0:T(8,128)S(1)}) custom-call(bf16[2,36,768]{2,1,0:T(8,128)(2,1)S(1)} %get-tuple-element.57.block, bf16[768,768]{1,0:T(8,128)(2,1)S(1)} %get-tuple-element.58.w_query, bf16[768,768]{1,0:T(8,128)(2,1)S(1)} %get-tuple-element.59.w_key.refs_3_, ...), custom_call_target="tpu_custom_call" | custom-call | flops 169869312 | bytes 4194304 | tf_op jit(solution)/shard_map/mix_own/pallas_call | solution.py:254
  24.2 2.7 %collective-permute-done.12.block = bf16[2,36,768]{2,1,0:T(8,128)(2,1)S(1)} collective-permute-done((bf16[2,36,768]{2,1,0:T(8,128)(2,1)S(1)}, bf16[2,36,768]{2,1,0:T(8,128)(2,1)S(1)}, u32[]{:S(2)}, u32[]{:S(2)}) %collective-permute-start.12) | collective-permute-done | bytes 110624 | tf_op jit(solution)/shard_map/ppermute | solution.py:337
  26.9 0.8 %mix_part.1 = (f32[80,128]{1,0:T(8,128)S(1)}, f32[80,768]{1,0:T(8,128)S(1)}) custom-call(bf16[2,36,768]{2,1,0:T(8,128)(2,1)S(1)} %collective-permute-done.12.block, f32[40,768]{1,0:T(8,128)S(1)} %get-tuple-element.61.query.refs_2_, bf16[768,768]{1,0:T(8,128)(2,1)S(1)} %get-tuple-element.59.w_key.refs_3_, bf16[768,768]{1,0:T(8,128)(2,1)S(1)} %get-tuple-element.60.w_value.refs_4_), custom_call_target="tpu_custom_call" | custom-call | flops 169869312 | bytes 4194304 | tf_op jit(solution)/shard_map/mix_part/pallas_call | solution.py:254
  27.7 0.9 %collective-permute-done.10.refs_0_ = bf16[2,36,768]{2,1,0:T(8,128)(2,1)S(1)} collective-permute-done((bf16[2,36,768]{2,1,0:T(8,128)(2,1)S(1)}, bf16[2,36,768]{2,1,0:T(8,128)(2,1)S(1)}, u32[]{:S(2)}, u32[]{:S(2)}) %collective-permute-start.10) | collective-permute-done | bytes 110624 | tf_op jit(solution)/shard_map/ppermute | solution.py:337
  28.6 1.6 %mix_last.1 = bf16[1,36,768]{2,1,0:T(8,128)(2,1)} custom-call(bf16[2,36,768]{2,1,0:T(8,128)(2,1)S(1)} %collective-permute-done.10.refs_0_, bf16[2,36,768]{2,1,0:T(8,128)(2,1)S(1)} %collective-permute-done.11.refs_1_, f32[40,768]{1,0:T(8,128)S(1)} %get-tuple-element.61.query.refs_2_, bf16[768,768]{1,0:T(8,128)(2,1)S(1)} %get-tuple-element.59.w_key.refs_3_, ...), custom_call_target="tpu_custom_call" | custom-call | flops 339738624 | bytes 4194304 | tf_op jit(solution)/shard_map/mix_last/pallas_call | solution.py:254
  (9 shorter events, 0.0 us)
Async XLA Ops:
  0.9 8.9 %collective-permute-start = (bf16[2,36,768]{2,1,0:T(8,128)(2,1)S(1)}, bf16[2,36,768]{2,1,0:T(8,128)(2,1)S(1)}, u32[]{:S(2)}, u32[]{:S(2)}) collective-permute-start(bf16[2,36,768]{2,1,0:T(8,128)(2,1)S(1)} %get-tuple-element.47.refs_4_), channel_id=1, source_target_pairs={{0,1},{1,0},{2,3},{3,2},{4,5},{5,4},{6,7},{7,6},{8,9},{9,8},{10,11... | collective-permute-start | bytes 331784 | tf_op jit(solution)/shard_map/ppermute | solution.py:318
  4.0 12.3 %collective-permute-start.4 = (bf16[2,36,768]{2,1,0:T(8,128)(2,1)S(1)}, bf16[2,36,768]{2,1,0:T(8,128)(2,1)S(1)}, u32[]{:S(2)}, u32[]{:S(2)}) collective-permute-start(bf16[2,36,768]{2,1,0:T(8,128)(2,1)S(1)} %get-tuple-element.47.refs_4_), channel_id=1, source_target_pairs={{0,2},{1,3},{2,0},{3,1},{4,6},{5,7},{6,4},{7,5},{8,10},{9,11},{10,... | collective-permute-start | bytes 331784 | tf_op jit(solution)/shard_map/ppermute | solution.py:318
  6.6 9.7 %collective-permute-start.5 = (bf16[2,36,768]{2,1,0:T(8,128)(2,1)S(1)}, bf16[2,36,768]{2,1,0:T(8,128)(2,1)S(1)}, u32[]{:S(2)}, u32[]{:S(2)}) collective-permute-start(bf16[2,36,768]{2,1,0:T(8,128)(2,1)S(1)} %get-tuple-element.47.refs_4_), channel_id=1, source_target_pairs={{0,3},{1,2},{2,1},{3,0},{4,7},{5,6},{6,5},{7,4},{8,11},{9,10},{10,... | collective-permute-start | bytes 331784 | tf_op jit(solution)/shard_map/ppermute | solution.py:318
  6.6 5.8 %collective-permute-start.2 = (bf16[1,36,768]{2,1,0:T(8,128)(2,1)S(1)}, bf16[1,36,768]{2,1,0:T(8,128)(2,1)S(1)}, u32[]{:S(2)}, u32[]{:S(2)}) collective-permute-start(bf16[1,36,768]{2,1,0:T(8,128)(2,1)S(1)} %get-tuple-element.42.refs_0_), channel_id=1, source_target_pairs={{0,16},{4,20},{8,24},{12,28},{16,0},{20,4},{24,8},{28,12},{1,17},{... | collective-permute-start | bytes 165896 | tf_op jit(solution)/shard_map/ppermute | solution.py:322
  8.3 5.1 %collective-permute-start.3 = (bf16[1,36,768]{2,1,0:T(8,128)(2,1)S(1)}, bf16[1,36,768]{2,1,0:T(8,128)(2,1)S(1)}, u32[]{:S(2)}, u32[]{:S(2)}) collective-permute-start(bf16[1,36,768]{2,1,0:T(8,128)(2,1)S(1)} %get-tuple-element.42.refs_0_), channel_id=1, source_target_pairs={{0,24},{4,28},{8,16},{12,20},{16,8},{20,12},{24,0},{28,4},{1,25},{... | collective-permute-start | bytes 165896 | tf_op jit(solution)/shard_map/ppermute | solution.py:322
  9.8 4.2 %collective-permute-start.1 = (bf16[1,36,768]{2,1,0:T(8,128)(2,1)S(1)}, bf16[1,36,768]{2,1,0:T(8,128)(2,1)S(1)}, u32[]{:S(2)}, u32[]{:S(2)}) collective-permute-start(bf16[1,36,768]{2,1,0:T(8,128)(2,1)S(1)} %get-tuple-element.42.refs_0_), channel_id=1, source_target_pairs={{0,8},{4,12},{8,0},{12,4},{16,24},{20,28},{24,16},{28,20},{1,9},{5... | collective-permute-start | bytes 165896 | tf_op jit(solution)/shard_map/ppermute | solution.py:322
  14.0 4.3 %collective-permute-start.6 = (bf16[2,36,768]{2,1,0:T(8,128)(2,1)S(1)}, bf16[2,36,768]{2,1,0:T(8,128)(2,1)S(1)}, u32[]{:S(2)}, u32[]{:S(2)}) collective-permute-start(bf16[2,36,768]{2,1,0:T(8,128)(2,1)S(1)} %get-tuple-element.47.refs_4_), channel_id=1, source_target_pairs={{0,4},{4,0},{8,12},{12,8},{16,20},{20,16},{24,28},{28,24},{1,5},{5... | collective-permute-start | bytes 331784 | tf_op jit(solution)/shard_map/ppermute | solution.py:329
  14.0 4.3 %collective-permute-start.7 = (bf16[2,36,768]{2,1,0:T(8,128)(2,1)S(1)}, bf16[2,36,768]{2,1,0:T(8,128)(2,1)S(1)}, u32[]{:S(2)}, u32[]{:S(2)}) collective-permute-start(bf16[2,36,768]{2,1,0:T(8,128)(2,1)S(1)} %collective-permute-done.refs_5_), channel_id=1, source_target_pairs={{0,4},{4,0},{8,12},{12,8},{16,20},{20,16},{24,28},{28,24},{1,5},{5... | collective-permute-start | bytes 331784 | tf_op jit(solution)/shard_map/ppermute | solution.py:329
  16.3 2.0 %collective-permute-start.8 = (bf16[2,36,768]{2,1,0:T(8,128)(2,1)S(1)}, bf16[2,36,768]{2,1,0:T(8,128)(2,1)S(1)}, u32[]{:S(2)}, u32[]{:S(2)}) collective-permute-start(bf16[2,36,768]{2,1,0:T(8,128)(2,1)S(1)} %collective-permute-done.4.refs_6_), channel_id=1, source_target_pairs={{0,4},{4,0},{8,12},{12,8},{16,20},{20,16},{24,28},{28,24},{1,5},{5... | collective-permute-start | bytes 331784 | tf_op jit(solution)/shard_map/ppermute | solution.py:329
  16.3 2.0 %collective-permute-start.9 = (bf16[2,36,768]{2,1,0:T(8,128)(2,1)S(1)}, bf16[2,36,768]{2,1,0:T(8,128)(2,1)S(1)}, u32[]{:S(2)}, u32[]{:S(2)}) collective-permute-start(bf16[2,36,768]{2,1,0:T(8,128)(2,1)S(1)} %collective-permute-done.5.refs_7_), channel_id=1, source_target_pairs={{0,4},{4,0},{8,12},{12,8},{16,20},{20,16},{24,28},{28,24},{1,5},{5... | collective-permute-start | bytes 331784 | tf_op jit(solution)/shard_map/ppermute | solution.py:329
  19.7 7.2 %collective-permute-start.12 = (bf16[2,36,768]{2,1,0:T(8,128)(2,1)S(1)}, bf16[2,36,768]{2,1,0:T(8,128)(2,1)S(1)}, u32[]{:S(2)}, u32[]{:S(2)}) collective-permute-start(bf16[2,36,768]{2,1,0:T(8,128)(2,1)S(1)} %get-tuple-element.63), channel_id=1, source_target_pairs={{24,0},{28,4},{16,8},{20,12},{8,16},{12,20},{0,24},{4,28},{25,1},{... | collective-permute-start | bytes 331784 | tf_op jit(solution)/shard_map/ppermute | solution.py:337
  22.2 6.4 %collective-permute-start.10 = (bf16[2,36,768]{2,1,0:T(8,128)(2,1)S(1)}, bf16[2,36,768]{2,1,0:T(8,128)(2,1)S(1)}, u32[]{:S(2)}, u32[]{:S(2)}) collective-permute-start(bf16[2,36,768]{2,1,0:T(8,128)(2,1)S(1)} %get-tuple-element.55), channel_id=1, source_target_pairs={{8,0},{12,4},{0,8},{4,12},{24,16},{28,20},{16,24},{20,28},{9,1},{1... | collective-permute-start | bytes 331784 | tf_op jit(solution)/shard_map/ppermute | solution.py:337
  22.8 5.8 %collective-permute-start.11 = (bf16[2,36,768]{2,1,0:T(8,128)(2,1)S(1)}, bf16[2,36,768]{2,1,0:T(8,128)(2,1)S(1)}, u32[]{:S(2)}, u32[]{:S(2)}) collective-permute-start(bf16[2,36,768]{2,1,0:T(8,128)(2,1)S(1)} %get-tuple-element.56), channel_id=1, source_target_pairs={{16,0},{20,4},{24,8},{28,12},{0,16},{4,20},{8,24},{12,28},{17,1},{... | collective-permute-start | bytes 331784 | tf_op jit(solution)/shard_map/ppermute | solution.py:337

commit v5 on v4

--- a/solution.py
+++ b/solution.py
@@ -13,6 +13,7 @@
 VMEM = pl.BlockSpec(memory_space=pltpu.VMEM)
 FAR = pl.BlockSpec(memory_space=pltpu.HBM)
 NT = (((1,), (1,)), ((), ()))
+TN = (((0,), (0,)), ((), ()))
 
 
 def far(array):
@@ -23,43 +24,41 @@
     return -(-value // unit) * unit
 
 
-def stack_rows(blocks, stage):
+def stack_rows(blocks, stage, pitch):
     rows = blocks[0].shape[0]
-    pitch = ceil_to(rows, 8)
     for index, block in enumerate(blocks):
         stage[pl.ds(index * pitch, rows), :] = block.astype(jnp.float32)
-        if pitch > rows:
-            stage[pl.ds(index * pitch + rows, pitch - rows), :] = jnp.zeros(
-                (pitch - rows, stage.shape[1]), jnp.float32
-            )
+        end = stage.shape[0] if index == len(blocks) - 1 else (index + 1) * pitch
+        gap = end - index * pitch - rows
+        if gap:
+            stage[pl.ds(index * pitch + rows, gap), :] = jnp.zeros((gap, stage.shape[1]), jnp.float32)
     return stage[...].astype(jnp.bfloat16)
 
 
-def attend(query, key, value, valid, head_width, put):
+def attend(query, key, value, key_count, head_width, out):
     per_slab = LANES // head_width
     factor = math.log2(math.e) / math.sqrt(head_width)
-    key_total = key.shape[0]
-    lane = lax.broadcasted_iota(jnp.int32, (key_total, LANES), 1) // head_width
-    bias = jnp.where(valid, 0.0, -1e30)
-    for slab in range(query.shape[1] // LANES):
-        cut = slice(slab * LANES, (slab + 1) * LANES)
-        query_slab, key_slab, value_slab = query[:, cut], key[:, cut], value[:, cut]
-        total = None
-        for head in range(per_slab):
-            own = lane == head
-            masked_key = jnp.where(own, key_slab, 0)
-            scores = lax.dot_general(query_slab, masked_key, NT, preferred_element_type=jnp.float32)
-            scores = scores + bias
-            top = jnp.max(scores, axis=1, keepdims=True)
-            weights = jnp.exp2((scores - top) * factor)
-            weights = weights * (1.0 / jnp.sum(weights, axis=1, keepdims=True))
-            part = jnp.dot(
-                weights.astype(jnp.bfloat16),
-                jnp.where(own, value_slab, 0),
-                preferred_element_type=jnp.float32,
-            )
-            total = part if total is None else total + part
-        put(slab, total)
+    query_total, key_total = query.shape[0], key.shape[0]
+    head = lax.broadcasted_iota(jnp.int32, (query_total, LANES), 1) // head_width
+    for at in range(0, query.shape[1], LANES):
+        cut = slice(at, at + LANES)
+        side = jnp.concatenate(
+            [jnp.where(head == index, query[:, cut], 0) for index in range(per_slab)], axis=0
+        )
+        scores = lax.dot_general(key[:, cut], side, NT, preferred_element_type=jnp.float32)
+        if key_count < key_total:
+            place = lax.broadcasted_iota(jnp.int32, (key_total, 1), 0)
+            scores = scores + jnp.where(place < key_count, 0.0, -1e30)
+        top = jnp.max(scores, axis=0, keepdims=True)
+        weights = jnp.exp2((scores - top) * factor)
+        weights = weights * (1.0 / jnp.sum(weights, axis=0, keepdims=True))
+        pooled = lax.dot_general(
+            weights.astype(jnp.bfloat16), value[:, cut], TN, preferred_element_type=jnp.float32
+        )
+        mine = pooled[:query_total]
+        for index in range(1, per_slab):
+            mine = jnp.where(head == index, pooled[index * query_total : (index + 1) * query_total], mine)
+        out[:, cut] = mine
 
 
 def load_kernel(key, value, query, pair, near_query, sems):
@@ -114,60 +113,51 @@
     )(*map(far, weights))
 
 
-def attention_kernel(head_width, query_count, forms, *refs):
-    first = query_count > 1
+def attention_kernel(head_width, query_count, earlier_count, forms, *refs):
     queries, refs = refs[:query_count], refs[query_count:]
     keys, values = [], []
     for form in forms:
         keys.append(refs[0].at[0])
         values.append(refs[form - 1].at[2 - form])
         refs = refs[form:]
-    if first:
-        *outs, stacked, key_stage, value_stage, query_stage = refs
-        query = stack_rows([ref[0] for ref in queries], query_stage)
+    *refs, key_stage, value_stage, query_stage = refs
+    rows = keys[0].shape[-2]
+    if earlier_count:
+        earlier, outs = refs[:earlier_count], refs[earlier_count:]
+        query = queries[0][...]
+    else:
+        earlier, (*outs, stacked) = (), refs
+        query = stack_rows([ref[0] for ref in queries], query_stage, rows)
         stacked[...] = query
-        earlier = ()
-    else:
-        *refs, key_stage, value_stage = refs
-        earlier, outs = refs[: len(refs) // 2], refs[len(refs) // 2 :]
-        query = queries[0][...]
-    rows = keys[0].shape[-2]
-    pitch = ceil_to(rows, 8)
-    key = stack_rows([ref[...] for ref in keys], key_stage)
-    value = stack_rows([ref[...] for ref in values], value_stage)
-    place = lax.broadcasted_iota(jnp.int32, (1, key.shape[0]), 1)
-    valid = lax.rem(place, pitch) < rows
-
-    def put(slab, pooled):
-        for index, out in enumerate(outs):
-            out[out.shape[0] - 1, :, pl.ds(slab * LANES, LANES)] = pooled[
-                index * pitch : index * pitch + rows
-            ].astype(jnp.bfloat16)
-
-    attend(query, key, value, valid, head_width, put)
+    key = stack_rows([ref[...] for ref in keys], key_stage, rows)
+    value = stack_rows([ref[...] for ref in values], value_stage, rows)
+    attend(query, key, value, len(keys) * rows, head_width, query_stage)
+    for index, out in enumerate(outs):
+        out[out.shape[0] - 1] = query_stage[pl.ds(index * rows, rows), :].astype(out.dtype)
     for out, ref in zip(outs, earlier):
         out[0] = ref[0]
 
 
 def attention(queries, blocks, earlier=()):
     _, rows, width = blocks[0][0].shape
-    pitch = ceil_to(rows, 8)
     count = len(earlier) or len(queries)
-    total = count * pitch
+    query_total, key_total = ceil_to(count * rows, 16), ceil_to(len(blocks) * rows, 16)
     flops = 4 * count * rows * len(blocks) * rows * width
     shape = jax.ShapeDtypeStruct((2 if earlier else 1, rows, width), jnp.bfloat16)
     first = not earlier
-    out = pl.pallas_call(
-        functools.partial(attention_kernel, width // HEADS, len(queries), [len(block) for block in blocks]),
-        out_shape=[shape] * count + [near((total, width), jnp.bfloat16)] * first,
+    kernel = functools.partial(
+        attention_kernel, width // HEADS, len(queries), len(earlier), [len(block) for block in blocks]
+    )
+    return pl.pallas_call(
+        kernel,
+        out_shape=[shape] * count + [near((query_total, width), jnp.bfloat16)] * first,
         in_specs=[VMEM] * (len(queries) + sum(map(len, blocks)) + len(earlier)),
         out_specs=[VMEM] * (count + first),
-        scratch_shapes=[near((len(blocks) * pitch, width))] * 2 + [near((total, width))] * first,
-        compiler_params=pltpu.CompilerParams(vmem_limit_bytes=32 << 20),
+        scratch_shapes=[near((key_total, width))] * 2 + [near((query_total, width))],
+        compiler_params=pltpu.CompilerParams(vmem_limit_bytes=48 << 20),
         cost_estimate=pl.CostEstimate(flops=flops, bytes_accessed=1 << 20, transcendentals=0),
         name="attention",
     )(*queries, *(array for block in blocks for array in block), *earlier)
-    return out
 
 
 def head_members(width, head_width):
@@ -201,7 +191,7 @@
 
 
 def stack_pooled(ref, stage):
-    return stack_rows([ref[index] for index in range(ref.shape[0])], stage)
+    return stack_rows([ref[index] for index in range(ref.shape[0])], stage, ceil_to(ref.shape[1], 8))
 
 
 def own_kernel(head_width, block, w_query, w_key, w_value, query, scores, values, stage):
@@ -221,8 +211,8 @@
 def last_kernel(head_width, earlier, count, *refs):
     blocks, (query, w_key, w_value), refs = refs[:count], refs[count : count + 3], refs[count + 3 :]
     score_refs, value_refs, (out, stage) = refs[:earlier], refs[earlier : 2 * earlier], refs[-2:]
-    pooled = stack_rows([ref[index] for ref in blocks for index in range(ref.shape[0])], stage)
     pitch, width = query.shape
+    pooled = stack_rows([ref[index] for ref in blocks for index in range(ref.shape[0])], stage, pitch)
     score_parts = [ref[...] for ref in score_refs] + [score(query[...], pooled, w_key, head_width)]
     value_parts = [ref[...] for ref in value_refs] + [project(pooled, w_value)]
     places = [
@@ -324,7 +314,11 @@
     ]
     w_query, w_key, w_value = fetch((w_query, w_key, w_value))
     *queries, w_query, w_key, w_value = lax.optimization_barrier((*queries, w_query, w_key, w_value))
-    turned = [lax.optimization_barrier((block, *queries))[0] for block in blocks]
+    turned = [
+        lax.optimization_barrier((block, *queries, *blocks[index + 1 :]))[0]
+        for index, block in enumerate(blocks)
+    ]
+    turned[:2] = [lax.optimization_barrier((block, *queries))[0] for block in blocks[:2]]
     other_blocks = [
         tuple(lax.ppermute(array, "frame", swap) for array in block) for block in turned
     ]

time: 30.4 us -> 29.8 us (0.980)
  Pallas kernels: 9.13 us -> 8.14 us
  waiting for transfers between devices: 6.99 us -> 7.36 us
    pallas_call x2, Pallas kernels: 2.85 us -> 1.86 us  [attention(): pl.pallas_call(kernel, out_shape=[shape] * count + [near((query_total, wi...]
    ppermute x3, waiting for transfers between devices: 3.57 us -> 3.9 us  [per_device(): lax.ppermute(block, 'frame', back)]
  transfers between devices with their start and end apart: 13 -> 13, of which waited for: 5 -> 5; matrix products, arithmetic and copies ran while one was open for 0% -> 0% of each run, Pallas kernels for 17% -> 16%
where the time goes in v5:
time: 29.8 us; the launch traced here: 29.6 us
  starting transfers between devices  14 us (47%)
  Pallas kernels  8.14 us (27%)
  waiting for transfers between devices  7.36 us (25%)
    ppermute x3, starting transfers between devices, per_device(): lax.ppermute(own_block, 'qblk', there)  5.68 us
    ppermute x3, waiting for transfers between devices, per_device(): lax.ppermute(block, 'frame', back)  3.9 us
    ppermute x3, starting transfers between devices, per_device(): lax.ppermute(ready_query if step == 0 else near_query, 'frame', there)  3.77 us
    ppermute x3, starting transfers between devices, per_device(): lax.ppermute(block, 'frame', back)  3.55 us
    pallas_call x3, Pallas kernels, mix_call(): pl.pallas_call(functools.partial(kernel, width // HEADS), out_shape=out_s...  3.36 us
    pallas_call x1, Pallas kernels, fetch(): pl.pallas_call(fetch_kernel, out_shape=[pltpu.VMEM(matrix.shape, matrix.d...  2.01 us
    pallas_call x2, Pallas kernels, attention(): pl.pallas_call(kernel, out_shape=[shape] * count + [near((query_total, wi...  1.86 us
    ppermute x3, waiting for transfers between devices, per_device(): lax.ppermute(own_block, 'qblk', there)  1.81 us
  transfers between devices with their start and end apart: 13, of which 5 were waited for; matrix products, arithmetic and copies ran while one was open for 0% of the time, Pallas kernels for 16%

profile of v5, /device:TPU:0, one launch (start us, length us, event | category | flops | bytes accessed | tf_op | source)
XLA Modules:
  0.0 29.6 jit_solution(2646660934237449831)
XLA Ops:
  0.0 0.9 %load.1 = (bf16[2,36,768]{2,1,0:T(8,128)(2,1)S(1)}, bf16[1,36,768]{2,1,0:T(8,128)(2,1)S(1)}) custom-call(bf16[1,36,768]{2,1,0:T(8,128)(2,1)} %key.1, bf16[1,36,768]{2,1,0:T(8,128)(2,1)} %value.1, bf16[1,36,768]{2,1,0:T(8,128)(2,1)} %query.1), custom_call_target="tpu_custom_call" | custom-call | tf_op jit(solution)/shard_map/load/pallas_call | solution.py:77
  0.9 3.1 %collective-permute-start = (bf16[2,36,768]{2,1,0:T(8,128)(2,1)S(1)}, bf16[2,36,768]{2,1,0:T(8,128)(2,1)S(1)}, u32[]{:S(2)}, u32[]{:S(2)}) collective-permute-start(bf16[2,36,768]{2,1,0:T(8,128)(2,1)S(1)} %get-tuple-element.47.refs_4_), channel_id=1, source_target_pairs={{0,1},{1,0},{2,3},{3,2},{4,5},{5,4},{6,7},{7,6},{8,9},{9,8},{10,11... | collective-permute-start | bytes 331784 | tf_op jit(solution)/shard_map/ppermute | solution.py:308
  4.0 2.6 %collective-permute-start.4 = (bf16[2,36,768]{2,1,0:T(8,128)(2,1)S(1)}, bf16[2,36,768]{2,1,0:T(8,128)(2,1)S(1)}, u32[]{:S(2)}, u32[]{:S(2)}) collective-permute-start(bf16[2,36,768]{2,1,0:T(8,128)(2,1)S(1)} %get-tuple-element.47.refs_4_), channel_id=1, source_target_pairs={{0,2},{1,3},{2,0},{3,1},{4,6},{5,7},{6,4},{7,5},{8,10},{9,11},{10,... | collective-permute-start | bytes 331784 | tf_op jit(solution)/shard_map/ppermute | solution.py:308
  6.6 1.7 %collective-permute-start.2 = (bf16[1,36,768]{2,1,0:T(8,128)(2,1)S(1)}, bf16[1,36,768]{2,1,0:T(8,128)(2,1)S(1)}, u32[]{:S(2)}, u32[]{:S(2)}) collective-permute-start(bf16[1,36,768]{2,1,0:T(8,128)(2,1)S(1)} %get-tuple-element.42.refs_0_), channel_id=1, source_target_pairs={{0,16},{4,20},{8,24},{12,28},{16,0},{20,4},{24,8},{28,12},{1,17},{... | collective-permute-start | bytes 165896 | tf_op jit(solution)/shard_map/ppermute | solution.py:312
  8.3 1.4 %collective-permute-start.3 = (bf16[1,36,768]{2,1,0:T(8,128)(2,1)S(1)}, bf16[1,36,768]{2,1,0:T(8,128)(2,1)S(1)}, u32[]{:S(2)}, u32[]{:S(2)}) collective-permute-start(bf16[1,36,768]{2,1,0:T(8,128)(2,1)S(1)} %get-tuple-element.42.refs_0_), channel_id=1, source_target_pairs={{0,24},{4,28},{8,16},{12,20},{16,8},{20,12},{24,0},{28,4},{1,25},{... | collective-permute-start | bytes 165896 | tf_op jit(solution)/shard_map/ppermute | solution.py:312
  9.8 0.6 %collective-permute-start.1 = (bf16[1,36,768]{2,1,0:T(8,128)(2,1)S(1)}, bf16[1,36,768]{2,1,0:T(8,128)(2,1)S(1)}, u32[]{:S(2)}, u32[]{:S(2)}) collective-permute-start(bf16[1,36,768]{2,1,0:T(8,128)(2,1)S(1)} %get-tuple-element.42.refs_0_), channel_id=1, source_target_pairs={{0,8},{4,12},{8,0},{12,4},{16,24},{20,28},{24,16},{28,20},{1,9},{5... | collective-permute-start | bytes 165896 | tf_op jit(solution)/shard_map/ppermute | solution.py:312
  10.4 2.0 %fetch.1 = (bf16[768,768]{1,0:T(8,128)(2,1)S(1)}, bf16[768,768]{1,0:T(8,128)(2,1)S(1)}, bf16[768,768]{1,0:T(8,128)(2,1)S(1)}) custom-call(bf16[768,768]{1,0:T(8,128)(2,1)} %refs_0_.1, bf16[768,768]{1,0:T(8,128)(2,1)} %refs_1_.1, bf16[768,768]{1,0:T(8,128)(2,1)} %refs_2_.1), custom_call_target="tpu_custom_call" | custom-call | bytes 6291456 | tf_op jit(solution)/shard_map/fetch/pallas_call | solution.py:104
  12.4 0.0 collective-permute-done.2.refs_2_
  12.4 1.1 %collective-permute-done.3.refs_3_ = bf16[1,36,768]{2,1,0:T(8,128)(2,1)S(1)} collective-permute-done((bf16[1,36,768]{2,1,0:T(8,128)(2,1)S(1)}, bf16[1,36,768]{2,1,0:T(8,128)(2,1)S(1)}, u32[]{:S(2)}, u32[]{:S(2)}) %collective-permute-start.3) | collective-permute-done | bytes 55328 | tf_op jit(solution)/shard_map/ppermute | solution.py:312
  13.5 0.5 %collective-permute-done.1.refs_1_ = bf16[1,36,768]{2,1,0:T(8,128)(2,1)S(1)} collective-permute-done((bf16[1,36,768]{2,1,0:T(8,128)(2,1)S(1)}, bf16[1,36,768]{2,1,0:T(8,128)(2,1)S(1)}, u32[]{:S(2)}, u32[]{:S(2)}) %collective-permute-start.1) | collective-permute-done | bytes 55328 | tf_op jit(solution)/shard_map/ppermute | solution.py:312
  14.0 0.5 %collective-permute-start.7 = (bf16[2,36,768]{2,1,0:T(8,128)(2,1)S(1)}, bf16[2,36,768]{2,1,0:T(8,128)(2,1)S(1)}, u32[]{:S(2)}, u32[]{:S(2)}) collective-permute-start(bf16[2,36,768]{2,1,0:T(8,128)(2,1)S(1)} %collective-permute-done.refs_5_), channel_id=1, source_target_pairs={{0,4},{4,0},{8,12},{12,8},{16,20},{20,16},{24,28},{28,24},{1,5},{5... | collective-permute-start | bytes 331784 | tf_op jit(solution)/shard_map/ppermute | solution.py:323
  14.5 1.8 %collective-permute-done.4.refs_6_ = bf16[2,36,768]{2,1,0:T(8,128)(2,1)S(1)} collective-permute-done((bf16[2,36,768]{2,1,0:T(8,128)(2,1)S(1)}, bf16[2,36,768]{2,1,0:T(8,128)(2,1)S(1)}, u32[]{:S(2)}, u32[]{:S(2)}) %collective-permute-start.4) | collective-permute-done | bytes 110624 | tf_op jit(solution)/shard_map/ppermute | solution.py:308
  16.3 0.5 %collective-permute-start.9 = (bf16[2,36,768]{2,1,0:T(8,128)(2,1)S(1)}, bf16[2,36,768]{2,1,0:T(8,128)(2,1)S(1)}, u32[]{:S(2)}, u32[]{:S(2)}) collective-permute-start(bf16[2,36,768]{2,1,0:T(8,128)(2,1)S(1)} %collective-permute-done.5.refs_7_), channel_id=1, source_target_pairs={{0,4},{4,0},{8,12},{12,8},{16,20},{20,16},{24,28},{28,24},{1,5},{5... | collective-permute-start | bytes 331784 | tf_op jit(solution)/shard_map/ppermute | solution.py:323
  16.8 0.9 %attention.2 = (bf16[1,36,768]{2,1,0:T(8,128)(2,1)S(1)}, bf16[1,36,768]{2,1,0:T(8,128)(2,1)S(1)}, bf16[1,36,768]{2,1,0:T(8,128)(2,1)S(1)}, bf16[1,36,768]{2,1,0:T(8,128)(2,1)S(1)}, bf16[144,768]{1,0:T(8,128)(2,1)S(1)}) custom-call(bf16[1,36,768]{2,1,0:T(8,128)(2,1)S(1)} %get-tuple-element.42.refs_0_, bf16[1,36,768]{2,1,0:T(8,128)(2,1)S(1)} %collective-permute-done.1.refs_1_, ...), custom_call_target="tpu_custom_call" | custom-call | flops 63700992 | bytes 1048576 | tf_op jit(solution)/shard_map/attention/pallas_call | solution.py:151
  17.8 0.0 collective-permute-done.9.refs_4_
  17.8 0.9 %attention.3 = (bf16[2,36,768]{2,1,0:T(8,128)(2,1)S(1)}, bf16[2,36,768]{2,1,0:T(8,128)(2,1)S(1)}, bf16[2,36,768]{2,1,0:T(8,128)(2,1)S(1)}, bf16[2,36,768]{2,1,0:T(8,128)(2,1)S(1)}) custom-call(bf16[144,768]{1,0:T(8,128)(2,1)S(1)} %get-tuple-element.46.refs_0_, bf16[2,36,768]{2,1,0:T(8,128)(2,1)S(1)} %collective-permute-done.6.refs_1_, ...), custom_call_target="tpu_custom_call" | custom-call | flops 63700992 | bytes 1048576 | tf_op jit(solution)/shard_map/attention/pallas_call | solution.py:151
  18.8 2.5 %collective-permute-start.12 = (bf16[2,36,768]{2,1,0:T(8,128)(2,1)S(1)}, bf16[2,36,768]{2,1,0:T(8,128)(2,1)S(1)}, u32[]{:S(2)}, u32[]{:S(2)}) collective-permute-start(bf16[2,36,768]{2,1,0:T(8,128)(2,1)S(1)} %get-tuple-element.63), channel_id=1, source_target_pairs={{24,0},{28,4},{16,8},{20,12},{8,16},{12,20},{0,24},{4,28},{25,1},{... | collective-permute-start | bytes 331784 | tf_op jit(solution)/shard_map/ppermute | solution.py:331
  21.3 0.5 %collective-permute-start.10 = (bf16[2,36,768]{2,1,0:T(8,128)(2,1)S(1)}, bf16[2,36,768]{2,1,0:T(8,128)(2,1)S(1)}, u32[]{:S(2)}, u32[]{:S(2)}) collective-permute-start(bf16[2,36,768]{2,1,0:T(8,128)(2,1)S(1)} %get-tuple-element.55), channel_id=1, source_target_pairs={{8,0},{12,4},{0,8},{4,12},{24,16},{28,20},{16,24},{20,28},{9,1},{1... | collective-permute-start | bytes 331784 | tf_op jit(solution)/shard_map/ppermute | solution.py:331
  21.8 0.5 %collective-permute-start.11 = (bf16[2,36,768]{2,1,0:T(8,128)(2,1)S(1)}, bf16[2,36,768]{2,1,0:T(8,128)(2,1)S(1)}, u32[]{:S(2)}, u32[]{:S(2)}) collective-permute-start(bf16[2,36,768]{2,1,0:T(8,128)(2,1)S(1)} %get-tuple-element.56), channel_id=1, source_target_pairs={{16,0},{20,4},{24,8},{28,12},{0,16},{4,20},{8,24},{12,28},{17,1},{... | collective-permute-start | bytes 331784 | tf_op jit(solution)/shard_map/ppermute | solution.py:331
  22.3 0.9 %mix_own.1 = (f32[40,768]{1,0:T(8,128)S(1)}, f32[80,128]{1,0:T(8,128)S(1)}, f32[80,768]{1,0:T(8,128)S(1)}) custom-call(bf16[2,36,768]{2,1,0:T(8,128)(2,1)S(1)} %get-tuple-element.57.block, bf16[768,768]{1,0:T(8,128)(2,1)S(1)} %get-tuple-element.58.w_query, bf16[768,768]{1,0:T(8,128)(2,1)S(1)} %get-tuple-element.59.w_key.refs_3_, ...), custom_call_target="tpu_custom_call" | custom-call | flops 169869312 | bytes 4194304 | tf_op jit(solution)/shard_map/mix_own/pallas_call | solution.py:244
  23.3 2.6 %collective-permute-done.12.block = bf16[2,36,768]{2,1,0:T(8,128)(2,1)S(1)} collective-permute-done((bf16[2,36,768]{2,1,0:T(8,128)(2,1)S(1)}, bf16[2,36,768]{2,1,0:T(8,128)(2,1)S(1)}, u32[]{:S(2)}, u32[]{:S(2)}) %collective-permute-start.12) | collective-permute-done | bytes 110624 | tf_op jit(solution)/shard_map/ppermute | solution.py:331
  25.9 0.8 %mix_part.1 = (f32[80,128]{1,0:T(8,128)S(1)}, f32[80,768]{1,0:T(8,128)S(1)}) custom-call(bf16[2,36,768]{2,1,0:T(8,128)(2,1)S(1)} %collective-permute-done.12.block, f32[40,768]{1,0:T(8,128)S(1)} %get-tuple-element.61.query.refs_2_, bf16[768,768]{1,0:T(8,128)(2,1)S(1)} %get-tuple-element.59.w_key.refs_3_, bf16[768,768]{1,0:T(8,128)(2,1)S(1)} %get-tuple-element.60.w_value.refs_4_), custom_call_target="tpu_custom_call" | custom-call | flops 169869312 | bytes 4194304 | tf_op jit(solution)/shard_map/mix_part/pallas_call | solution.py:244
  26.7 1.3 %collective-permute-done.10.refs_0_ = bf16[2,36,768]{2,1,0:T(8,128)(2,1)S(1)} collective-permute-done((bf16[2,36,768]{2,1,0:T(8,128)(2,1)S(1)}, bf16[2,36,768]{2,1,0:T(8,128)(2,1)S(1)}, u32[]{:S(2)}, u32[]{:S(2)}) %collective-permute-start.10) | collective-permute-done | bytes 110624 | tf_op jit(solution)/shard_map/ppermute | solution.py:331
  28.0 1.6 %mix_last.1 = bf16[1,36,768]{2,1,0:T(8,128)(2,1)} custom-call(bf16[2,36,768]{2,1,0:T(8,128)(2,1)S(1)} %collective-permute-done.10.refs_0_, bf16[2,36,768]{2,1,0:T(8,128)(2,1)S(1)} %collective-permute-done.11.refs_1_, f32[40,768]{1,0:T(8,128)S(1)} %get-tuple-element.61.query.refs_2_, bf16[768,768]{1,0:T(8,128)(2,1)S(1)} %get-tuple-element.59.w_key.refs_3_, ...), custom_call_target="tpu_custom_call" | custom-call | flops 339738624 | bytes 4194304 | tf_op jit(solution)/shard_map/mix_last/pallas_call | solution.py:244
  (9 shorter events, 0.0 us)
Async XLA Ops:
  0.9 8.9 %collective-permute-start = (bf16[2,36,768]{2,1,0:T(8,128)(2,1)S(1)}, bf16[2,36,768]{2,1,0:T(8,128)(2,1)S(1)}, u32[]{:S(2)}, u32[]{:S(2)}) collective-permute-start(bf16[2,36,768]{2,1,0:T(8,128)(2,1)S(1)} %get-tuple-element.47.refs_4_), channel_id=1, source_target_pairs={{0,1},{1,0},{2,3},{3,2},{4,5},{5,4},{6,7},{7,6},{8,9},{9,8},{10,11... | collective-permute-start | bytes 331784 | tf_op jit(solution)/shard_map/ppermute | solution.py:308
  4.0 12.3 %collective-permute-start.4 = (bf16[2,36,768]{2,1,0:T(8,128)(2,1)S(1)}, bf16[2,36,768]{2,1,0:T(8,128)(2,1)S(1)}, u32[]{:S(2)}, u32[]{:S(2)}) collective-permute-start(bf16[2,36,768]{2,1,0:T(8,128)(2,1)S(1)} %get-tuple-element.47.refs_4_), channel_id=1, source_target_pairs={{0,2},{1,3},{2,0},{3,1},{4,6},{5,7},{6,4},{7,5},{8,10},{9,11},{10,... | collective-permute-start | bytes 331784 | tf_op jit(solution)/shard_map/ppermute | solution.py:308
  6.6 9.7 %collective-permute-start.5 = (bf16[2,36,768]{2,1,0:T(8,128)(2,1)S(1)}, bf16[2,36,768]{2,1,0:T(8,128)(2,1)S(1)}, u32[]{:S(2)}, u32[]{:S(2)}) collective-permute-start(bf16[2,36,768]{2,1,0:T(8,128)(2,1)S(1)} %get-tuple-element.47.refs_4_), channel_id=1, source_target_pairs={{0,3},{1,2},{2,1},{3,0},{4,7},{5,6},{6,5},{7,4},{8,11},{9,10},{10,... | collective-permute-start | bytes 331784 | tf_op jit(solution)/shard_map/ppermute | solution.py:308
  6.6 5.8 %collective-permute-start.2 = (bf16[1,36,768]{2,1,0:T(8,128)(2,1)S(1)}, bf16[1,36,768]{2,1,0:T(8,128)(2,1)S(1)}, u32[]{:S(2)}, u32[]{:S(2)}) collective-permute-start(bf16[1,36,768]{2,1,0:T(8,128)(2,1)S(1)} %get-tuple-element.42.refs_0_), channel_id=1, source_target_pairs={{0,16},{4,20},{8,24},{12,28},{16,0},{20,4},{24,8},{28,12},{1,17},{... | collective-permute-start | bytes 165896 | tf_op jit(solution)/shard_map/ppermute | solution.py:312
  8.3 5.1 %collective-permute-start.3 = (bf16[1,36,768]{2,1,0:T(8,128)(2,1)S(1)}, bf16[1,36,768]{2,1,0:T(8,128)(2,1)S(1)}, u32[]{:S(2)}, u32[]{:S(2)}) collective-permute-start(bf16[1,36,768]{2,1,0:T(8,128)(2,1)S(1)} %get-tuple-element.42.refs_0_), channel_id=1, source_target_pairs={{0,24},{4,28},{8,16},{12,20},{16,8},{20,12},{24,0},{28,4},{1,25},{... | collective-permute-start | bytes 165896 | tf_op jit(solution)/shard_map/ppermute | solution.py:312
  9.8 4.2 %collective-permute-start.1 = (bf16[1,36,768]{2,1,0:T(8,128)(2,1)S(1)}, bf16[1,36,768]{2,1,0:T(8,128)(2,1)S(1)}, u32[]{:S(2)}, u32[]{:S(2)}) collective-permute-start(bf16[1,36,768]{2,1,0:T(8,128)(2,1)S(1)} %get-tuple-element.42.refs_0_), channel_id=1, source_target_pairs={{0,8},{4,12},{8,0},{12,4},{16,24},{20,28},{24,16},{28,20},{1,9},{5... | collective-permute-start | bytes 165896 | tf_op jit(solution)/shard_map/ppermute | solution.py:312
  14.0 3.8 %collective-permute-start.6 = (bf16[2,36,768]{2,1,0:T(8,128)(2,1)S(1)}, bf16[2,36,768]{2,1,0:T(8,128)(2,1)S(1)}, u32[]{:S(2)}, u32[]{:S(2)}) collective-permute-start(bf16[2,36,768]{2,1,0:T(8,128)(2,1)S(1)} %get-tuple-element.47.refs_4_), channel_id=1, source_target_pairs={{0,4},{4,0},{8,12},{12,8},{16,20},{20,16},{24,28},{28,24},{1,5},{5... | collective-permute-start | bytes 331784 | tf_op jit(solution)/shard_map/ppermute | solution.py:323
  14.0 3.8 %collective-permute-start.7 = (bf16[2,36,768]{2,1,0:T(8,128)(2,1)S(1)}, bf16[2,36,768]{2,1,0:T(8,128)(2,1)S(1)}, u32[]{:S(2)}, u32[]{:S(2)}) collective-permute-start(bf16[2,36,768]{2,1,0:T(8,128)(2,1)S(1)} %collective-permute-done.refs_5_), channel_id=1, source_target_pairs={{0,4},{4,0},{8,12},{12,8},{16,20},{20,16},{24,28},{28,24},{1,5},{5... | collective-permute-start | bytes 331784 | tf_op jit(solution)/shard_map/ppermute | solution.py:323
  16.3 1.5 %collective-permute-start.8 = (bf16[2,36,768]{2,1,0:T(8,128)(2,1)S(1)}, bf16[2,36,768]{2,1,0:T(8,128)(2,1)S(1)}, u32[]{:S(2)}, u32[]{:S(2)}) collective-permute-start(bf16[2,36,768]{2,1,0:T(8,128)(2,1)S(1)} %collective-permute-done.4.refs_6_), channel_id=1, source_target_pairs={{0,4},{4,0},{8,12},{12,8},{16,20},{20,16},{24,28},{28,24},{1,5},{5... | collective-permute-start | bytes 331784 | tf_op jit(solution)/shard_map/ppermute | solution.py:323
  16.3 1.5 %collective-permute-start.9 = (bf16[2,36,768]{2,1,0:T(8,128)(2,1)S(1)}, bf16[2,36,768]{2,1,0:T(8,128)(2,1)S(1)}, u32[]{:S(2)}, u32[]{:S(2)}) collective-permute-start(bf16[2,36,768]{2,1,0:T(8,128)(2,1)S(1)} %collective-permute-done.5.refs_7_), channel_id=1, source_target_pairs={{0,4},{4,0},{8,12},{12,8},{16,20},{20,16},{24,28},{28,24},{1,5},{5... | collective-permute-start | bytes 331784 | tf_op jit(solution)/shard_map/ppermute | solution.py:323
  18.8 7.1 %collective-permute-start.12 = (bf16[2,36,768]{2,1,0:T(8,128)(2,1)S(1)}, bf16[2,36,768]{2,1,0:T(8,128)(2,1)S(1)}, u32[]{:S(2)}, u32[]{:S(2)}) collective-permute-start(bf16[2,36,768]{2,1,0:T(8,128)(2,1)S(1)} %get-tuple-element.63), channel_id=1, source_target_pairs={{24,0},{28,4},{16,8},{20,12},{8,16},{12,20},{0,24},{4,28},{25,1},{... | collective-permute-start | bytes 331784 | tf_op jit(solution)/shard_map/ppermute | solution.py:331
  21.3 6.7 %collective-permute-start.10 = (bf16[2,36,768]{2,1,0:T(8,128)(2,1)S(1)}, bf16[2,36,768]{2,1,0:T(8,128)(2,1)S(1)}, u32[]{:S(2)}, u32[]{:S(2)}) collective-permute-start(bf16[2,36,768]{2,1,0:T(8,128)(2,1)S(1)} %get-tuple-element.55), channel_id=1, source_target_pairs={{8,0},{12,4},{0,8},{4,12},{24,16},{28,20},{16,24},{20,28},{9,1},{1... | collective-permute-start | bytes 331784 | tf_op jit(solution)/shard_map/ppermute | solution.py:331
  21.8 6.2 %collective-permute-start.11 = (bf16[2,36,768]{2,1,0:T(8,128)(2,1)S(1)}, bf16[2,36,768]{2,1,0:T(8,128)(2,1)S(1)}, u32[]{:S(2)}, u32[]{:S(2)}) collective-permute-start(bf16[2,36,768]{2,1,0:T(8,128)(2,1)S(1)} %get-tuple-element.56), channel_id=1, source_target_pairs={{16,0},{20,4},{24,8},{28,12},{0,16},{4,20},{8,24},{12,28},{17,1},{... | collective-permute-start | bytes 331784 | tf_op jit(solution)/shard_map/ppermute | solution.py:331

commit v6 on v5

--- a/solution.py
+++ b/solution.py
@@ -305,13 +305,11 @@
     block_total = lax.axis_size("qblk")
     swap = [(index, index ^ 1) for index in range(frame_total)]
     own_block, near_query = load(key_tokens, value_tokens, query_tokens)
-    blocks = [(own_block,)] + [(lax.ppermute(own_block, "qblk", there),) for there, _ in rounds(block_total)]
+    steps = [there for there, _ in rounds(block_total)]
+    order = steps[1:] + steps[:1]
+    blocks = [(own_block,)] + [(lax.ppermute(own_block, "qblk", there),) for there in order]
     paths = list(chip_rounds(frame_total))
-    ready_query = lax.optimization_barrier((near_query, blocks[1 % len(blocks)][0]))[0]
-    queries = [near_query] + [
-        lax.ppermute(ready_query if step == 0 else near_query, "frame", there)
-        for step, (there, _) in enumerate(paths)
-    ]
+    queries = [near_query] + [lax.ppermute(near_query, "frame", there) for there, _ in paths]
     w_query, w_key, w_value = fetch((w_query, w_key, w_value))
     *queries, w_query, w_key, w_value = lax.optimization_barrier((*queries, w_query, w_key, w_value))
     turned = [

time: 29.8 us -> 29.7 us (level)
  starting transfers between devices: 14 us -> 13.2 us
  waiting for transfers between devices: 7.36 us -> 8.07 us
    ppermute x3, starting transfers between devices: 5.68 us -> 4.17 us  [per_device(): lax.ppermute(own_block, 'qblk', there)]
    ppermute x3, starting transfers between devices: 3.77 us -> 5 us  [per_device(): lax.ppermute(near_query, 'frame', there)]
    ppermute x3, waiting for transfers between devices: 1.6 us -> 2.63 us  [per_device(): lax.ppermute(near_query, 'frame', there)]
    ppermute x4, starting transfers between devices: 1.02 us -> 0.52 us  [per_device(): lax.ppermute(array, 'frame', swap)]
    ppermute x3, waiting for transfers between devices: 1.81 us -> 1.49 us  [per_device(): lax.ppermute(own_block, 'qblk', there)]
  transfers between devices with their start and end apart: 13 -> 13, of which waited for: 5 -> 7; matrix products, arithmetic and copies ran while one was open for 0% -> 0% of each run, Pallas kernels for 16% -> 16%
where the time goes in v6:
time: 29.7 us; the launch traced here: 29.5 us
  starting transfers between devices  13.2 us (44%)
  Pallas kernels  8.14 us (27%)
  waiting for transfers between devices  8.07 us (27%)
    ppermute x3, starting transfers between devices, per_device(): lax.ppermute(near_query, 'frame', there)  5 us
    ppermute x3, starting transfers between devices, per_device(): lax.ppermute(own_block, 'qblk', there)  4.17 us
    ppermute x3, waiting for transfers between devices, per_device(): lax.ppermute(block, 'frame', back)  3.75 us
    ppermute x3, starting transfers between devices, per_device(): lax.ppermute(block, 'frame', back)  3.55 us
    pallas_call x3, Pallas kernels, mix_call(): pl.pallas_call(functools.partial(kernel, width // HEADS), out_shape=out_s...  3.36 us
    ppermute x3, waiting for transfers between devices, per_device(): lax.ppermute(near_query, 'frame', there)  2.63 us
    pallas_call x1, Pallas kernels, fetch(): pl.pallas_call(fetch_kernel, out_shape=[pltpu.VMEM(matrix.shape, matrix.d...  2.01 us
    pallas_call x2, Pallas kernels, attention(): pl.pallas_call(kernel, out_shape=[shape] * count + [near((query_total, wi...  1.86 us
  transfers between devices with their start and end apart: 13, of which 7 were waited for; matrix products, arithmetic and copies ran while one was open for 0% of the time, Pallas kernels for 16%

profile of v6, /device:TPU:0, one launch (start us, length us, event | category | flops | bytes accessed | tf_op | source)
XLA Modules:
  0.0 29.5 jit_solution(3804470035593460056)
XLA Ops:
  0.0 0.9 %load.1 = (bf16[2,36,768]{2,1,0:T(8,128)(2,1)S(1)}, bf16[1,36,768]{2,1,0:T(8,128)(2,1)S(1)}) custom-call(bf16[1,36,768]{2,1,0:T(8,128)(2,1)} %key.1, bf16[1,36,768]{2,1,0:T(8,128)(2,1)} %value.1, bf16[1,36,768]{2,1,0:T(8,128)(2,1)} %query.1), custom_call_target="tpu_custom_call" | custom-call | tf_op jit(solution)/shard_map/load/pallas_call | solution.py:77
  0.9 3.0 %collective-permute-start = (bf16[1,36,768]{2,1,0:T(8,128)(2,1)S(1)}, bf16[1,36,768]{2,1,0:T(8,128)(2,1)S(1)}, u32[]{:S(2)}, u32[]{:S(2)}) collective-permute-start(bf16[1,36,768]{2,1,0:T(8,128)(2,1)S(1)} %get-tuple-element.39.refs_0_), channel_id=1, source_target_pairs={{0,8},{4,12},{8,0},{12,4},{16,24},{20,28},{24,16},{28,20},{1,9},{5... | collective-permute-start | bytes 165896 | tf_op jit(solution)/shard_map/ppermute | solution.py:312
  3.9 2.6 %collective-permute-start.3 = (bf16[2,36,768]{2,1,0:T(8,128)(2,1)S(1)}, bf16[2,36,768]{2,1,0:T(8,128)(2,1)S(1)}, u32[]{:S(2)}, u32[]{:S(2)}) collective-permute-start(bf16[2,36,768]{2,1,0:T(8,128)(2,1)S(1)} %get-tuple-element.45.refs_4_), channel_id=1, source_target_pairs={{0,2},{1,3},{2,0},{3,1},{4,6},{5,7},{6,4},{7,5},{8,10},{9,11},{10,... | collective-permute-start | bytes 331784 | tf_op jit(solution)/shard_map/ppermute | solution.py:310
  6.5 1.3 %collective-permute-start.4 = (bf16[2,36,768]{2,1,0:T(8,128)(2,1)S(1)}, bf16[2,36,768]{2,1,0:T(8,128)(2,1)S(1)}, u32[]{:S(2)}, u32[]{:S(2)}) collective-permute-start(bf16[2,36,768]{2,1,0:T(8,128)(2,1)S(1)} %get-tuple-element.45.refs_4_), channel_id=1, source_target_pairs={{0,3},{1,2},{2,1},{3,0},{4,7},{5,6},{6,5},{7,4},{8,11},{9,10},{10,... | collective-permute-start | bytes 331784 | tf_op jit(solution)/shard_map/ppermute | solution.py:310
  7.9 0.2 collective-permute-start.5
  8.1 1.5 %collective-permute-start.1 = (bf16[1,36,768]{2,1,0:T(8,128)(2,1)S(1)}, bf16[1,36,768]{2,1,0:T(8,128)(2,1)S(1)}, u32[]{:S(2)}, u32[]{:S(2)}) collective-permute-start(bf16[1,36,768]{2,1,0:T(8,128)(2,1)S(1)} %get-tuple-element.39.refs_0_), channel_id=1, source_target_pairs={{0,16},{4,20},{8,24},{12,28},{16,0},{20,4},{24,8},{28,12},{1,17},{... | collective-permute-start | bytes 165896 | tf_op jit(solution)/shard_map/ppermute | solution.py:312
  9.6 0.5 %collective-permute-start.2 = (bf16[1,36,768]{2,1,0:T(8,128)(2,1)S(1)}, bf16[1,36,768]{2,1,0:T(8,128)(2,1)S(1)}, u32[]{:S(2)}, u32[]{:S(2)}) collective-permute-start(bf16[1,36,768]{2,1,0:T(8,128)(2,1)S(1)} %get-tuple-element.39.refs_0_), channel_id=1, source_target_pairs={{0,24},{4,28},{8,16},{12,20},{16,8},{20,12},{24,0},{28,4},{1,25},{... | collective-permute-start | bytes 165896 | tf_op jit(solution)/shard_map/ppermute | solution.py:312
  10.1 2.0 %fetch.1 = (bf16[768,768]{1,0:T(8,128)(2,1)S(1)}, bf16[768,768]{1,0:T(8,128)(2,1)S(1)}, bf16[768,768]{1,0:T(8,128)(2,1)S(1)}) custom-call(bf16[768,768]{1,0:T(8,128)(2,1)} %refs_0_.1, bf16[768,768]{1,0:T(8,128)(2,1)} %refs_1_.1, bf16[768,768]{1,0:T(8,128)(2,1)} %refs_2_.1), custom_call_target="tpu_custom_call" | custom-call | bytes 6291456 | tf_op jit(solution)/shard_map/fetch/pallas_call | solution.py:104
  12.1 0.9 %collective-permute-done.1.refs_2_ = bf16[1,36,768]{2,1,0:T(8,128)(2,1)S(1)} collective-permute-done((bf16[1,36,768]{2,1,0:T(8,128)(2,1)S(1)}, bf16[1,36,768]{2,1,0:T(8,128)(2,1)S(1)}, u32[]{:S(2)}, u32[]{:S(2)}) %collective-permute-start.1) | collective-permute-done | bytes 55328 | tf_op jit(solution)/shard_map/ppermute | solution.py:312
  13.0 1.8 %collective-permute-done.2.refs_3_ = bf16[1,36,768]{2,1,0:T(8,128)(2,1)S(1)} collective-permute-done((bf16[1,36,768]{2,1,0:T(8,128)(2,1)S(1)}, bf16[1,36,768]{2,1,0:T(8,128)(2,1)S(1)}, u32[]{:S(2)}, u32[]{:S(2)}) %collective-permute-start.2) | collective-permute-done | bytes 55328 | tf_op jit(solution)/shard_map/ppermute | solution.py:312
  14.7 1.3 %collective-permute-done.3.refs_5_ = bf16[2,36,768]{2,1,0:T(8,128)(2,1)S(1)} collective-permute-done((bf16[2,36,768]{2,1,0:T(8,128)(2,1)S(1)}, bf16[2,36,768]{2,1,0:T(8,128)(2,1)S(1)}, u32[]{:S(2)}, u32[]{:S(2)}) %collective-permute-start.3) | collective-permute-done | bytes 110624 | tf_op jit(solution)/shard_map/ppermute | solution.py:310
  16.0 0.2 collective-permute-done.5.refs_7_
  16.2 0.3 %collective-permute-start.8 = (bf16[2,36,768]{2,1,0:T(8,128)(2,1)S(1)}, bf16[2,36,768]{2,1,0:T(8,128)(2,1)S(1)}, u32[]{:S(2)}, u32[]{:S(2)}) collective-permute-start(bf16[2,36,768]{2,1,0:T(8,128)(2,1)S(1)} %collective-permute-done.4.refs_6_), channel_id=1, source_target_pairs={{0,4},{4,0},{8,12},{12,8},{16,20},{20,16},{24,28},{28,24},{1,5},{5... | collective-permute-start | bytes 331784 | tf_op jit(solution)/shard_map/ppermute | solution.py:321
  16.6 0.2 collective-permute-start.9
  16.7 0.9 %attention.2 = (bf16[1,36,768]{2,1,0:T(8,128)(2,1)S(1)}, bf16[1,36,768]{2,1,0:T(8,128)(2,1)S(1)}, bf16[1,36,768]{2,1,0:T(8,128)(2,1)S(1)}, bf16[1,36,768]{2,1,0:T(8,128)(2,1)S(1)}, bf16[144,768]{1,0:T(8,128)(2,1)S(1)}) custom-call(bf16[1,36,768]{2,1,0:T(8,128)(2,1)S(1)} %get-tuple-element.39.refs_0_, bf16[1,36,768]{2,1,0:T(8,128)(2,1)S(1)} %collective-permute-done.refs_1_, ...), custom_call_target="tpu_custom_call" | custom-call | flops 63700992 | bytes 1048576 | tf_op jit(solution)/shard_map/attention/pallas_call | solution.py:151
  17.9 0.9 %attention.3 = (bf16[2,36,768]{2,1,0:T(8,128)(2,1)S(1)}, bf16[2,36,768]{2,1,0:T(8,128)(2,1)S(1)}, bf16[2,36,768]{2,1,0:T(8,128)(2,1)S(1)}, bf16[2,36,768]{2,1,0:T(8,128)(2,1)S(1)}) custom-call(bf16[144,768]{1,0:T(8,128)(2,1)S(1)} %get-tuple-element.44.refs_0_, bf16[2,36,768]{2,1,0:T(8,128)(2,1)S(1)} %collective-permute-done.6.refs_1_, ...), custom_call_target="tpu_custom_call" | custom-call | flops 63700992 | bytes 1048576 | tf_op jit(solution)/shard_map/attention/pallas_call | solution.py:151
  18.8 1.6 %collective-permute-start.12 = (bf16[2,36,768]{2,1,0:T(8,128)(2,1)S(1)}, bf16[2,36,768]{2,1,0:T(8,128)(2,1)S(1)}, u32[]{:S(2)}, u32[]{:S(2)}) collective-permute-start(bf16[2,36,768]{2,1,0:T(8,128)(2,1)S(1)} %get-tuple-element.61), channel_id=1, source_target_pairs={{24,0},{28,4},{16,8},{20,12},{8,16},{12,20},{0,24},{4,28},{25,1},{... | collective-permute-start | bytes 331784 | tf_op jit(solution)/shard_map/ppermute | solution.py:329
  20.4 1.5 %collective-permute-start.10 = (bf16[2,36,768]{2,1,0:T(8,128)(2,1)S(1)}, bf16[2,36,768]{2,1,0:T(8,128)(2,1)S(1)}, u32[]{:S(2)}, u32[]{:S(2)}) collective-permute-start(bf16[2,36,768]{2,1,0:T(8,128)(2,1)S(1)} %get-tuple-element.53), channel_id=1, source_target_pairs={{8,0},{12,4},{0,8},{4,12},{24,16},{28,20},{16,24},{20,28},{9,1},{1... | collective-permute-start | bytes 331784 | tf_op jit(solution)/shard_map/ppermute | solution.py:329
  21.9 0.5 %collective-permute-start.11 = (bf16[2,36,768]{2,1,0:T(8,128)(2,1)S(1)}, bf16[2,36,768]{2,1,0:T(8,128)(2,1)S(1)}, u32[]{:S(2)}, u32[]{:S(2)}) collective-permute-start(bf16[2,36,768]{2,1,0:T(8,128)(2,1)S(1)} %get-tuple-element.54), channel_id=1, source_target_pairs={{16,0},{20,4},{24,8},{28,12},{0,16},{4,20},{8,24},{12,28},{17,1},{... | collective-permute-start | bytes 331784 | tf_op jit(solution)/shard_map/ppermute | solution.py:329
  22.4 0.9 %mix_own.1 = (f32[40,768]{1,0:T(8,128)S(1)}, f32[80,128]{1,0:T(8,128)S(1)}, f32[80,768]{1,0:T(8,128)S(1)}) custom-call(bf16[2,36,768]{2,1,0:T(8,128)(2,1)S(1)} %get-tuple-element.55.block, bf16[768,768]{1,0:T(8,128)(2,1)S(1)} %get-tuple-element.56.w_query, bf16[768,768]{1,0:T(8,128)(2,1)S(1)} %get-tuple-element.57.w_key.refs_3_, ...), custom_call_target="tpu_custom_call" | custom-call | flops 169869312 | bytes 4194304 | tf_op jit(solution)/shard_map/mix_own/pallas_call | solution.py:244
  23.3 2.6 %collective-permute-done.12.block = bf16[2,36,768]{2,1,0:T(8,128)(2,1)S(1)} collective-permute-done((bf16[2,36,768]{2,1,0:T(8,128)(2,1)S(1)}, bf16[2,36,768]{2,1,0:T(8,128)(2,1)S(1)}, u32[]{:S(2)}, u32[]{:S(2)}) %collective-permute-start.12) | collective-permute-done | bytes 110624 | tf_op jit(solution)/shard_map/ppermute | solution.py:329
  26.0 0.8 %mix_part.1 = (f32[80,128]{1,0:T(8,128)S(1)}, f32[80,768]{1,0:T(8,128)S(1)}) custom-call(bf16[2,36,768]{2,1,0:T(8,128)(2,1)S(1)} %collective-permute-done.12.block, f32[40,768]{1,0:T(8,128)S(1)} %get-tuple-element.59.query.refs_2_, bf16[768,768]{1,0:T(8,128)(2,1)S(1)} %get-tuple-element.57.w_key.refs_3_, bf16[768,768]{1,0:T(8,128)(2,1)S(1)} %get-tuple-element.58.w_value.refs_4_), custom_call_target="tpu_custom_call" | custom-call | flops 169869312 | bytes 4194304 | tf_op jit(solution)/shard_map/mix_part/pallas_call | solution.py:244
  26.8 1.1 %collective-permute-done.10.refs_0_ = bf16[2,36,768]{2,1,0:T(8,128)(2,1)S(1)} collective-permute-done((bf16[2,36,768]{2,1,0:T(8,128)(2,1)S(1)}, bf16[2,36,768]{2,1,0:T(8,128)(2,1)S(1)}, u32[]{:S(2)}, u32[]{:S(2)}) %collective-permute-start.10) | collective-permute-done | bytes 110624 | tf_op jit(solution)/shard_map/ppermute | solution.py:329
  27.9 1.6 %mix_last.1 = bf16[1,36,768]{2,1,0:T(8,128)(2,1)} custom-call(bf16[2,36,768]{2,1,0:T(8,128)(2,1)S(1)} %collective-permute-done.10.refs_0_, bf16[2,36,768]{2,1,0:T(8,128)(2,1)S(1)} %collective-permute-done.11.refs_1_, f32[40,768]{1,0:T(8,128)S(1)} %get-tuple-element.59.query.refs_2_, bf16[768,768]{1,0:T(8,128)(2,1)S(1)} %get-tuple-element.57.w_key.refs_3_, ...), custom_call_target="tpu_custom_call" | custom-call | flops 339738624 | bytes 4194304 | tf_op jit(solution)/shard_map/mix_last/pallas_call | solution.py:244
  (9 shorter events, 0.2 us)
Async XLA Ops:
  0.9 8.7 %collective-permute-start = (bf16[1,36,768]{2,1,0:T(8,128)(2,1)S(1)}, bf16[1,36,768]{2,1,0:T(8,128)(2,1)S(1)}, u32[]{:S(2)}, u32[]{:S(2)}) collective-permute-start(bf16[1,36,768]{2,1,0:T(8,128)(2,1)S(1)} %get-tuple-element.39.refs_0_), channel_id=1, source_target_pairs={{0,8},{4,12},{8,0},{12,4},{16,24},{20,28},{24,16},{28,20},{1,9},{5... | collective-permute-start | bytes 165896 | tf_op jit(solution)/shard_map/ppermute | solution.py:312
  3.9 12.1 %collective-permute-start.3 = (bf16[2,36,768]{2,1,0:T(8,128)(2,1)S(1)}, bf16[2,36,768]{2,1,0:T(8,128)(2,1)S(1)}, u32[]{:S(2)}, u32[]{:S(2)}) collective-permute-start(bf16[2,36,768]{2,1,0:T(8,128)(2,1)S(1)} %get-tuple-element.45.refs_4_), channel_id=1, source_target_pairs={{0,2},{1,3},{2,0},{3,1},{4,6},{5,7},{6,4},{7,5},{8,10},{9,11},{10,... | collective-permute-start | bytes 331784 | tf_op jit(solution)/shard_map/ppermute | solution.py:310
  6.5 9.5 %collective-permute-start.4 = (bf16[2,36,768]{2,1,0:T(8,128)(2,1)S(1)}, bf16[2,36,768]{2,1,0:T(8,128)(2,1)S(1)}, u32[]{:S(2)}, u32[]{:S(2)}) collective-permute-start(bf16[2,36,768]{2,1,0:T(8,128)(2,1)S(1)} %get-tuple-element.45.refs_4_), channel_id=1, source_target_pairs={{0,3},{1,2},{2,1},{3,0},{4,7},{5,6},{6,5},{7,4},{8,11},{9,10},{10,... | collective-permute-start | bytes 331784 | tf_op jit(solution)/shard_map/ppermute | solution.py:310
  7.9 8.4 %collective-permute-start.5 = (bf16[2,36,768]{2,1,0:T(8,128)(2,1)S(1)}, bf16[2,36,768]{2,1,0:T(8,128)(2,1)S(1)}, u32[]{:S(2)}, u32[]{:S(2)}) collective-permute-start(bf16[2,36,768]{2,1,0:T(8,128)(2,1)S(1)} %get-tuple-element.45.refs_4_), channel_id=1, source_target_pairs={{0,1},{1,0},{2,3},{3,2},{4,5},{5,4},{6,7},{7,6},{8,9},{9,8},{10,11... | collective-permute-start | bytes 331784 | tf_op jit(solution)/shard_map/ppermute | solution.py:310
  8.1 4.9 %collective-permute-start.1 = (bf16[1,36,768]{2,1,0:T(8,128)(2,1)S(1)}, bf16[1,36,768]{2,1,0:T(8,128)(2,1)S(1)}, u32[]{:S(2)}, u32[]{:S(2)}) collective-permute-start(bf16[1,36,768]{2,1,0:T(8,128)(2,1)S(1)} %get-tuple-element.39.refs_0_), channel_id=1, source_target_pairs={{0,16},{4,20},{8,24},{12,28},{16,0},{20,4},{24,8},{28,12},{1,17},{... | collective-permute-start | bytes 165896 | tf_op jit(solution)/shard_map/ppermute | solution.py:312
  9.6 5.1 %collective-permute-start.2 = (bf16[1,36,768]{2,1,0:T(8,128)(2,1)S(1)}, bf16[1,36,768]{2,1,0:T(8,128)(2,1)S(1)}, u32[]{:S(2)}, u32[]{:S(2)}) collective-permute-start(bf16[1,36,768]{2,1,0:T(8,128)(2,1)S(1)} %get-tuple-element.39.refs_0_), channel_id=1, source_target_pairs={{0,24},{4,28},{8,16},{12,20},{16,8},{20,12},{24,0},{28,4},{1,25},{... | collective-permute-start | bytes 165896 | tf_op jit(solution)/shard_map/ppermute | solution.py:312
  14.7 2.9 %collective-permute-start.6 = (bf16[2,36,768]{2,1,0:T(8,128)(2,1)S(1)}, bf16[2,36,768]{2,1,0:T(8,128)(2,1)S(1)}, u32[]{:S(2)}, u32[]{:S(2)}) collective-permute-start(bf16[2,36,768]{2,1,0:T(8,128)(2,1)S(1)} %get-tuple-element.45.refs_4_), channel_id=1, source_target_pairs={{0,4},{4,0},{8,12},{12,8},{16,20},{20,16},{24,28},{28,24},{1,5},{5... | collective-permute-start | bytes 331784 | tf_op jit(solution)/shard_map/ppermute | solution.py:321
  16.0 1.7 %collective-permute-start.7 = (bf16[2,36,768]{2,1,0:T(8,128)(2,1)S(1)}, bf16[2,36,768]{2,1,0:T(8,128)(2,1)S(1)}, u32[]{:S(2)}, u32[]{:S(2)}) collective-permute-start(bf16[2,36,768]{2,1,0:T(8,128)(2,1)S(1)} %collective-permute-done.3.refs_5_), channel_id=1, source_target_pairs={{0,4},{4,0},{8,12},{12,8},{16,20},{20,16},{24,28},{28,24},{1,5},{5... | collective-permute-start | bytes 331784 | tf_op jit(solution)/shard_map/ppermute | solution.py:321
  16.2 1.5 %collective-permute-start.8 = (bf16[2,36,768]{2,1,0:T(8,128)(2,1)S(1)}, bf16[2,36,768]{2,1,0:T(8,128)(2,1)S(1)}, u32[]{:S(2)}, u32[]{:S(2)}) collective-permute-start(bf16[2,36,768]{2,1,0:T(8,128)(2,1)S(1)} %collective-permute-done.4.refs_6_), channel_id=1, source_target_pairs={{0,4},{4,0},{8,12},{12,8},{16,20},{20,16},{24,28},{28,24},{1,5},{5... | collective-permute-start | bytes 331784 | tf_op jit(solution)/shard_map/ppermute | solution.py:321
  16.6 1.3 %collective-permute-start.9 = (bf16[2,36,768]{2,1,0:T(8,128)(2,1)S(1)}, bf16[2,36,768]{2,1,0:T(8,128)(2,1)S(1)}, u32[]{:S(2)}, u32[]{:S(2)}) collective-permute-start(bf16[2,36,768]{2,1,0:T(8,128)(2,1)S(1)} %collective-permute-done.5.refs_7_), channel_id=1, source_target_pairs={{0,4},{4,0},{8,12},{12,8},{16,20},{20,16},{24,28},{28,24},{1,5},{5... | collective-permute-start | bytes 331784 | tf_op jit(solution)/shard_map/ppermute | solution.py:321
  18.8 7.1 %collective-permute-start.12 = (bf16[2,36,768]{2,1,0:T(8,128)(2,1)S(1)}, bf16[2,36,768]{2,1,0:T(8,128)(2,1)S(1)}, u32[]{:S(2)}, u32[]{:S(2)}) collective-permute-start(bf16[2,36,768]{2,1,0:T(8,128)(2,1)S(1)} %get-tuple-element.61), channel_id=1, source_target_pairs={{24,0},{28,4},{16,8},{20,12},{8,16},{12,20},{0,24},{4,28},{25,1},{... | collective-permute-start | bytes 331784 | tf_op jit(solution)/shard_map/ppermute | solution.py:329
  20.4 7.5 %collective-permute-start.10 = (bf16[2,36,768]{2,1,0:T(8,128)(2,1)S(1)}, bf16[2,36,768]{2,1,0:T(8,128)(2,1)S(1)}, u32[]{:S(2)}, u32[]{:S(2)}) collective-permute-start(bf16[2,36,768]{2,1,0:T(8,128)(2,1)S(1)} %get-tuple-element.53), channel_id=1, source_target_pairs={{8,0},{12,4},{0,8},{4,12},{24,16},{28,20},{16,24},{20,28},{9,1},{1... | collective-permute-start | bytes 331784 | tf_op jit(solution)/shard_map/ppermute | solution.py:329
  21.9 6.0 %collective-permute-start.11 = (bf16[2,36,768]{2,1,0:T(8,128)(2,1)S(1)}, bf16[2,36,768]{2,1,0:T(8,128)(2,1)S(1)}, u32[]{:S(2)}, u32[]{:S(2)}) collective-permute-start(bf16[2,36,768]{2,1,0:T(8,128)(2,1)S(1)} %get-tuple-element.54), channel_id=1, source_target_pairs={{16,0},{20,4},{24,8},{28,12},{0,16},{4,20},{8,24},{12,28},{17,1},{... | collective-permute-start | bytes 331784 | tf_op jit(solution)/shard_map/ppermute | solution.py:329

commit v7 on v6

--- a/solution.py
+++ b/solution.py
@@ -33,6 +33,12 @@
         if gap:
             stage[pl.ds(index * pitch + rows, gap), :] = jnp.zeros((gap, stage.shape[1]), jnp.float32)
     return stage[...].astype(jnp.bfloat16)
+
+
+def halves(pair, apart):
+    rows = pair.shape[0] // 2
+    apart[...] = pair[...].astype(jnp.float32)
+    return [apart[pl.ds(at, rows), :] for at in (0, rows)]
 
 
 def attend(query, key, value, key_count, head_width, out):
@@ -61,8 +67,8 @@
         out[:, cut] = mine
 
 
-def load_kernel(key, value, query, pair, near_query, sems):
-    targets = (pair.at[0], pair.at[1], near_query.at[0])
+def load_kernel(key, value, query, pair, near_query, near_key, near_value, apart, sems):
+    targets = (near_key, near_value, near_query.at[0])
     copies = [
         pltpu.make_async_copy(source.at[0], target, sems.at[index])
         for index, (source, target) in enumerate(zip((key, value, query), targets))
@@ -71,18 +77,22 @@
         copy.start()
     for copy in copies:
         copy.wait()
+    pair[...] = stack_rows([near_key[...], near_value[...]], apart, near_key.shape[0])
 
 
 def load(key, value, query):
+    _, rows, width = key.shape
     return pl.pallas_call(
         load_kernel,
-        out_shape=[
-            pltpu.VMEM((2,) + key.shape[1:], key.dtype),
-            pltpu.VMEM(query.shape, query.dtype),
-        ],
+        out_shape=[near((2 * rows, width), key.dtype), near(query.shape, query.dtype)],
         in_specs=[FAR] * 3,
         out_specs=[VMEM] * 2,
-        scratch_shapes=[pltpu.SemaphoreType.DMA((3,))],
+        scratch_shapes=[
+            near((rows, width), key.dtype),
+            near((rows, width), key.dtype),
+            near((2 * rows, width)),
+            pltpu.SemaphoreType.DMA((3,)),
+        ],
         name="load",
     )(far(key), far(value), far(query))
 
@@ -113,15 +123,11 @@
     )(*map(far, weights))
 
 
-def attention_kernel(head_width, query_count, earlier_count, forms, *refs):
+def attention_kernel(head_width, query_count, earlier_count, block_count, *refs):
     queries, refs = refs[:query_count], refs[query_count:]
-    keys, values = [], []
-    for form in forms:
-        keys.append(refs[0].at[0])
-        values.append(refs[form - 1].at[2 - form])
-        refs = refs[form:]
-    *refs, key_stage, value_stage, query_stage = refs
-    rows = keys[0].shape[-2]
+    blocks, refs = refs[:block_count], refs[block_count:]
+    *refs, key_stage, value_stage, query_stage, apart = refs
+    rows = blocks[0].shape[0] // 2
     if earlier_count:
         earlier, outs = refs[:earlier_count], refs[earlier_count:]
         query = queries[0][...]
@@ -129,35 +135,40 @@
         earlier, (*outs, stacked) = (), refs
         query = stack_rows([ref[0] for ref in queries], query_stage, rows)
         stacked[...] = query
-    key = stack_rows([ref[...] for ref in keys], key_stage, rows)
-    value = stack_rows([ref[...] for ref in values], value_stage, rows)
-    attend(query, key, value, len(keys) * rows, head_width, query_stage)
+    keys, values = zip(*[halves(ref, apart) for ref in blocks])
+    key = stack_rows(keys, key_stage, rows)
+    value = stack_rows(values, value_stage, rows)
+    attend(query, key, value, block_count * rows, head_width, query_stage)
     for index, out in enumerate(outs):
-        out[out.shape[0] - 1] = query_stage[pl.ds(index * rows, rows), :].astype(out.dtype)
-    for out, ref in zip(outs, earlier):
-        out[0] = ref[0]
+        mine = query_stage[pl.ds(index * rows, rows), :]
+        if earlier:
+            out[...] = stack_rows([earlier[index][0], mine], apart, rows)
+        else:
+            out[0] = mine.astype(out.dtype)
 
 
 def attention(queries, blocks, earlier=()):
-    _, rows, width = blocks[0][0].shape
+    width = blocks[0].shape[1]
+    rows = blocks[0].shape[0] // 2
     count = len(earlier) or len(queries)
     query_total, key_total = ceil_to(count * rows, 16), ceil_to(len(blocks) * rows, 16)
     flops = 4 * count * rows * len(blocks) * rows * width
-    shape = jax.ShapeDtypeStruct((2 if earlier else 1, rows, width), jnp.bfloat16)
+    shape = jax.ShapeDtypeStruct((2 * rows, width) if earlier else (1, rows, width), jnp.bfloat16)
     first = not earlier
     kernel = functools.partial(
-        attention_kernel, width // HEADS, len(queries), len(earlier), [len(block) for block in blocks]
+        attention_kernel, width // HEADS, len(queries), len(earlier), len(blocks)
     )
     return pl.pallas_call(
         kernel,
         out_shape=[shape] * count + [near((query_total, width), jnp.bfloat16)] * first,
-        in_specs=[VMEM] * (len(queries) + sum(map(len, blocks)) + len(earlier)),
+        in_specs=[VMEM] * (len(queries) + len(blocks) + len(earlier)),
         out_specs=[VMEM] * (count + first),
-        scratch_shapes=[near((key_total, width))] * 2 + [near((query_total, width))],
+        scratch_shapes=[near((key_total, width))] * 2
+        + [near((query_total, width)), near((2 * rows, width))],
         compiler_params=pltpu.CompilerParams(vmem_limit_bytes=48 << 20),
         cost_estimate=pl.CostEstimate(flops=flops, bytes_accessed=1 << 20, transcendentals=0),
         name="attention",
-    )(*queries, *(array for block in blocks for array in block), *earlier)
+    )(*queries, *blocks, *earlier)
 
 
 def head_members(width, head_width):
@@ -190,29 +201,30 @@
     return scores * (1.0 / math.sqrt(head_width))
 
 
-def stack_pooled(ref, stage):
-    return stack_rows([ref[index] for index in range(ref.shape[0])], stage, ceil_to(ref.shape[1], 8))
-
-
-def own_kernel(head_width, block, w_query, w_key, w_value, query, scores, values, stage):
-    pooled = stack_pooled(block, stage)
-    rows, pitch = block.shape[1], query.shape[0]
+def stack_pooled(refs, stage, apart, pitch):
+    return stack_rows([half for ref in refs for half in halves(ref, apart)], stage, pitch)
+
+
+def own_kernel(head_width, block, w_query, w_key, w_value, query, scores, values, stage, apart):
+    rows, pitch = block.shape[0] // 2, query.shape[0]
+    pooled = stack_pooled([block], stage, apart, pitch)
     query[...] = project(pooled[: ceil_to(rows, 16)], w_query)[:pitch]
     scores[...] = score(query[...], pooled, w_key, head_width)
     values[...] = project(pooled, w_value)
 
 
-def part_kernel(head_width, block, query, w_key, w_value, scores, values, stage):
-    pooled = stack_pooled(block, stage)
+def part_kernel(head_width, block, query, w_key, w_value, scores, values, stage, apart):
+    pooled = stack_pooled([block], stage, apart, query.shape[0])
     scores[...] = score(query[...], pooled, w_key, head_width)
     values[...] = project(pooled, w_value)
 
 
 def last_kernel(head_width, earlier, count, *refs):
     blocks, (query, w_key, w_value), refs = refs[:count], refs[count : count + 3], refs[count + 3 :]
-    score_refs, value_refs, (out, stage) = refs[:earlier], refs[earlier : 2 * earlier], refs[-2:]
+    score_refs, value_refs = refs[:earlier], refs[earlier : 2 * earlier]
+    out, stage, apart = refs[-3:]
     pitch, width = query.shape
-    pooled = stack_rows([ref[index] for ref in blocks for index in range(ref.shape[0])], stage, pitch)
+    pooled = stack_pooled(blocks, stage, apart, pitch)
     score_parts = [ref[...] for ref in score_refs] + [score(query[...], pooled, w_key, head_width)]
     value_parts = [ref[...] for ref in value_refs] + [project(pooled, w_value)]
     places = [
@@ -231,7 +243,7 @@
             for index, (part, at) in enumerate(places)
         ],
     )
-    out[0] = mixed[: blocks[0].shape[1]].astype(jnp.bfloat16)
+    out[0] = mixed[: blocks[0].shape[0] // 2].astype(jnp.bfloat16)
 
 
 def near(shape, dtype=jnp.float32):
@@ -239,14 +251,15 @@
 
 
 def mix_call(kernel, blocks, out_shape, operands, name):
-    _, rows, width = blocks[0].shape
-    count = sum(block.shape[0] for block in blocks)
+    width = blocks[0].shape[1]
+    rows = blocks[0].shape[0] // 2
+    count = 2 * len(blocks)
     return pl.pallas_call(
         functools.partial(kernel, width // HEADS),
         out_shape=out_shape,
         in_specs=[VMEM] * (len(blocks) + len(operands)),
         out_specs=jax.tree.map(lambda _: VMEM, out_shape),
-        scratch_shapes=[near((count * ceil_to(rows, 8), width))],
+        scratch_shapes=[near((count * ceil_to(rows, 8), width)), near((2 * rows, width))],
         compiler_params=pltpu.CompilerParams(vmem_limit_bytes=32 << 20),
         cost_estimate=pl.CostEstimate(
             flops=4 * count * rows * width * width, bytes_accessed=4 << 20, transcendentals=0
@@ -256,14 +269,13 @@
 
 
 def part_shapes(block):
-    count, rows, width = block.shape
-    total = count * ceil_to(rows, 8)
+    width = block.shape[1]
+    total = 2 * ceil_to(block.shape[0] // 2, 8)
     return [near((total, LANES)), near((total, width))]
 
 
 def mix_own(block, weights):
-    _, rows, width = block.shape
-    shapes = [near((ceil_to(rows, 8), width)), *part_shapes(block)]
+    shapes = [near((ceil_to(block.shape[0] // 2, 8), block.shape[1])), *part_shapes(block)]
     query, *part = mix_call(own_kernel, [block], shapes, weights, "mix_own")
     return query, tuple(part)
 
@@ -277,7 +289,7 @@
     return mix_call(
         lambda head_width, *refs: last_kernel(head_width, len(parts), len(blocks), *refs),
         blocks,
-        jax.ShapeDtypeStruct((1,) + blocks[0].shape[1:], blocks[0].dtype),
+        jax.ShapeDtypeStruct((1, blocks[0].shape[0] // 2, blocks[0].shape[1]), blocks[0].dtype),
         (query, w_key, w_value, *scores, *values),
         "mix_last",
     )
@@ -307,7 +319,7 @@
     own_block, near_query = load(key_tokens, value_tokens, query_tokens)
     steps = [there for there, _ in rounds(block_total)]
     order = steps[1:] + steps[:1]
-    blocks = [(own_block,)] + [(lax.ppermute(own_block, "qblk", there),) for there in order]
+    blocks = [own_block] + [lax.ppermute(own_block, "qblk", there) for there in order]
     paths = list(chip_rounds(frame_total))
     queries = [near_query] + [lax.ppermute(near_query, "frame", there) for there, _ in paths]
     w_query, w_key, w_value = fetch((w_query, w_key, w_value))
@@ -317,9 +329,7 @@
         for index, block in enumerate(blocks)
     ]
     turned[:2] = [lax.optimization_barrier((block, *queries))[0] for block in blocks[:2]]
-    other_blocks = [
-        tuple(lax.ppermute(array, "frame", swap) for array in block) for block in turned
-    ]
+    other_blocks = [lax.ppermute(block, "frame", swap) for block in turned]
     *own, query = attention(queries, blocks)
     pooled = attention([query], other_blocks, own)
     own_query, part = mix_own(pooled[0], (w_query, w_key, w_value))

time: 29.7 us -> 28.4 us (0.956)
  waiting for transfers between devices: 8.07 us -> 6.64 us
    ppermute x3, waiting for transfers between devices: 1.49 us -> 0.54 us  [per_device(): lax.ppermute(own_block, 'qblk', there)]
    ppermute x3, waiting for transfers between devices: 3.75 us -> 3.22 us  [per_device(): lax.ppermute(block, 'frame', back)]
  transfers between devices with their start and end apart: 13 -> 13, of which waited for: 7 -> 7; matrix products, arithmetic and copies ran while one was open for 0% -> 0% of each run, Pallas kernels for 16% -> 17%
where the time goes in v7:
time: 28.4 us; the launch traced here: 28.2 us
  starting transfers between devices  13.3 us (47%)
  Pallas kernels  8.24 us (29%)
  waiting for transfers between devices  6.64 us (23%)
    ppermute x3, starting transfers between devices, per_device(): lax.ppermute(near_query, 'frame', there)  5 us
    ppermute x3, starting transfers between devices, per_device(): lax.ppermute(own_block, 'qblk', there)  4.17 us
    ppermute x3, starting transfers between devices, per_device(): lax.ppermute(block, 'frame', back)  3.55 us
    pallas_call x3, Pallas kernels, mix_call(): pl.pallas_call(functools.partial(kernel, width // HEADS), out_shape=out_s...  3.37 us
    ppermute x3, waiting for transfers between devices, per_device(): lax.ppermute(block, 'frame', back)  3.22 us
    ppermute x3, waiting for transfers between devices, per_device(): lax.ppermute(near_query, 'frame', there)  2.63 us
    pallas_call x1, Pallas kernels, fetch(): pl.pallas_call(fetch_kernel, out_shape=[pltpu.VMEM(matrix.shape, matrix.d...  2.01 us
    pallas_call x2, Pallas kernels, attention(): pl.pallas_call(kernel, out_shape=[shape] * count + [near((query_total, wi...  1.94 us
  transfers between devices with their start and end apart: 13, of which 7 were waited for; matrix products, arithmetic and copies ran while one was open for 0% of the time, Pallas kernels for 17%

profile of v7, /device:TPU:0, one launch (start us, length us, event | category | flops | bytes accessed | tf_op | source)
XLA Modules:
  0.0 28.2 jit_solution(16672761284586525833)
XLA Ops:
  0.0 0.9 %load.1 = (bf16[72,768]{1,0:T(8,128)(2,1)S(1)}, bf16[1,36,768]{2,1,0:T(8,128)(2,1)S(1)}) custom-call(bf16[1,36,768]{2,1,0:T(8,128)(2,1)} %key.1, bf16[1,36,768]{2,1,0:T(8,128)(2,1)} %value.1, bf16[1,36,768]{2,1,0:T(8,128)(2,1)} %query.1), custom_call_target="tpu_custom_call" | custom-call | tf_op jit(solution)/shard_map/load/pallas_call | solution.py:85
  0.9 3.0 %collective-permute-start = (bf16[1,36,768]{2,1,0:T(8,128)(2,1)S(1)}, bf16[1,36,768]{2,1,0:T(8,128)(2,1)S(1)}, u32[]{:S(2)}, u32[]{:S(2)}) collective-permute-start(bf16[1,36,768]{2,1,0:T(8,128)(2,1)S(1)} %get-tuple-element.39.refs_0_), channel_id=1, source_target_pairs={{0,8},{4,12},{8,0},{12,4},{16,24},{20,28},{24,16},{28,20},{1,9},{5... | collective-permute-start | bytes 165896 | tf_op jit(solution)/shard_map/ppermute | solution.py:324
  3.9 2.6 %collective-permute-start.3 = (bf16[72,768]{1,0:T(8,128)(2,1)S(1)}, bf16[72,768]{1,0:T(8,128)(2,1)S(1)}, u32[]{:S(2)}, u32[]{:S(2)}) collective-permute-start(bf16[72,768]{1,0:T(8,128)(2,1)S(1)} %get-tuple-element.45.refs_4_), channel_id=1, source_target_pairs={{0,2},{1,3},{2,0},{3,1},{4,6},{5,7},{6,4},{7,5},{8,10},{9,11},{10,... | collective-permute-start | bytes 331784 | tf_op jit(solution)/shard_map/ppermute | solution.py:322
  6.5 1.3 %collective-permute-start.4 = (bf16[72,768]{1,0:T(8,128)(2,1)S(1)}, bf16[72,768]{1,0:T(8,128)(2,1)S(1)}, u32[]{:S(2)}, u32[]{:S(2)}) collective-permute-start(bf16[72,768]{1,0:T(8,128)(2,1)S(1)} %get-tuple-element.45.refs_4_), channel_id=1, source_target_pairs={{0,3},{1,2},{2,1},{3,0},{4,7},{5,6},{6,5},{7,4},{8,11},{9,10},{10,... | collective-permute-start | bytes 331784 | tf_op jit(solution)/shard_map/ppermute | solution.py:322
  7.9 0.2 collective-permute-start.5
  8.1 1.5 %collective-permute-start.1 = (bf16[1,36,768]{2,1,0:T(8,128)(2,1)S(1)}, bf16[1,36,768]{2,1,0:T(8,128)(2,1)S(1)}, u32[]{:S(2)}, u32[]{:S(2)}) collective-permute-start(bf16[1,36,768]{2,1,0:T(8,128)(2,1)S(1)} %get-tuple-element.39.refs_0_), channel_id=1, source_target_pairs={{0,16},{4,20},{8,24},{12,28},{16,0},{20,4},{24,8},{28,12},{1,17},{... | collective-permute-start | bytes 165896 | tf_op jit(solution)/shard_map/ppermute | solution.py:324
  9.6 0.5 %collective-permute-start.2 = (bf16[1,36,768]{2,1,0:T(8,128)(2,1)S(1)}, bf16[1,36,768]{2,1,0:T(8,128)(2,1)S(1)}, u32[]{:S(2)}, u32[]{:S(2)}) collective-permute-start(bf16[1,36,768]{2,1,0:T(8,128)(2,1)S(1)} %get-tuple-element.39.refs_0_), channel_id=1, source_target_pairs={{0,24},{4,28},{8,16},{12,20},{16,8},{20,12},{24,0},{28,4},{1,25},{... | collective-permute-start | bytes 165896 | tf_op jit(solution)/shard_map/ppermute | solution.py:324
  10.1 2.0 %fetch.1 = (bf16[768,768]{1,0:T(8,128)(2,1)S(1)}, bf16[768,768]{1,0:T(8,128)(2,1)S(1)}, bf16[768,768]{1,0:T(8,128)(2,1)S(1)}) custom-call(bf16[768,768]{1,0:T(8,128)(2,1)} %refs_0_.1, bf16[768,768]{1,0:T(8,128)(2,1)} %refs_1_.1, bf16[768,768]{1,0:T(8,128)(2,1)} %refs_2_.1), custom_call_target="tpu_custom_call" | custom-call | bytes 6291456 | tf_op jit(solution)/shard_map/fetch/pallas_call | solution.py:114
  12.1 0.9 %collective-permute-done.1.refs_2_ = bf16[1,36,768]{2,1,0:T(8,128)(2,1)S(1)} collective-permute-done((bf16[1,36,768]{2,1,0:T(8,128)(2,1)S(1)}, bf16[1,36,768]{2,1,0:T(8,128)(2,1)S(1)}, u32[]{:S(2)}, u32[]{:S(2)}) %collective-permute-start.1) | collective-permute-done | bytes 55328 | tf_op jit(solution)/shard_map/ppermute | solution.py:324
  13.0 1.8 %collective-permute-done.2.refs_3_ = bf16[1,36,768]{2,1,0:T(8,128)(2,1)S(1)} collective-permute-done((bf16[1,36,768]{2,1,0:T(8,128)(2,1)S(1)}, bf16[1,36,768]{2,1,0:T(8,128)(2,1)S(1)}, u32[]{:S(2)}, u32[]{:S(2)}) %collective-permute-start.2) | collective-permute-done | bytes 55328 | tf_op jit(solution)/shard_map/ppermute | solution.py:324
  14.8 0.5 %collective-permute-done.3.refs_5_ = bf16[72,768]{1,0:T(8,128)(2,1)S(1)} collective-permute-done((bf16[72,768]{1,0:T(8,128)(2,1)S(1)}, bf16[72,768]{1,0:T(8,128)(2,1)S(1)}, u32[]{:S(2)}, u32[]{:S(2)}) %collective-permute-start.3) | collective-permute-done | bytes 110624 | tf_op jit(solution)/shard_map/ppermute | solution.py:322
  15.3 0.4 %collective-permute-start.8 = (bf16[72,768]{1,0:T(8,128)(2,1)S(1)}, bf16[72,768]{1,0:T(8,128)(2,1)S(1)}, u32[]{:S(2)}, u32[]{:S(2)}) collective-permute-start(bf16[72,768]{1,0:T(8,128)(2,1)S(1)} %collective-permute-done.4.refs_6_), channel_id=1, source_target_pairs={{0,4},{4,0},{8,12},{12,8},{16,20},{20,16},{24,28},{28,24},{1,5},{5... | collective-permute-start | bytes 331784 | tf_op jit(solution)/shard_map/ppermute | solution.py:332
  15.8 0.1 collective-permute-start.9
  15.9 1.0 %attention.2 = (bf16[1,36,768]{2,1,0:T(8,128)(2,1)S(1)}, bf16[1,36,768]{2,1,0:T(8,128)(2,1)S(1)}, bf16[1,36,768]{2,1,0:T(8,128)(2,1)S(1)}, bf16[1,36,768]{2,1,0:T(8,128)(2,1)S(1)}, bf16[144,768]{1,0:T(8,128)(2,1)S(1)}) custom-call(bf16[1,36,768]{2,1,0:T(8,128)(2,1)S(1)} %get-tuple-element.39.refs_0_, bf16[1,36,768]{2,1,0:T(8,128)(2,1)S(1)} %collective-permute-done.refs_1_, ...), custom_call_target="tpu_custom_call" | custom-call | flops 63700992 | bytes 1048576 | tf_op jit(solution)/shard_map/attention/pallas_call | solution.py:161
  16.8 0.2 collective-permute-done.9.refs_4_
  17.1 1.0 %attention.3 = (bf16[72,768]{1,0:T(8,128)(2,1)S(1)}, bf16[72,768]{1,0:T(8,128)(2,1)S(1)}, bf16[72,768]{1,0:T(8,128)(2,1)S(1)}, bf16[72,768]{1,0:T(8,128)(2,1)S(1)}) custom-call(bf16[144,768]{1,0:T(8,128)(2,1)S(1)} %get-tuple-element.44.refs_0_, bf16[72,768]{1,0:T(8,128)(2,1)S(1)} %collective-permute-done.6.refs_1_, ...), custom_call_target="tpu_custom_call" | custom-call | flops 63700992 | bytes 1048576 | tf_op jit(solution)/shard_map/attention/pallas_call | solution.py:161
  18.1 1.6 %collective-permute-start.12 = (bf16[72,768]{1,0:T(8,128)(2,1)S(1)}, bf16[72,768]{1,0:T(8,128)(2,1)S(1)}, u32[]{:S(2)}, u32[]{:S(2)}) collective-permute-start(bf16[72,768]{1,0:T(8,128)(2,1)S(1)} %get-tuple-element.61), channel_id=1, source_target_pairs={{24,0},{28,4},{16,8},{20,12},{8,16},{12,20},{0,24},{4,28},{25,1},{... | collective-permute-start | bytes 331784 | tf_op jit(solution)/shard_map/ppermute | solution.py:339
  19.6 1.5 %collective-permute-start.10 = (bf16[72,768]{1,0:T(8,128)(2,1)S(1)}, bf16[72,768]{1,0:T(8,128)(2,1)S(1)}, u32[]{:S(2)}, u32[]{:S(2)}) collective-permute-start(bf16[72,768]{1,0:T(8,128)(2,1)S(1)} %get-tuple-element.53), channel_id=1, source_target_pairs={{8,0},{12,4},{0,8},{4,12},{24,16},{28,20},{16,24},{20,28},{9,1},{1... | collective-permute-start | bytes 331784 | tf_op jit(solution)/shard_map/ppermute | solution.py:339
  21.1 0.5 %collective-permute-start.11 = (bf16[72,768]{1,0:T(8,128)(2,1)S(1)}, bf16[72,768]{1,0:T(8,128)(2,1)S(1)}, u32[]{:S(2)}, u32[]{:S(2)}) collective-permute-start(bf16[72,768]{1,0:T(8,128)(2,1)S(1)} %get-tuple-element.54), channel_id=1, source_target_pairs={{16,0},{20,4},{24,8},{28,12},{0,16},{4,20},{8,24},{12,28},{17,1},{... | collective-permute-start | bytes 331784 | tf_op jit(solution)/shard_map/ppermute | solution.py:339
  21.6 0.9 %mix_own.1 = (f32[40,768]{1,0:T(8,128)S(1)}, f32[80,128]{1,0:T(8,128)S(1)}, f32[80,768]{1,0:T(8,128)S(1)}) custom-call(bf16[72,768]{1,0:T(8,128)(2,1)S(1)} %get-tuple-element.55.block, bf16[768,768]{1,0:T(8,128)(2,1)S(1)} %get-tuple-element.56.w_query, bf16[768,768]{1,0:T(8,128)(2,1)S(1)} %get-tuple-element.57.w_key.refs_3_, ...), custom_call_target="tpu_custom_call" | custom-call | flops 169869312 | bytes 4194304 | tf_op jit(solution)/shard_map/mix_own/pallas_call | solution.py:257
  22.6 2.4 %collective-permute-done.12.block = bf16[72,768]{1,0:T(8,128)(2,1)S(1)} collective-permute-done((bf16[72,768]{1,0:T(8,128)(2,1)S(1)}, bf16[72,768]{1,0:T(8,128)(2,1)S(1)}, u32[]{:S(2)}, u32[]{:S(2)}) %collective-permute-start.12) | collective-permute-done | bytes 110624 | tf_op jit(solution)/shard_map/ppermute | solution.py:339
  24.9 0.8 %mix_part.1 = (f32[80,128]{1,0:T(8,128)S(1)}, f32[80,768]{1,0:T(8,128)S(1)}) custom-call(bf16[72,768]{1,0:T(8,128)(2,1)S(1)} %collective-permute-done.12.block, f32[40,768]{1,0:T(8,128)S(1)} %get-tuple-element.59.query.refs_2_, bf16[768,768]{1,0:T(8,128)(2,1)S(1)} %get-tuple-element.57.w_key.refs_3_, bf16[768,768]{1,0:T(8,128)(2,1)S(1)} %get-tuple-element.58.w_value.refs_4_), custom_call_target="tpu_custom_call" | custom-call | flops 169869312 | bytes 4194304 | tf_op jit(solution)/shard_map/mix_part/pallas_call | solution.py:257
  25.8 0.9 %collective-permute-done.10.refs_0_ = bf16[72,768]{1,0:T(8,128)(2,1)S(1)} collective-permute-done((bf16[72,768]{1,0:T(8,128)(2,1)S(1)}, bf16[72,768]{1,0:T(8,128)(2,1)S(1)}, u32[]{:S(2)}, u32[]{:S(2)}) %collective-permute-start.10) | collective-permute-done | bytes 110624 | tf_op jit(solution)/shard_map/ppermute | solution.py:339
  26.6 1.6 %mix_last.1 = bf16[1,36,768]{2,1,0:T(8,128)(2,1)} custom-call(bf16[72,768]{1,0:T(8,128)(2,1)S(1)} %collective-permute-done.10.refs_0_, bf16[72,768]{1,0:T(8,128)(2,1)S(1)} %collective-permute-done.11.refs_1_, f32[40,768]{1,0:T(8,128)S(1)} %get-tuple-element.59.query.refs_2_, bf16[768,768]{1,0:T(8,128)(2,1)S(1)} %get-tuple-element.57.w_key.refs_3_, ...), custom_call_target="tpu_custom_call" | custom-call | flops 339738624 | bytes 4194304 | tf_op jit(solution)/shard_map/mix_last/pallas_call | solution.py:257
  (9 shorter events, 0.1 us)
Async XLA Ops:
  0.9 8.7 %collective-permute-start = (bf16[1,36,768]{2,1,0:T(8,128)(2,1)S(1)}, bf16[1,36,768]{2,1,0:T(8,128)(2,1)S(1)}, u32[]{:S(2)}, u32[]{:S(2)}) collective-permute-start(bf16[1,36,768]{2,1,0:T(8,128)(2,1)S(1)} %get-tuple-element.39.refs_0_), channel_id=1, source_target_pairs={{0,8},{4,12},{8,0},{12,4},{16,24},{20,28},{24,16},{28,20},{1,9},{5... | collective-permute-start | bytes 165896 | tf_op jit(solution)/shard_map/ppermute | solution.py:324
  3.9 11.3 %collective-permute-start.3 = (bf16[72,768]{1,0:T(8,128)(2,1)S(1)}, bf16[72,768]{1,0:T(8,128)(2,1)S(1)}, u32[]{:S(2)}, u32[]{:S(2)}) collective-permute-start(bf16[72,768]{1,0:T(8,128)(2,1)S(1)} %get-tuple-element.45.refs_4_), channel_id=1, source_target_pairs={{0,2},{1,3},{2,0},{3,1},{4,6},{5,7},{6,4},{7,5},{8,10},{9,11},{10,... | collective-permute-start | bytes 331784 | tf_op jit(solution)/shard_map/ppermute | solution.py:322
  6.5 8.7 %collective-permute-start.4 = (bf16[72,768]{1,0:T(8,128)(2,1)S(1)}, bf16[72,768]{1,0:T(8,128)(2,1)S(1)}, u32[]{:S(2)}, u32[]{:S(2)}) collective-permute-start(bf16[72,768]{1,0:T(8,128)(2,1)S(1)} %get-tuple-element.45.refs_4_), channel_id=1, source_target_pairs={{0,3},{1,2},{2,1},{3,0},{4,7},{5,6},{6,5},{7,4},{8,11},{9,10},{10,... | collective-permute-start | bytes 331784 | tf_op jit(solution)/shard_map/ppermute | solution.py:322
  7.9 7.5 %collective-permute-start.5 = (bf16[72,768]{1,0:T(8,128)(2,1)S(1)}, bf16[72,768]{1,0:T(8,128)(2,1)S(1)}, u32[]{:S(2)}, u32[]{:S(2)}) collective-permute-start(bf16[72,768]{1,0:T(8,128)(2,1)S(1)} %get-tuple-element.45.refs_4_), channel_id=1, source_target_pairs={{0,1},{1,0},{2,3},{3,2},{4,5},{5,4},{6,7},{7,6},{8,9},{9,8},{10,11... | collective-permute-start | bytes 331784 | tf_op jit(solution)/shard_map/ppermute | solution.py:322
  8.1 4.9 %collective-permute-start.1 = (bf16[1,36,768]{2,1,0:T(8,128)(2,1)S(1)}, bf16[1,36,768]{2,1,0:T(8,128)(2,1)S(1)}, u32[]{:S(2)}, u32[]{:S(2)}) collective-permute-start(bf16[1,36,768]{2,1,0:T(8,128)(2,1)S(1)} %get-tuple-element.39.refs_0_), channel_id=1, source_target_pairs={{0,16},{4,20},{8,24},{12,28},{16,0},{20,4},{24,8},{28,12},{1,17},{... | collective-permute-start | bytes 165896 | tf_op jit(solution)/shard_map/ppermute | solution.py:324
  9.6 5.1 %collective-permute-start.2 = (bf16[1,36,768]{2,1,0:T(8,128)(2,1)S(1)}, bf16[1,36,768]{2,1,0:T(8,128)(2,1)S(1)}, u32[]{:S(2)}, u32[]{:S(2)}) collective-permute-start(bf16[1,36,768]{2,1,0:T(8,128)(2,1)S(1)} %get-tuple-element.39.refs_0_), channel_id=1, source_target_pairs={{0,24},{4,28},{8,16},{12,20},{16,8},{20,12},{24,0},{28,4},{1,25},{... | collective-permute-start | bytes 165896 | tf_op jit(solution)/shard_map/ppermute | solution.py:324
  14.8 2.1 %collective-permute-start.6 = (bf16[72,768]{1,0:T(8,128)(2,1)S(1)}, bf16[72,768]{1,0:T(8,128)(2,1)S(1)}, u32[]{:S(2)}, u32[]{:S(2)}) collective-permute-start(bf16[72,768]{1,0:T(8,128)(2,1)S(1)} %get-tuple-element.45.refs_4_), channel_id=1, source_target_pairs={{0,4},{4,0},{8,12},{12,8},{16,20},{20,16},{24,28},{28,24},{1,5},{5... | collective-permute-start | bytes 331784 | tf_op jit(solution)/shard_map/ppermute | solution.py:332
  15.2 1.6 %collective-permute-start.7 = (bf16[72,768]{1,0:T(8,128)(2,1)S(1)}, bf16[72,768]{1,0:T(8,128)(2,1)S(1)}, u32[]{:S(2)}, u32[]{:S(2)}) collective-permute-start(bf16[72,768]{1,0:T(8,128)(2,1)S(1)} %collective-permute-done.3.refs_5_), channel_id=1, source_target_pairs={{0,4},{4,0},{8,12},{12,8},{16,20},{20,16},{24,28},{28,24},{1,5},{5... | collective-permute-start | bytes 331784 | tf_op jit(solution)/shard_map/ppermute | solution.py:332
  15.3 1.5 %collective-permute-start.8 = (bf16[72,768]{1,0:T(8,128)(2,1)S(1)}, bf16[72,768]{1,0:T(8,128)(2,1)S(1)}, u32[]{:S(2)}, u32[]{:S(2)}) collective-permute-start(bf16[72,768]{1,0:T(8,128)(2,1)S(1)} %collective-permute-done.4.refs_6_), channel_id=1, source_target_pairs={{0,4},{4,0},{8,12},{12,8},{16,20},{20,16},{24,28},{28,24},{1,5},{5... | collective-permute-start | bytes 331784 | tf_op jit(solution)/shard_map/ppermute | solution.py:332
  15.8 1.3 %collective-permute-start.9 = (bf16[72,768]{1,0:T(8,128)(2,1)S(1)}, bf16[72,768]{1,0:T(8,128)(2,1)S(1)}, u32[]{:S(2)}, u32[]{:S(2)}) collective-permute-start(bf16[72,768]{1,0:T(8,128)(2,1)S(1)} %collective-permute-done.5.refs_7_), channel_id=1, source_target_pairs={{0,4},{4,0},{8,12},{12,8},{16,20},{20,16},{24,28},{28,24},{1,5},{5... | collective-permute-start | bytes 331784 | tf_op jit(solution)/shard_map/ppermute | solution.py:332
  18.1 6.9 %collective-permute-start.12 = (bf16[72,768]{1,0:T(8,128)(2,1)S(1)}, bf16[72,768]{1,0:T(8,128)(2,1)S(1)}, u32[]{:S(2)}, u32[]{:S(2)}) collective-permute-start(bf16[72,768]{1,0:T(8,128)(2,1)S(1)} %get-tuple-element.61), channel_id=1, source_target_pairs={{24,0},{28,4},{16,8},{20,12},{8,16},{12,20},{0,24},{4,28},{25,1},{... | collective-permute-start | bytes 331784 | tf_op jit(solution)/shard_map/ppermute | solution.py:339
  19.6 7.0 %collective-permute-start.10 = (bf16[72,768]{1,0:T(8,128)(2,1)S(1)}, bf16[72,768]{1,0:T(8,128)(2,1)S(1)}, u32[]{:S(2)}, u32[]{:S(2)}) collective-permute-start(bf16[72,768]{1,0:T(8,128)(2,1)S(1)} %get-tuple-element.53), channel_id=1, source_target_pairs={{8,0},{12,4},{0,8},{4,12},{24,16},{28,20},{16,24},{20,28},{9,1},{1... | collective-permute-start | bytes 331784 | tf_op jit(solution)/shard_map/ppermute | solution.py:339
  21.1 5.5 %collective-permute-start.11 = (bf16[72,768]{1,0:T(8,128)(2,1)S(1)}, bf16[72,768]{1,0:T(8,128)(2,1)S(1)}, u32[]{:S(2)}, u32[]{:S(2)}) collective-permute-start(bf16[72,768]{1,0:T(8,128)(2,1)S(1)} %get-tuple-element.54), channel_id=1, source_target_pairs={{16,0},{20,4},{24,8},{28,12},{0,16},{4,20},{8,24},{12,28},{17,1},{... | collective-permute-start | bytes 331784 | tf_op jit(solution)/shard_map/ppermute | solution.py:339

commit v8 on v7

--- a/solution.py
+++ b/solution.py
@@ -67,8 +67,8 @@
         out[:, cut] = mine
 
 
-def load_kernel(key, value, query, pair, near_query, near_key, near_value, apart, sems):
-    targets = (near_key, near_value, near_query.at[0])
+def load_kernel(key, value, query, pair, packed, near_key, near_value, near_query, apart, apart_query, sems):
+    targets = (near_key, near_value, near_query)
     copies = [
         pltpu.make_async_copy(source.at[0], target, sems.at[index])
         for index, (source, target) in enumerate(zip((key, value, query), targets))
@@ -78,19 +78,24 @@
     for copy in copies:
         copy.wait()
     pair[...] = stack_rows([near_key[...], near_value[...]], apart, near_key.shape[0])
+    middle = near_query.shape[1] // 2
+    sides = [near_query[:, :middle], near_query[:, middle:]]
+    packed[...] = stack_rows(sides, apart_query, near_query.shape[0])
 
 
 def load(key, value, query):
     _, rows, width = key.shape
     return pl.pallas_call(
         load_kernel,
-        out_shape=[near((2 * rows, width), key.dtype), near(query.shape, query.dtype)],
+        out_shape=[near((2 * rows, width), key.dtype), near((2 * rows, width // 2), query.dtype)],
         in_specs=[FAR] * 3,
         out_specs=[VMEM] * 2,
         scratch_shapes=[
             near((rows, width), key.dtype),
             near((rows, width), key.dtype),
+            near((rows, width), query.dtype),
             near((2 * rows, width)),
+            near((2 * rows, width // 2)),
             pltpu.SemaphoreType.DMA((3,)),
         ],
         name="load",
@@ -126,14 +131,15 @@
 def attention_kernel(head_width, query_count, earlier_count, block_count, *refs):
     queries, refs = refs[:query_count], refs[query_count:]
     blocks, refs = refs[:block_count], refs[block_count:]
-    *refs, key_stage, value_stage, query_stage, apart = refs
+    *refs, key_stage, value_stage, query_stage, apart, apart_query = refs
     rows = blocks[0].shape[0] // 2
     if earlier_count:
         earlier, outs = refs[:earlier_count], refs[earlier_count:]
         query = queries[0][...]
     else:
         earlier, (*outs, stacked) = (), refs
-        query = stack_rows([ref[0] for ref in queries], query_stage, rows)
+        sides = [halves(ref, apart_query) for ref in queries]
+        query = stack_rows([jnp.concatenate(side, axis=1) for side in sides], query_stage, rows)
         stacked[...] = query
     keys, values = zip(*[halves(ref, apart) for ref in blocks])
     key = stack_rows(keys, key_stage, rows)
@@ -164,7 +170,7 @@
         in_specs=[VMEM] * (len(queries) + len(blocks) + len(earlier)),
         out_specs=[VMEM] * (count + first),
         scratch_shapes=[near((key_total, width))] * 2
-        + [near((query_total, width)), near((2 * rows, width))],
+        + [near((query_total, width)), near((2 * rows, width)), near((2 * rows, width // 2))],
         compiler_params=pltpu.CompilerParams(vmem_limit_bytes=48 << 20),
         cost_estimate=pl.CostEstimate(flops=flops, bytes_accessed=1 << 20, transcendentals=0),
         name="attention",

time: 28.4 us -> 28.4 us (level)
  no operation moved by 1% of the time
where the time goes in v8:
time: 28.4 us; the launch traced here: 28.3 us
  starting transfers between devices  13.2 us (46%)
  Pallas kernels  8.28 us (29%)
  waiting for transfers between devices  6.67 us (23%)
    ppermute x3, starting transfers between devices, per_device(): lax.ppermute(near_query, 'frame', there)  5 us
    ppermute x3, starting transfers between devices, per_device(): lax.ppermute(own_block, 'qblk', there)  4.17 us
    ppermute x3, starting transfers between devices, per_device(): lax.ppermute(block, 'frame', back)  3.55 us
    pallas_call x3, Pallas kernels, mix_call(): pl.pallas_call(functools.partial(kernel, width // HEADS), out_shape=out_s...  3.37 us
    ppermute x3, waiting for transfers between devices, per_device(): lax.ppermute(block, 'frame', back)  3.24 us
    ppermute x3, waiting for transfers between devices, per_device(): lax.ppermute(near_query, 'frame', there)  2.57 us
    pallas_call x1, Pallas kernels, fetch(): pl.pallas_call(fetch_kernel, out_shape=[pltpu.VMEM(matrix.shape, matrix.d...  2.01 us
    pallas_call x2, Pallas kernels, attention(): pl.pallas_call(kernel, out_shape=[shape] * count + [near((query_total, wi...  1.96 us
  transfers between devices with their start and end apart: 13, of which 7 were waited for; matrix products, arithmetic and copies ran while one was open for 0% of the time, Pallas kernels for 17%

profile of v8, /device:TPU:0, one launch (start us, length us, event | category | flops | bytes accessed | tf_op | source)
XLA Modules:
  0.0 28.3 jit_solution(13107880434217162737)
XLA Ops:
  0.0 0.9 %load.1 = (bf16[72,768]{1,0:T(8,128)(2,1)S(1)}, bf16[72,384]{1,0:T(8,128)(2,1)S(1)}) custom-call(bf16[1,36,768]{2,1,0:T(8,128)(2,1)} %key.1, bf16[1,36,768]{2,1,0:T(8,128)(2,1)} %value.1, bf16[1,36,768]{2,1,0:T(8,128)(2,1)} %query.1), custom_call_target="tpu_custom_call" | custom-call | tf_op jit(solution)/shard_map/load/pallas_call | solution.py:88
  0.9 3.0 %collective-permute-start = (bf16[72,384]{1,0:T(8,128)(2,1)S(1)}, bf16[72,384]{1,0:T(8,128)(2,1)S(1)}, u32[]{:S(2)}, u32[]{:S(2)}) collective-permute-start(bf16[72,384]{1,0:T(8,128)(2,1)S(1)} %get-tuple-element.39.refs_0_), channel_id=1, source_target_pairs={{0,8},{4,12},{8,0},{12,4},{16,24},{20,28},{24,16},{28,20},{1,9},{5... | collective-permute-start | bytes 165896 | tf_op jit(solution)/shard_map/ppermute | solution.py:330
  4.0 2.6 %collective-permute-start.3 = (bf16[72,768]{1,0:T(8,128)(2,1)S(1)}, bf16[72,768]{1,0:T(8,128)(2,1)S(1)}, u32[]{:S(2)}, u32[]{:S(2)}) collective-permute-start(bf16[72,768]{1,0:T(8,128)(2,1)S(1)} %get-tuple-element.45.refs_4_), channel_id=1, source_target_pairs={{0,2},{1,3},{2,0},{3,1},{4,6},{5,7},{6,4},{7,5},{8,10},{9,11},{10,... | collective-permute-start | bytes 331784 | tf_op jit(solution)/shard_map/ppermute | solution.py:328
  6.5 1.3 %collective-permute-start.4 = (bf16[72,768]{1,0:T(8,128)(2,1)S(1)}, bf16[72,768]{1,0:T(8,128)(2,1)S(1)}, u32[]{:S(2)}, u32[]{:S(2)}) collective-permute-start(bf16[72,768]{1,0:T(8,128)(2,1)S(1)} %get-tuple-element.45.refs_4_), channel_id=1, source_target_pairs={{0,3},{1,2},{2,1},{3,0},{4,7},{5,6},{6,5},{7,4},{8,11},{9,10},{10,... | collective-permute-start | bytes 331784 | tf_op jit(solution)/shard_map/ppermute | solution.py:328
  7.9 0.2 collective-permute-start.5
  8.1 1.5 %collective-permute-start.1 = (bf16[72,384]{1,0:T(8,128)(2,1)S(1)}, bf16[72,384]{1,0:T(8,128)(2,1)S(1)}, u32[]{:S(2)}, u32[]{:S(2)}) collective-permute-start(bf16[72,384]{1,0:T(8,128)(2,1)S(1)} %get-tuple-element.39.refs_0_), channel_id=1, source_target_pairs={{0,16},{4,20},{8,24},{12,28},{16,0},{20,4},{24,8},{28,12},{1,17},{... | collective-permute-start | bytes 165896 | tf_op jit(solution)/shard_map/ppermute | solution.py:330
  9.6 0.5 %collective-permute-start.2 = (bf16[72,384]{1,0:T(8,128)(2,1)S(1)}, bf16[72,384]{1,0:T(8,128)(2,1)S(1)}, u32[]{:S(2)}, u32[]{:S(2)}) collective-permute-start(bf16[72,384]{1,0:T(8,128)(2,1)S(1)} %get-tuple-element.39.refs_0_), channel_id=1, source_target_pairs={{0,24},{4,28},{8,16},{12,20},{16,8},{20,12},{24,0},{28,4},{1,25},{... | collective-permute-start | bytes 165896 | tf_op jit(solution)/shard_map/ppermute | solution.py:330
  10.1 2.0 %fetch.1 = (bf16[768,768]{1,0:T(8,128)(2,1)S(1)}, bf16[768,768]{1,0:T(8,128)(2,1)S(1)}, bf16[768,768]{1,0:T(8,128)(2,1)S(1)}) custom-call(bf16[768,768]{1,0:T(8,128)(2,1)} %refs_0_.1, bf16[768,768]{1,0:T(8,128)(2,1)} %refs_1_.1, bf16[768,768]{1,0:T(8,128)(2,1)} %refs_2_.1), custom_call_target="tpu_custom_call" | custom-call | bytes 6291456 | tf_op jit(solution)/shard_map/fetch/pallas_call | solution.py:119
  12.1 0.7 %collective-permute-done.1.refs_2_ = bf16[72,384]{1,0:T(8,128)(2,1)S(1)} collective-permute-done((bf16[72,384]{1,0:T(8,128)(2,1)S(1)}, bf16[72,384]{1,0:T(8,128)(2,1)S(1)}, u32[]{:S(2)}, u32[]{:S(2)}) %collective-permute-start.1) | collective-permute-done | bytes 55328 | tf_op jit(solution)/shard_map/ppermute | solution.py:330
  12.9 1.8 %collective-permute-done.2.refs_3_ = bf16[72,384]{1,0:T(8,128)(2,1)S(1)} collective-permute-done((bf16[72,384]{1,0:T(8,128)(2,1)S(1)}, bf16[72,384]{1,0:T(8,128)(2,1)S(1)}, u32[]{:S(2)}, u32[]{:S(2)}) %collective-permute-start.2) | collective-permute-done | bytes 55328 | tf_op jit(solution)/shard_map/ppermute | solution.py:330
  14.7 0.5 %collective-permute-done.3.refs_5_ = bf16[72,768]{1,0:T(8,128)(2,1)S(1)} collective-permute-done((bf16[72,768]{1,0:T(8,128)(2,1)S(1)}, bf16[72,768]{1,0:T(8,128)(2,1)S(1)}, u32[]{:S(2)}, u32[]{:S(2)}) %collective-permute-start.3) | collective-permute-done | bytes 110624 | tf_op jit(solution)/shard_map/ppermute | solution.py:328
  15.3 0.1 collective-permute-done.5.refs_7_
  15.3 0.4 %collective-permute-start.8 = (bf16[72,768]{1,0:T(8,128)(2,1)S(1)}, bf16[72,768]{1,0:T(8,128)(2,1)S(1)}, u32[]{:S(2)}, u32[]{:S(2)}) collective-permute-start(bf16[72,768]{1,0:T(8,128)(2,1)S(1)} %collective-permute-done.4.refs_6_), channel_id=1, source_target_pairs={{0,4},{4,0},{8,12},{12,8},{16,20},{20,16},{24,28},{28,24},{1,5},{5... | collective-permute-start | bytes 331784 | tf_op jit(solution)/shard_map/ppermute | solution.py:338
  15.9 1.0 %attention.2 = (bf16[1,36,768]{2,1,0:T(8,128)(2,1)S(1)}, bf16[1,36,768]{2,1,0:T(8,128)(2,1)S(1)}, bf16[1,36,768]{2,1,0:T(8,128)(2,1)S(1)}, bf16[1,36,768]{2,1,0:T(8,128)(2,1)S(1)}, bf16[144,768]{1,0:T(8,128)(2,1)S(1)}) custom-call(bf16[72,384]{1,0:T(8,128)(2,1)S(1)} %get-tuple-element.39.refs_0_, bf16[72,384]{1,0:T(8,128)(2,1)S(1)} %collective-permute-done.refs_1_, ...), custom_call_target="tpu_custom_call" | custom-call | flops 63700992 | bytes 1048576 | tf_op jit(solution)/shard_map/attention/pallas_call | solution.py:167
  16.9 0.2 collective-permute-done.9.refs_4_
  17.1 1.0 %attention.3 = (bf16[72,768]{1,0:T(8,128)(2,1)S(1)}, bf16[72,768]{1,0:T(8,128)(2,1)S(1)}, bf16[72,768]{1,0:T(8,128)(2,1)S(1)}, bf16[72,768]{1,0:T(8,128)(2,1)S(1)}) custom-call(bf16[144,768]{1,0:T(8,128)(2,1)S(1)} %get-tuple-element.44.refs_0_, bf16[72,768]{1,0:T(8,128)(2,1)S(1)} %collective-permute-done.6.refs_1_, ...), custom_call_target="tpu_custom_call" | custom-call | flops 63700992 | bytes 1048576 | tf_op jit(solution)/shard_map/attention/pallas_call | solution.py:167
  18.1 1.6 %collective-permute-start.12 = (bf16[72,768]{1,0:T(8,128)(2,1)S(1)}, bf16[72,768]{1,0:T(8,128)(2,1)S(1)}, u32[]{:S(2)}, u32[]{:S(2)}) collective-permute-start(bf16[72,768]{1,0:T(8,128)(2,1)S(1)} %get-tuple-element.61), channel_id=1, source_target_pairs={{24,0},{28,4},{16,8},{20,12},{8,16},{12,20},{0,24},{4,28},{25,1},{... | collective-permute-start | bytes 331784 | tf_op jit(solution)/shard_map/ppermute | solution.py:345
  19.6 1.5 %collective-permute-start.10 = (bf16[72,768]{1,0:T(8,128)(2,1)S(1)}, bf16[72,768]{1,0:T(8,128)(2,1)S(1)}, u32[]{:S(2)}, u32[]{:S(2)}) collective-permute-start(bf16[72,768]{1,0:T(8,128)(2,1)S(1)} %get-tuple-element.53), channel_id=1, source_target_pairs={{8,0},{12,4},{0,8},{4,12},{24,16},{28,20},{16,24},{20,28},{9,1},{1... | collective-permute-start | bytes 331784 | tf_op jit(solution)/shard_map/ppermute | solution.py:345
  21.1 0.5 %collective-permute-start.11 = (bf16[72,768]{1,0:T(8,128)(2,1)S(1)}, bf16[72,768]{1,0:T(8,128)(2,1)S(1)}, u32[]{:S(2)}, u32[]{:S(2)}) collective-permute-start(bf16[72,768]{1,0:T(8,128)(2,1)S(1)} %get-tuple-element.54), channel_id=1, source_target_pairs={{16,0},{20,4},{24,8},{28,12},{0,16},{4,20},{8,24},{12,28},{17,1},{... | collective-permute-start | bytes 331784 | tf_op jit(solution)/shard_map/ppermute | solution.py:345
  21.6 0.9 %mix_own.1 = (f32[40,768]{1,0:T(8,128)S(1)}, f32[80,128]{1,0:T(8,128)S(1)}, f32[80,768]{1,0:T(8,128)S(1)}) custom-call(bf16[72,768]{1,0:T(8,128)(2,1)S(1)} %get-tuple-element.55.block, bf16[768,768]{1,0:T(8,128)(2,1)S(1)} %get-tuple-element.56.w_query, bf16[768,768]{1,0:T(8,128)(2,1)S(1)} %get-tuple-element.57.w_key.refs_3_, ...), custom_call_target="tpu_custom_call" | custom-call | flops 169869312 | bytes 4194304 | tf_op jit(solution)/shard_map/mix_own/pallas_call | solution.py:263
  22.6 2.4 %collective-permute-done.12.block = bf16[72,768]{1,0:T(8,128)(2,1)S(1)} collective-permute-done((bf16[72,768]{1,0:T(8,128)(2,1)S(1)}, bf16[72,768]{1,0:T(8,128)(2,1)S(1)}, u32[]{:S(2)}, u32[]{:S(2)}) %collective-permute-start.12) | collective-permute-done | bytes 110624 | tf_op jit(solution)/shard_map/ppermute | solution.py:345
  24.9 0.8 %mix_part.1 = (f32[80,128]{1,0:T(8,128)S(1)}, f32[80,768]{1,0:T(8,128)S(1)}) custom-call(bf16[72,768]{1,0:T(8,128)(2,1)S(1)} %collective-permute-done.12.block, f32[40,768]{1,0:T(8,128)S(1)} %get-tuple-element.59.query.refs_2_, bf16[768,768]{1,0:T(8,128)(2,1)S(1)} %get-tuple-element.57.w_key.refs_3_, bf16[768,768]{1,0:T(8,128)(2,1)S(1)} %get-tuple-element.58.w_value.refs_4_), custom_call_target="tpu_custom_call" | custom-call | flops 169869312 | bytes 4194304 | tf_op jit(solution)/shard_map/mix_part/pallas_call | solution.py:263
  25.8 0.9 %collective-permute-done.10.refs_0_ = bf16[72,768]{1,0:T(8,128)(2,1)S(1)} collective-permute-done((bf16[72,768]{1,0:T(8,128)(2,1)S(1)}, bf16[72,768]{1,0:T(8,128)(2,1)S(1)}, u32[]{:S(2)}, u32[]{:S(2)}) %collective-permute-start.10) | collective-permute-done | bytes 110624 | tf_op jit(solution)/shard_map/ppermute | solution.py:345
  26.7 1.6 %mix_last.1 = bf16[1,36,768]{2,1,0:T(8,128)(2,1)} custom-call(bf16[72,768]{1,0:T(8,128)(2,1)S(1)} %collective-permute-done.10.refs_0_, bf16[72,768]{1,0:T(8,128)(2,1)S(1)} %collective-permute-done.11.refs_1_, f32[40,768]{1,0:T(8,128)S(1)} %get-tuple-element.59.query.refs_2_, bf16[768,768]{1,0:T(8,128)(2,1)S(1)} %get-tuple-element.57.w_key.refs_3_, ...), custom_call_target="tpu_custom_call" | custom-call | flops 339738624 | bytes 4194304 | tf_op jit(solution)/shard_map/mix_last/pallas_call | solution.py:263
  (9 shorter events, 0.1 us)
Async XLA Ops:
  0.9 8.7 %collective-permute-start = (bf16[72,384]{1,0:T(8,128)(2,1)S(1)}, bf16[72,384]{1,0:T(8,128)(2,1)S(1)}, u32[]{:S(2)}, u32[]{:S(2)}) collective-permute-start(bf16[72,384]{1,0:T(8,128)(2,1)S(1)} %get-tuple-element.39.refs_0_), channel_id=1, source_target_pairs={{0,8},{4,12},{8,0},{12,4},{16,24},{20,28},{24,16},{28,20},{1,9},{5... | collective-permute-start | bytes 165896 | tf_op jit(solution)/shard_map/ppermute | solution.py:330
  4.0 11.3 %collective-permute-start.3 = (bf16[72,768]{1,0:T(8,128)(2,1)S(1)}, bf16[72,768]{1,0:T(8,128)(2,1)S(1)}, u32[]{:S(2)}, u32[]{:S(2)}) collective-permute-start(bf16[72,768]{1,0:T(8,128)(2,1)S(1)} %get-tuple-element.45.refs_4_), channel_id=1, source_target_pairs={{0,2},{1,3},{2,0},{3,1},{4,6},{5,7},{6,4},{7,5},{8,10},{9,11},{10,... | collective-permute-start | bytes 331784 | tf_op jit(solution)/shard_map/ppermute | solution.py:328
  6.5 8.7 %collective-permute-start.4 = (bf16[72,768]{1,0:T(8,128)(2,1)S(1)}, bf16[72,768]{1,0:T(8,128)(2,1)S(1)}, u32[]{:S(2)}, u32[]{:S(2)}) collective-permute-start(bf16[72,768]{1,0:T(8,128)(2,1)S(1)} %get-tuple-element.45.refs_4_), channel_id=1, source_target_pairs={{0,3},{1,2},{2,1},{3,0},{4,7},{5,6},{6,5},{7,4},{8,11},{9,10},{10,... | collective-permute-start | bytes 331784 | tf_op jit(solution)/shard_map/ppermute | solution.py:328
  7.9 7.5 %collective-permute-start.5 = (bf16[72,768]{1,0:T(8,128)(2,1)S(1)}, bf16[72,768]{1,0:T(8,128)(2,1)S(1)}, u32[]{:S(2)}, u32[]{:S(2)}) collective-permute-start(bf16[72,768]{1,0:T(8,128)(2,1)S(1)} %get-tuple-element.45.refs_4_), channel_id=1, source_target_pairs={{0,1},{1,0},{2,3},{3,2},{4,5},{5,4},{6,7},{7,6},{8,9},{9,8},{10,11... | collective-permute-start | bytes 331784 | tf_op jit(solution)/shard_map/ppermute | solution.py:328
  8.1 4.7 %collective-permute-start.1 = (bf16[72,384]{1,0:T(8,128)(2,1)S(1)}, bf16[72,384]{1,0:T(8,128)(2,1)S(1)}, u32[]{:S(2)}, u32[]{:S(2)}) collective-permute-start(bf16[72,384]{1,0:T(8,128)(2,1)S(1)} %get-tuple-element.39.refs_0_), channel_id=1, source_target_pairs={{0,16},{4,20},{8,24},{12,28},{16,0},{20,4},{24,8},{28,12},{1,17},{... | collective-permute-start | bytes 165896 | tf_op jit(solution)/shard_map/ppermute | solution.py:330
  9.6 5.1 %collective-permute-start.2 = (bf16[72,384]{1,0:T(8,128)(2,1)S(1)}, bf16[72,384]{1,0:T(8,128)(2,1)S(1)}, u32[]{:S(2)}, u32[]{:S(2)}) collective-permute-start(bf16[72,384]{1,0:T(8,128)(2,1)S(1)} %get-tuple-element.39.refs_0_), channel_id=1, source_target_pairs={{0,24},{4,28},{8,16},{12,20},{16,8},{20,12},{24,0},{28,4},{1,25},{... | collective-permute-start | bytes 165896 | tf_op jit(solution)/shard_map/ppermute | solution.py:330
  14.7 2.1 %collective-permute-start.6 = (bf16[72,768]{1,0:T(8,128)(2,1)S(1)}, bf16[72,768]{1,0:T(8,128)(2,1)S(1)}, u32[]{:S(2)}, u32[]{:S(2)}) collective-permute-start(bf16[72,768]{1,0:T(8,128)(2,1)S(1)} %get-tuple-element.45.refs_4_), channel_id=1, source_target_pairs={{0,4},{4,0},{8,12},{12,8},{16,20},{20,16},{24,28},{28,24},{1,5},{5... | collective-permute-start | bytes 331784 | tf_op jit(solution)/shard_map/ppermute | solution.py:338
  15.2 1.6 %collective-permute-start.7 = (bf16[72,768]{1,0:T(8,128)(2,1)S(1)}, bf16[72,768]{1,0:T(8,128)(2,1)S(1)}, u32[]{:S(2)}, u32[]{:S(2)}) collective-permute-start(bf16[72,768]{1,0:T(8,128)(2,1)S(1)} %collective-permute-done.3.refs_5_), channel_id=1, source_target_pairs={{0,4},{4,0},{8,12},{12,8},{16,20},{20,16},{24,28},{28,24},{1,5},{5... | collective-permute-start | bytes 331784 | tf_op jit(solution)/shard_map/ppermute | solution.py:338
  15.3 1.5 %collective-permute-start.8 = (bf16[72,768]{1,0:T(8,128)(2,1)S(1)}, bf16[72,768]{1,0:T(8,128)(2,1)S(1)}, u32[]{:S(2)}, u32[]{:S(2)}) collective-permute-start(bf16[72,768]{1,0:T(8,128)(2,1)S(1)} %collective-permute-done.4.refs_6_), channel_id=1, source_target_pairs={{0,4},{4,0},{8,12},{12,8},{16,20},{20,16},{24,28},{28,24},{1,5},{5... | collective-permute-start | bytes 331784 | tf_op jit(solution)/shard_map/ppermute | solution.py:338
  15.8 1.3 %collective-permute-start.9 = (bf16[72,768]{1,0:T(8,128)(2,1)S(1)}, bf16[72,768]{1,0:T(8,128)(2,1)S(1)}, u32[]{:S(2)}, u32[]{:S(2)}) collective-permute-start(bf16[72,768]{1,0:T(8,128)(2,1)S(1)} %collective-permute-done.5.refs_7_), channel_id=1, source_target_pairs={{0,4},{4,0},{8,12},{12,8},{16,20},{20,16},{24,28},{28,24},{1,5},{5... | collective-permute-start | bytes 331784 | tf_op jit(solution)/shard_map/ppermute | solution.py:338
  18.1 6.9 %collective-permute-start.12 = (bf16[72,768]{1,0:T(8,128)(2,1)S(1)}, bf16[72,768]{1,0:T(8,128)(2,1)S(1)}, u32[]{:S(2)}, u32[]{:S(2)}) collective-permute-start(bf16[72,768]{1,0:T(8,128)(2,1)S(1)} %get-tuple-element.61), channel_id=1, source_target_pairs={{24,0},{28,4},{16,8},{20,12},{8,16},{12,20},{0,24},{4,28},{25,1},{... | collective-permute-start | bytes 331784 | tf_op jit(solution)/shard_map/ppermute | solution.py:345
  19.6 7.0 %collective-permute-start.10 = (bf16[72,768]{1,0:T(8,128)(2,1)S(1)}, bf16[72,768]{1,0:T(8,128)(2,1)S(1)}, u32[]{:S(2)}, u32[]{:S(2)}) collective-permute-start(bf16[72,768]{1,0:T(8,128)(2,1)S(1)} %get-tuple-element.53), channel_id=1, source_target_pairs={{8,0},{12,4},{0,8},{4,12},{24,16},{28,20},{16,24},{20,28},{9,1},{1... | collective-permute-start | bytes 331784 | tf_op jit(solution)/shard_map/ppermute | solution.py:345
  21.1 5.5 %collective-permute-start.11 = (bf16[72,768]{1,0:T(8,128)(2,1)S(1)}, bf16[72,768]{1,0:T(8,128)(2,1)S(1)}, u32[]{:S(2)}, u32[]{:S(2)}) collective-permute-start(bf16[72,768]{1,0:T(8,128)(2,1)S(1)} %get-tuple-element.54), channel_id=1, source_target_pairs={{16,0},{20,4},{24,8},{28,12},{0,16},{4,20},{8,24},{12,28},{17,1},{... | collective-permute-start | bytes 331784 | tf_op jit(solution)/shard_map/ppermute | solution.py:345

commit v9 on v7

--- a/solution.py
+++ b/solution.py
@@ -325,10 +325,8 @@
     w_query, w_key, w_value = fetch((w_query, w_key, w_value))
     *queries, w_query, w_key, w_value = lax.optimization_barrier((*queries, w_query, w_key, w_value))
     turned = [
-        lax.optimization_barrier((block, *queries, *blocks[index + 1 :]))[0]
-        for index, block in enumerate(blocks)
-    ]
-    turned[:2] = [lax.optimization_barrier((block, *queries))[0] for block in blocks[:2]]
+        lax.optimization_barrier((block, *queries))[0] for block in blocks
+    ]
     other_blocks = [lax.ppermute(block, "frame", swap) for block in turned]
     *own, query = attention(queries, blocks)
     pooled = attention([query], other_blocks, own)

time: 28.4 us -> 28.4 us (level)
  transfers between devices with their start and end apart: 13 -> 13, of which waited for: 7 -> 6; matrix products, arithmetic and copies ran while one was open for 0% -> 0% of each run, Pallas kernels for 17% -> 17%
where the time goes in v9:
time: 28.4 us; the launch traced here: 28.2 us
  starting transfers between devices  13.3 us (47%)
  Pallas kernels  8.25 us (29%)
  waiting for transfers between devices  6.6 us (23%)
    ppermute x3, starting transfers between devices, per_device(): lax.ppermute(near_query, 'frame', there)  5 us
    ppermute x3, starting transfers between devices, per_device(): lax.ppermute(own_block, 'qblk', there)  4.17 us
    ppermute x3, starting transfers between devices, per_device(): lax.ppermute(block, 'frame', back)  3.55 us
    pallas_call x3, Pallas kernels, mix_call(): pl.pallas_call(functools.partial(kernel, width // HEADS), out_shape=out_s...  3.37 us
    ppermute x3, waiting for transfers between devices, per_device(): lax.ppermute(block, 'frame', back)  3.22 us
    ppermute x3, waiting for transfers between devices, per_device(): lax.ppermute(near_query, 'frame', there)  2.63 us
    pallas_call x1, Pallas kernels, fetch(): pl.pallas_call(fetch_kernel, out_shape=[pltpu.VMEM(matrix.shape, matrix.d...  2.01 us
    pallas_call x2, Pallas kernels, attention(): pl.pallas_call(kernel, out_shape=[shape] * count + [near((query_total, wi...  1.94 us
  transfers between devices with their start and end apart: 13, of which 6 were waited for; matrix products, arithmetic and copies ran while one was open for 0% of the time, Pallas kernels for 17%

profile of v9, /device:TPU:0, one launch (start us, length us, event | category | flops | bytes accessed | tf_op | source)
XLA Modules:
  0.0 28.2 jit_solution(4649320576078565970)
XLA Ops:
  0.0 0.9 %load.1 = (bf16[72,768]{1,0:T(8,128)(2,1)S(1)}, bf16[1,36,768]{2,1,0:T(8,128)(2,1)S(1)}) custom-call(bf16[1,36,768]{2,1,0:T(8,128)(2,1)} %key.1, bf16[1,36,768]{2,1,0:T(8,128)(2,1)} %value.1, bf16[1,36,768]{2,1,0:T(8,128)(2,1)} %query.1), custom_call_target="tpu_custom_call" | custom-call | tf_op jit(solution)/shard_map/load/pallas_call | solution.py:85
  0.9 3.0 %collective-permute-start = (bf16[1,36,768]{2,1,0:T(8,128)(2,1)S(1)}, bf16[1,36,768]{2,1,0:T(8,128)(2,1)S(1)}, u32[]{:S(2)}, u32[]{:S(2)}) collective-permute-start(bf16[1,36,768]{2,1,0:T(8,128)(2,1)S(1)} %get-tuple-element.39.refs_0_), channel_id=1, source_target_pairs={{0,8},{4,12},{8,0},{12,4},{16,24},{20,28},{24,16},{28,20},{1,9},{5... | collective-permute-start | bytes 165896 | tf_op jit(solution)/shard_map/ppermute | solution.py:324
  3.9 2.6 %collective-permute-start.3 = (bf16[72,768]{1,0:T(8,128)(2,1)S(1)}, bf16[72,768]{1,0:T(8,128)(2,1)S(1)}, u32[]{:S(2)}, u32[]{:S(2)}) collective-permute-start(bf16[72,768]{1,0:T(8,128)(2,1)S(1)} %get-tuple-element.45.refs_4_), channel_id=1, source_target_pairs={{0,2},{1,3},{2,0},{3,1},{4,6},{5,7},{6,4},{7,5},{8,10},{9,11},{10,... | collective-permute-start | bytes 331784 | tf_op jit(solution)/shard_map/ppermute | solution.py:322
  6.5 1.3 %collective-permute-start.4 = (bf16[72,768]{1,0:T(8,128)(2,1)S(1)}, bf16[72,768]{1,0:T(8,128)(2,1)S(1)}, u32[]{:S(2)}, u32[]{:S(2)}) collective-permute-start(bf16[72,768]{1,0:T(8,128)(2,1)S(1)} %get-tuple-element.45.refs_4_), channel_id=1, source_target_pairs={{0,3},{1,2},{2,1},{3,0},{4,7},{5,6},{6,5},{7,4},{8,11},{9,10},{10,... | collective-permute-start | bytes 331784 | tf_op jit(solution)/shard_map/ppermute | solution.py:322
  7.9 0.2 collective-permute-start.5
  8.1 1.5 %collective-permute-start.1 = (bf16[1,36,768]{2,1,0:T(8,128)(2,1)S(1)}, bf16[1,36,768]{2,1,0:T(8,128)(2,1)S(1)}, u32[]{:S(2)}, u32[]{:S(2)}) collective-permute-start(bf16[1,36,768]{2,1,0:T(8,128)(2,1)S(1)} %get-tuple-element.39.refs_0_), channel_id=1, source_target_pairs={{0,16},{4,20},{8,24},{12,28},{16,0},{20,4},{24,8},{28,12},{1,17},{... | collective-permute-start | bytes 165896 | tf_op jit(solution)/shard_map/ppermute | solution.py:324
  9.6 0.5 %collective-permute-start.2 = (bf16[1,36,768]{2,1,0:T(8,128)(2,1)S(1)}, bf16[1,36,768]{2,1,0:T(8,128)(2,1)S(1)}, u32[]{:S(2)}, u32[]{:S(2)}) collective-permute-start(bf16[1,36,768]{2,1,0:T(8,128)(2,1)S(1)} %get-tuple-element.39.refs_0_), channel_id=1, source_target_pairs={{0,24},{4,28},{8,16},{12,20},{16,8},{20,12},{24,0},{28,4},{1,25},{... | collective-permute-start | bytes 165896 | tf_op jit(solution)/shard_map/ppermute | solution.py:324
  10.1 2.0 %fetch.1 = (bf16[768,768]{1,0:T(8,128)(2,1)S(1)}, bf16[768,768]{1,0:T(8,128)(2,1)S(1)}, bf16[768,768]{1,0:T(8,128)(2,1)S(1)}) custom-call(bf16[768,768]{1,0:T(8,128)(2,1)} %refs_0_.1, bf16[768,768]{1,0:T(8,128)(2,1)} %refs_1_.1, bf16[768,768]{1,0:T(8,128)(2,1)} %refs_2_.1), custom_call_target="tpu_custom_call" | custom-call | bytes 6291456 | tf_op jit(solution)/shard_map/fetch/pallas_call | solution.py:114
  12.1 0.9 %collective-permute-done.1.refs_2_ = bf16[1,36,768]{2,1,0:T(8,128)(2,1)S(1)} collective-permute-done((bf16[1,36,768]{2,1,0:T(8,128)(2,1)S(1)}, bf16[1,36,768]{2,1,0:T(8,128)(2,1)S(1)}, u32[]{:S(2)}, u32[]{:S(2)}) %collective-permute-start.1) | collective-permute-done | bytes 55328 | tf_op jit(solution)/shard_map/ppermute | solution.py:324
  13.0 1.8 %collective-permute-done.2.refs_3_ = bf16[1,36,768]{2,1,0:T(8,128)(2,1)S(1)} collective-permute-done((bf16[1,36,768]{2,1,0:T(8,128)(2,1)S(1)}, bf16[1,36,768]{2,1,0:T(8,128)(2,1)S(1)}, u32[]{:S(2)}, u32[]{:S(2)}) %collective-permute-start.2) | collective-permute-done | bytes 55328 | tf_op jit(solution)/shard_map/ppermute | solution.py:324
  14.8 0.5 %collective-permute-done.3.refs_5_ = bf16[72,768]{1,0:T(8,128)(2,1)S(1)} collective-permute-done((bf16[72,768]{1,0:T(8,128)(2,1)S(1)}, bf16[72,768]{1,0:T(8,128)(2,1)S(1)}, u32[]{:S(2)}, u32[]{:S(2)}) %collective-permute-start.3) | collective-permute-done | bytes 110624 | tf_op jit(solution)/shard_map/ppermute | solution.py:322
  15.3 0.5 %collective-permute-start.8 = (bf16[72,768]{1,0:T(8,128)(2,1)S(1)}, bf16[72,768]{1,0:T(8,128)(2,1)S(1)}, u32[]{:S(2)}, u32[]{:S(2)}) collective-permute-start(bf16[72,768]{1,0:T(8,128)(2,1)S(1)} %collective-permute-done.4.refs_6_), channel_id=1, source_target_pairs={{0,4},{4,0},{8,12},{12,8},{16,20},{20,16},{24,28},{28,24},{1,5},{5... | collective-permute-start | bytes 331784 | tf_op jit(solution)/shard_map/ppermute | solution.py:330
  15.8 0.1 collective-permute-start.9
  15.8 1.0 %attention.2 = (bf16[1,36,768]{2,1,0:T(8,128)(2,1)S(1)}, bf16[1,36,768]{2,1,0:T(8,128)(2,1)S(1)}, bf16[1,36,768]{2,1,0:T(8,128)(2,1)S(1)}, bf16[1,36,768]{2,1,0:T(8,128)(2,1)S(1)}, bf16[144,768]{1,0:T(8,128)(2,1)S(1)}) custom-call(bf16[1,36,768]{2,1,0:T(8,128)(2,1)S(1)} %get-tuple-element.39.refs_0_, bf16[1,36,768]{2,1,0:T(8,128)(2,1)S(1)} %collective-permute-done.refs_1_, ...), custom_call_target="tpu_custom_call" | custom-call | flops 63700992 | bytes 1048576 | tf_op jit(solution)/shard_map/attention/pallas_call | solution.py:161
  16.8 0.3 collective-permute-done.9.refs_4_
  17.1 1.0 %attention.3 = (bf16[72,768]{1,0:T(8,128)(2,1)S(1)}, bf16[72,768]{1,0:T(8,128)(2,1)S(1)}, bf16[72,768]{1,0:T(8,128)(2,1)S(1)}, bf16[72,768]{1,0:T(8,128)(2,1)S(1)}) custom-call(bf16[144,768]{1,0:T(8,128)(2,1)S(1)} %get-tuple-element.44.refs_0_, bf16[72,768]{1,0:T(8,128)(2,1)S(1)} %collective-permute-done.6.refs_1_, ...), custom_call_target="tpu_custom_call" | custom-call | flops 63700992 | bytes 1048576 | tf_op jit(solution)/shard_map/attention/pallas_call | solution.py:161
  18.1 1.6 %collective-permute-start.12 = (bf16[72,768]{1,0:T(8,128)(2,1)S(1)}, bf16[72,768]{1,0:T(8,128)(2,1)S(1)}, u32[]{:S(2)}, u32[]{:S(2)}) collective-permute-start(bf16[72,768]{1,0:T(8,128)(2,1)S(1)} %get-tuple-element.61), channel_id=1, source_target_pairs={{24,0},{28,4},{16,8},{20,12},{8,16},{12,20},{0,24},{4,28},{25,1},{... | collective-permute-start | bytes 331784 | tf_op jit(solution)/shard_map/ppermute | solution.py:337
  19.6 1.5 %collective-permute-start.10 = (bf16[72,768]{1,0:T(8,128)(2,1)S(1)}, bf16[72,768]{1,0:T(8,128)(2,1)S(1)}, u32[]{:S(2)}, u32[]{:S(2)}) collective-permute-start(bf16[72,768]{1,0:T(8,128)(2,1)S(1)} %get-tuple-element.53), channel_id=1, source_target_pairs={{8,0},{12,4},{0,8},{4,12},{24,16},{28,20},{16,24},{20,28},{9,1},{1... | collective-permute-start | bytes 331784 | tf_op jit(solution)/shard_map/ppermute | solution.py:337
  21.1 0.5 %collective-permute-start.11 = (bf16[72,768]{1,0:T(8,128)(2,1)S(1)}, bf16[72,768]{1,0:T(8,128)(2,1)S(1)}, u32[]{:S(2)}, u32[]{:S(2)}) collective-permute-start(bf16[72,768]{1,0:T(8,128)(2,1)S(1)} %get-tuple-element.54), channel_id=1, source_target_pairs={{16,0},{20,4},{24,8},{28,12},{0,16},{4,20},{8,24},{12,28},{17,1},{... | collective-permute-start | bytes 331784 | tf_op jit(solution)/shard_map/ppermute | solution.py:337
  21.6 0.9 %mix_own.1 = (f32[40,768]{1,0:T(8,128)S(1)}, f32[80,128]{1,0:T(8,128)S(1)}, f32[80,768]{1,0:T(8,128)S(1)}) custom-call(bf16[72,768]{1,0:T(8,128)(2,1)S(1)} %get-tuple-element.55.block, bf16[768,768]{1,0:T(8,128)(2,1)S(1)} %get-tuple-element.56.w_query, bf16[768,768]{1,0:T(8,128)(2,1)S(1)} %get-tuple-element.57.w_key.refs_3_, ...), custom_call_target="tpu_custom_call" | custom-call | flops 169869312 | bytes 4194304 | tf_op jit(solution)/shard_map/mix_own/pallas_call | solution.py:257
  22.6 2.4 %collective-permute-done.12.block = bf16[72,768]{1,0:T(8,128)(2,1)S(1)} collective-permute-done((bf16[72,768]{1,0:T(8,128)(2,1)S(1)}, bf16[72,768]{1,0:T(8,128)(2,1)S(1)}, u32[]{:S(2)}, u32[]{:S(2)}) %collective-permute-start.12) | collective-permute-done | bytes 110624 | tf_op jit(solution)/shard_map/ppermute | solution.py:337
  24.9 0.8 %mix_part.1 = (f32[80,128]{1,0:T(8,128)S(1)}, f32[80,768]{1,0:T(8,128)S(1)}) custom-call(bf16[72,768]{1,0:T(8,128)(2,1)S(1)} %collective-permute-done.12.block, f32[40,768]{1,0:T(8,128)S(1)} %get-tuple-element.59.query.refs_2_, bf16[768,768]{1,0:T(8,128)(2,1)S(1)} %get-tuple-element.57.w_key.refs_3_, bf16[768,768]{1,0:T(8,128)(2,1)S(1)} %get-tuple-element.58.w_value.refs_4_), custom_call_target="tpu_custom_call" | custom-call | flops 169869312 | bytes 4194304 | tf_op jit(solution)/shard_map/mix_part/pallas_call | solution.py:257
  25.8 0.9 %collective-permute-done.10.refs_0_ = bf16[72,768]{1,0:T(8,128)(2,1)S(1)} collective-permute-done((bf16[72,768]{1,0:T(8,128)(2,1)S(1)}, bf16[72,768]{1,0:T(8,128)(2,1)S(1)}, u32[]{:S(2)}, u32[]{:S(2)}) %collective-permute-start.10) | collective-permute-done | bytes 110624 | tf_op jit(solution)/shard_map/ppermute | solution.py:337
  26.6 1.6 %mix_last.1 = bf16[1,36,768]{2,1,0:T(8,128)(2,1)} custom-call(bf16[72,768]{1,0:T(8,128)(2,1)S(1)} %collective-permute-done.10.refs_0_, bf16[72,768]{1,0:T(8,128)(2,1)S(1)} %collective-permute-done.11.refs_1_, f32[40,768]{1,0:T(8,128)S(1)} %get-tuple-element.59.query.refs_2_, bf16[768,768]{1,0:T(8,128)(2,1)S(1)} %get-tuple-element.57.w_key.refs_3_, ...), custom_call_target="tpu_custom_call" | custom-call | flops 339738624 | bytes 4194304 | tf_op jit(solution)/shard_map/mix_last/pallas_call | solution.py:257
  (9 shorter events, 0.1 us)
Async XLA Ops:
  0.9 8.7 %collective-permute-start = (bf16[1,36,768]{2,1,0:T(8,128)(2,1)S(1)}, bf16[1,36,768]{2,1,0:T(8,128)(2,1)S(1)}, u32[]{:S(2)}, u32[]{:S(2)}) collective-permute-start(bf16[1,36,768]{2,1,0:T(8,128)(2,1)S(1)} %get-tuple-element.39.refs_0_), channel_id=1, source_target_pairs={{0,8},{4,12},{8,0},{12,4},{16,24},{20,28},{24,16},{28,20},{1,9},{5... | collective-permute-start | bytes 165896 | tf_op jit(solution)/shard_map/ppermute | solution.py:324
  3.9 11.3 %collective-permute-start.3 = (bf16[72,768]{1,0:T(8,128)(2,1)S(1)}, bf16[72,768]{1,0:T(8,128)(2,1)S(1)}, u32[]{:S(2)}, u32[]{:S(2)}) collective-permute-start(bf16[72,768]{1,0:T(8,128)(2,1)S(1)} %get-tuple-element.45.refs_4_), channel_id=1, source_target_pairs={{0,2},{1,3},{2,0},{3,1},{4,6},{5,7},{6,4},{7,5},{8,10},{9,11},{10,... | collective-permute-start | bytes 331784 | tf_op jit(solution)/shard_map/ppermute | solution.py:322
  6.5 8.7 %collective-permute-start.4 = (bf16[72,768]{1,0:T(8,128)(2,1)S(1)}, bf16[72,768]{1,0:T(8,128)(2,1)S(1)}, u32[]{:S(2)}, u32[]{:S(2)}) collective-permute-start(bf16[72,768]{1,0:T(8,128)(2,1)S(1)} %get-tuple-element.45.refs_4_), channel_id=1, source_target_pairs={{0,3},{1,2},{2,1},{3,0},{4,7},{5,6},{6,5},{7,4},{8,11},{9,10},{10,... | collective-permute-start | bytes 331784 | tf_op jit(solution)/shard_map/ppermute | solution.py:322
  7.9 7.9 %collective-permute-start.5 = (bf16[72,768]{1,0:T(8,128)(2,1)S(1)}, bf16[72,768]{1,0:T(8,128)(2,1)S(1)}, u32[]{:S(2)}, u32[]{:S(2)}) collective-permute-start(bf16[72,768]{1,0:T(8,128)(2,1)S(1)} %get-tuple-element.45.refs_4_), channel_id=1, source_target_pairs={{0,1},{1,0},{2,3},{3,2},{4,5},{5,4},{6,7},{7,6},{8,9},{9,8},{10,11... | collective-permute-start | bytes 331784 | tf_op jit(solution)/shard_map/ppermute | solution.py:322
  8.1 4.9 %collective-permute-start.1 = (bf16[1,36,768]{2,1,0:T(8,128)(2,1)S(1)}, bf16[1,36,768]{2,1,0:T(8,128)(2,1)S(1)}, u32[]{:S(2)}, u32[]{:S(2)}) collective-permute-start(bf16[1,36,768]{2,1,0:T(8,128)(2,1)S(1)} %get-tuple-element.39.refs_0_), channel_id=1, source_target_pairs={{0,16},{4,20},{8,24},{12,28},{16,0},{20,4},{24,8},{28,12},{1,17},{... | collective-permute-start | bytes 165896 | tf_op jit(solution)/shard_map/ppermute | solution.py:324
  9.6 5.1 %collective-permute-start.2 = (bf16[1,36,768]{2,1,0:T(8,128)(2,1)S(1)}, bf16[1,36,768]{2,1,0:T(8,128)(2,1)S(1)}, u32[]{:S(2)}, u32[]{:S(2)}) collective-permute-start(bf16[1,36,768]{2,1,0:T(8,128)(2,1)S(1)} %get-tuple-element.39.refs_0_), channel_id=1, source_target_pairs={{0,24},{4,28},{8,16},{12,20},{16,8},{20,12},{24,0},{28,4},{1,25},{... | collective-permute-start | bytes 165896 | tf_op jit(solution)/shard_map/ppermute | solution.py:324
  14.8 2.0 %collective-permute-start.6 = (bf16[72,768]{1,0:T(8,128)(2,1)S(1)}, bf16[72,768]{1,0:T(8,128)(2,1)S(1)}, u32[]{:S(2)}, u32[]{:S(2)}) collective-permute-start(bf16[72,768]{1,0:T(8,128)(2,1)S(1)} %get-tuple-element.45.refs_4_), channel_id=1, source_target_pairs={{0,4},{4,0},{8,12},{12,8},{16,20},{20,16},{24,28},{28,24},{1,5},{5... | collective-permute-start | bytes 331784 | tf_op jit(solution)/shard_map/ppermute | solution.py:330
  15.2 1.6 %collective-permute-start.7 = (bf16[72,768]{1,0:T(8,128)(2,1)S(1)}, bf16[72,768]{1,0:T(8,128)(2,1)S(1)}, u32[]{:S(2)}, u32[]{:S(2)}) collective-permute-start(bf16[72,768]{1,0:T(8,128)(2,1)S(1)} %collective-permute-done.3.refs_5_), channel_id=1, source_target_pairs={{0,4},{4,0},{8,12},{12,8},{16,20},{20,16},{24,28},{28,24},{1,5},{5... | collective-permute-start | bytes 331784 | tf_op jit(solution)/shard_map/ppermute | solution.py:330
  15.3 1.5 %collective-permute-start.8 = (bf16[72,768]{1,0:T(8,128)(2,1)S(1)}, bf16[72,768]{1,0:T(8,128)(2,1)S(1)}, u32[]{:S(2)}, u32[]{:S(2)}) collective-permute-start(bf16[72,768]{1,0:T(8,128)(2,1)S(1)} %collective-permute-done.4.refs_6_), channel_id=1, source_target_pairs={{0,4},{4,0},{8,12},{12,8},{16,20},{20,16},{24,28},{28,24},{1,5},{5... | collective-permute-start | bytes 331784 | tf_op jit(solution)/shard_map/ppermute | solution.py:330
  15.8 1.3 %collective-permute-start.9 = (bf16[72,768]{1,0:T(8,128)(2,1)S(1)}, bf16[72,768]{1,0:T(8,128)(2,1)S(1)}, u32[]{:S(2)}, u32[]{:S(2)}) collective-permute-start(bf16[72,768]{1,0:T(8,128)(2,1)S(1)} %collective-permute-done.5.refs_7_), channel_id=1, source_target_pairs={{0,4},{4,0},{8,12},{12,8},{16,20},{20,16},{24,28},{28,24},{1,5},{5... | collective-permute-start | bytes 331784 | tf_op jit(solution)/shard_map/ppermute | solution.py:330
  18.1 6.9 %collective-permute-start.12 = (bf16[72,768]{1,0:T(8,128)(2,1)S(1)}, bf16[72,768]{1,0:T(8,128)(2,1)S(1)}, u32[]{:S(2)}, u32[]{:S(2)}) collective-permute-start(bf16[72,768]{1,0:T(8,128)(2,1)S(1)} %get-tuple-element.61), channel_id=1, source_target_pairs={{24,0},{28,4},{16,8},{20,12},{8,16},{12,20},{0,24},{4,28},{25,1},{... | collective-permute-start | bytes 331784 | tf_op jit(solution)/shard_map/ppermute | solution.py:337
  19.6 7.0 %collective-permute-start.10 = (bf16[72,768]{1,0:T(8,128)(2,1)S(1)}, bf16[72,768]{1,0:T(8,128)(2,1)S(1)}, u32[]{:S(2)}, u32[]{:S(2)}) collective-permute-start(bf16[72,768]{1,0:T(8,128)(2,1)S(1)} %get-tuple-element.53), channel_id=1, source_target_pairs={{8,0},{12,4},{0,8},{4,12},{24,16},{28,20},{16,24},{20,28},{9,1},{1... | collective-permute-start | bytes 331784 | tf_op jit(solution)/shard_map/ppermute | solution.py:337
  21.1 5.5 %collective-permute-start.11 = (bf16[72,768]{1,0:T(8,128)(2,1)S(1)}, bf16[72,768]{1,0:T(8,128)(2,1)S(1)}, u32[]{:S(2)}, u32[]{:S(2)}) collective-permute-start(bf16[72,768]{1,0:T(8,128)(2,1)S(1)} %get-tuple-element.54), channel_id=1, source_target_pairs={{16,0},{20,4},{24,8},{28,12},{0,16},{4,20},{8,24},{12,28},{17,1},{... | collective-permute-start | bytes 331784 | tf_op jit(solution)/shard_map/ppermute | solution.py:337
